TPU v7x, 32 devices: a whole 2x2x4 slice. The times are simulated.
32 devices in a mesh: tok: 8 (over z, x), head: 4 (over y, core).
Axes of the slice: x: 2, y: 2, z: 4, core: 2. Of those that a mesh axis runs over, the one named last changes fastest.
Arguments:
- queries: bfloat16 [2, 1024, 2048], P(None, 'tok', 'head'), may hold values from -6 to 6
- keys: bfloat16 [1024, 2048], P('tok', 'head'), may hold values from -6 to 6
- values: bfloat16 [1024, 2048], P('tok', 'head'), may hold values from -6 to 6
- upstream: bfloat16 [2, 1024, 2048], P(None, 'tok', 'head'), may hold values from -6 to 6
- out_gain: float32 [2048], P('head'), may hold values from 0.5 to 2
- gate_weight: bfloat16 [4, 512, 512], P('head', 'tok'), may hold values from -0.25 to 0.25
- up_weight: bfloat16 [4, 512, 512], P('head', 'tok'), may hold values from -0.25 to 0.25
- down_weight: bfloat16 [4, 512, 512], P('head', 'tok'), may hold values from -0.25 to 0.25
Outputs:
- grad_queries: bfloat16 [2, 1024, 2048], P(None, 'tok', 'head')
- grad_keys: bfloat16 [1024, 2048], P('tok', 'head')
- grad_values: bfloat16 [1024, 2048], P('tok', 'head')
- grad_gate: float32 [4, 512, 512], P('head', 'tok')
- grad_up: float32 [4, 512, 512], P('head', 'tok')
- grad_down: float32 [4, 512, 512], P('head', 'tok')
All inputs are finite; a program needn't handle non-finite values.
Results may differ from a plain program's by a relative error of at most 0.02.
Values may be sent and summed in bfloat16 or wider, within the bound.
No kernel may reach another device: no remote copies, remote signals or barrier semaphores. Data moves between devices by JAX's collectives and lax.ppermute only.
A program may use at most 128 MiB of HBM per device.

v0:
```python
import math

import jax
import jax.numpy as jnp
from jax import lax
from jax.sharding import PartitionSpec as P

NS_STEPS = 2


lin_coef = 3.4445
cube_coef = -4.775
fifth_coef = 2.0315
rms_eps = 1e-06
fro_eps = 1e-07


def product(left, right):
    return jnp.dot(left, right, preferred_element_type=jnp.float32)


def across(left, right):
    return lax.dot_general(
        left, right, (((0,), (0,)), ((), ())), preferred_element_type=jnp.float32
    )


def against(left, right):
    return lax.dot_general(
        left, right, (((1,), (1,)), ((), ())), preferred_element_type=jnp.float32
    )


def fast_forward(keys, values, weights):
    gate_weight, up_weight, down_weight = weights
    gate_pre = product(keys, gate_weight)
    up_pre = product(keys, up_weight)
    sigma = jax.nn.sigmoid(gate_pre)
    active = gate_pre * sigma
    hidden = (active * up_pre).astype(jnp.bfloat16)
    back = -against(values, down_weight)
    slope = sigma * (1.0 + gate_pre * (1.0 - sigma))
    d_gate = (back * up_pre * slope).astype(jnp.bfloat16)
    d_up = (back * active).astype(jnp.bfloat16)
    fast = (across(keys, d_gate), across(keys, d_up), -across(hidden, values))
    saved = (gate_pre, up_pre, sigma, active, hidden, back, slope, d_gate, d_up)
    return (fast, saved)


def fast_second(keys, values, weights, saved, cots):
    gate_weight, up_weight, down_weight = weights
    gate_pre, up_pre, sigma, active, hidden, back, slope, d_gate, d_up = saved
    cot_gate, cot_up, cot_down = cots
    along_gate = product(keys, cot_gate)
    along_up = product(keys, cot_up)
    along_hidden = -against(values, cot_down)
    curve = sigma * (1.0 - sigma) * (2.0 + gate_pre * (1.0 - 2.0 * sigma))
    d_back = (along_gate * up_pre * slope + along_up * active).astype(jnp.bfloat16)
    d_upper = (along_gate * back * slope + along_hidden * active).astype(jnp.bfloat16)
    d_lower = (
        along_gate * back * up_pre * curve + along_up * back * slope + along_hidden * up_pre * slope
    ).astype(jnp.bfloat16)
    grad_keys = (
        against(d_gate, cot_gate)
        + against(d_up, cot_up)
        + against(d_lower, gate_weight)
        + against(d_upper, up_weight)
    ).astype(jnp.bfloat16)
    grad_values = (-product(hidden, cot_down) - product(d_back, down_weight)).astype(jnp.bfloat16)
    partial_value = (across(keys, d_lower), across(keys, d_upper), -across(d_back, values))
    return (grad_keys, grad_values, partial_value)


def apply_forward(queries, weights):
    gate_weight, up_weight, down_weight = weights
    gate_pre = product(queries, gate_weight)
    up_pre = product(queries, up_weight)
    sigma = jax.nn.sigmoid(gate_pre)
    hidden = (gate_pre * sigma * up_pre).astype(jnp.bfloat16)
    output = product(hidden, down_weight)
    return (gate_pre, up_pre, sigma, hidden, output)


def statistics(output, upstream, out_gain, width):
    weighted = out_gain * upstream.astype(jnp.float32)
    sums = lax.psum((jnp.sum(output * output, axis=1), jnp.sum(weighted * output, axis=1)), "head")
    return (lax.rsqrt(sums[0] / width + rms_eps), sums[1] / width)


def apply_backward(queries, weights, saved, upstream, out_gain, width):
    gate_weight, up_weight, down_weight = weights
    gate_pre, up_pre, sigma, hidden, output = saved
    inverse_rms, mean_dot = statistics(output, upstream, out_gain, width)
    weighted = out_gain * upstream.astype(jnp.float32)
    d_output = (
        inverse_rms[:, None] * weighted
        - output * (inverse_rms * inverse_rms * inverse_rms * mean_dot)[:, None]
    ).astype(jnp.bfloat16)
    back = against(d_output, down_weight)
    slope = sigma * (1.0 + gate_pre * (1.0 - sigma))
    d_gate = (back * up_pre * slope).astype(jnp.bfloat16)
    d_up = (back * gate_pre * sigma).astype(jnp.bfloat16)
    grad_queries = (against(d_gate, gate_weight) + against(d_up, up_weight)).astype(jnp.bfloat16)
    partial_value = (across(queries, d_gate), across(queries, d_up), across(hidden, d_output))
    return (grad_queries, partial_value)


def schulz_forward(begin):
    current = begin
    saved = []
    for sweep in range(NS_STEPS):
        gram = against(current, current).astype(jnp.bfloat16)
        blend = (cube_coef * gram.astype(jnp.float32) + fifth_coef * product(gram, gram)).astype(
            jnp.bfloat16
        )
        following = (lin_coef * current.astype(jnp.float32) + product(blend, current)).astype(
            jnp.bfloat16
        )
        saved.append((current, gram, blend))
        current = following
    return (current, saved)


def schulz_backward(cotan, saved):
    current = cotan
    for iterate, gram, blend in reversed(saved):
        cross = against(current, iterate)
        symmetric = (cross + cross.T).astype(jnp.bfloat16)
        bent = product(symmetric, gram)
        mixed = (cube_coef * symmetric.astype(jnp.float32) + fifth_coef * (bent + bent.T)).astype(
            jnp.bfloat16
        )
        current = (
            lin_coef * current.astype(jnp.float32)
            + product(blend, current)
            + product(mixed, iterate)
        ).astype(jnp.bfloat16)
    return current


def per_device(queries, keys, values, upstream, out_gain, gate_weight, up_weight, down_weight):
    shards = lax.axis_size("tok")
    owner = lax.axis_index("tok")
    width = out_gain.shape[0] * lax.axis_size("head")
    scale = 1.0 / math.sqrt(queries.shape[1] * shards)
    own_rows = (gate_weight[0], up_weight[0], down_weight[0])
    starts = [owner * own_rows[which].shape[0] for which in range(3)]
    first = (
        lax.all_gather(own_rows[0], "tok", axis=0, tiled=True),
        lax.all_gather(own_rows[1], "tok", axis=0, tiled=True),
        lax.all_gather(own_rows[2], "tok", axis=0, tiled=True),
    )
    fast, saved_keys = fast_forward(keys, values, first)
    apply_first = apply_forward(queries[0], first)
    grad_first, partial_first = apply_backward(
        queries[0], first, apply_first, upstream[0], out_gain, width
    )
    totals = lax.psum((fast[0], fast[1], fast[2]), "tok")
    roots = [jnp.sqrt(jnp.sum(totals[which] * totals[which])) for which in range(3)]
    forward = [
        schulz_forward((totals[which] / (roots[which] + fro_eps)).astype(jnp.bfloat16))
        for which in range(3)
    ]
    finals = [forward[which][0] for which in range(3)]
    second = tuple(
        (
            (first[which].astype(jnp.float32) - finals[which].astype(jnp.float32)).astype(
                jnp.bfloat16
            )
            for which in range(3)
        )
    )
    apply_second = apply_forward(queries[1], second)
    grad_second, partial_second = apply_backward(
        queries[1], second, apply_second, upstream[1], out_gain, width
    )
    rates = lax.psum((partial_second[0], partial_second[1], partial_second[2]), "tok")
    bottoms = [
        schulz_backward((-rates[which]).astype(jnp.bfloat16), forward[which][1])
        for which in range(3)
    ]
    cots = []
    for which in range(3):
        norm = roots[which] + fro_eps
        inner = jnp.sum(bottoms[which].astype(jnp.float32) * totals[which])
        cots.append(
            (
                bottoms[which].astype(jnp.float32) / norm
                - totals[which] * (inner / (norm * norm * roots[which]))
            ).astype(jnp.bfloat16)
        )
    rate_rows = [
        lax.dynamic_slice_in_dim(rates[which], starts[which], own_rows[which].shape[0], 0)
        for which in range(3)
    ]
    grad_keys, grad_values, second_order = fast_second(keys, values, first, saved_keys, cots)
    sums = (
        lax.psum_scatter(
            partial_first[0] + second_order[0], "tok", scatter_dimension=0, tiled=True
        ),
        lax.psum_scatter(
            partial_first[1] + second_order[1], "tok", scatter_dimension=0, tiled=True
        ),
        lax.psum_scatter(
            partial_first[2] + second_order[2], "tok", scatter_dimension=0, tiled=True
        ),
    )
    grad_gate = ((sums[0] + rate_rows[0]) * scale)[None]
    grad_up = ((sums[1] + rate_rows[1]) * scale)[None]
    grad_down = ((sums[2] + rate_rows[2]) * scale)[None]
    grad_queries = jnp.stack([grad_first, grad_second])
    return (grad_queries, grad_keys, grad_values, grad_gate, grad_up, grad_down)


def solution(mesh):
    in_specs = (
        P(None, "tok", "head"),
        P("tok", "head"),
        P("tok", "head"),
        P(None, "tok", "head"),
        P("head"),
        P("head", "tok", None),
        P("head", "tok", None),
        P("head", "tok", None),
    )
    out_specs = (
        P(None, "tok", "head"),
        P("tok", "head"),
        P("tok", "head"),
        P("head", "tok", None),
        P("head", "tok", None),
        P("head", "tok", None),
    )
    return jax.shard_map(
        per_device, mesh=mesh, in_specs=in_specs, out_specs=out_specs, check_vma=False
    )
```

profile of v0, /device:TPU:0, one launch (start us, length us, event | category | flops | bytes accessed | tf_op | source)
XLA Modules:
  0.0 725.8 jit_solution(1483022965633269936)
XLA Ops:
  7.2 33.4 %all-gather = bf16[1,512,512]{2,1,0:T(8,128)(2,1)S(1)} all-gather(bf16[1,64,512]{2,1,0:T(8,128)(2,1)} %param.13), channel_id=2, replica_groups=mesh['tok'=8,'head'=4] {'tok'}, dimensions={1}, use_global_device_ids=true | all-gather | bytes 589824 | tf_op jit(solution)/shard_map/all_gather | solution.py:149
  40.6 31.5 %all-gather.2 = bf16[1,512,512]{2,1,0:T(8,128)(2,1)S(1)} all-gather(bf16[1,64,512]{2,1,0:T(8,128)(2,1)S(1)} %copy-done.105), channel_id=4, replica_groups=mesh['tok'=8,'head'=4] {'tok'}, dimensions={1}, use_global_device_ids=true | all-gather | bytes 589824 | tf_op jit(solution)/shard_map/all_gather | solution.py:151
  72.1 31.5 %all-gather.1 = bf16[1,512,512]{2,1,0:T(8,128)(2,1)S(1)} all-gather(bf16[1,64,512]{2,1,0:T(8,128)(2,1)S(1)} %copy-done.106), channel_id=3, replica_groups=mesh['tok'=8,'head'=4] {'tok'}, dimensions={1}, use_global_device_ids=true | all-gather | bytes 589824 | tf_op jit(solution)/shard_map/all_gather | solution.py:150
  114.7 127.0 %all-reduce.8.cloned.1.call-done = (f32[512,512]{0,1:T(8,128)}, f32[512,512]{0,1:T(8,128)}, f32[512,512]{0,1:T(8,128)}) async-done(((f32[512,512]{0,1:T(8,128)}, f32[512,512]{0,1:T(8,128)}, f32[512,512]{0,1:T(8,128)}), (f32[512,512]{0,1:T(8,128)}, f32[512,512]{0,1:T(8,128)}, f32[512,512]{0,1:T(8,128)})) %all-reduce.8.cloned.1.call-update) | async-done | bytes 3145744 | tf_op jit(solution)/shard_map/psum | solution.py:158
  241.7 2.2 multiply_reduce_fusion.2
  271.2 7.5 %all-reduce.2 = (f32[128]{0:T(128)S(1)}, f32[128]{0:T(128)S(1)}, f32[128]{0:T(128)S(1)}, f32[128]{0:T(128)}) all-reduce(f32[128]{0:T(128)} %get-tuple-element.19, f32[128]{0:T(128)} %get-tuple-element.20, f32[128]{0:T(128)} %get-tuple-element.18, f32[128]{0:T(128)} %get-tuple-element.21), channel_id=1, replica_groups=mesh['tok'=8,'head'=4] {'head'}, use_global_device_ids=true, to_apply=%region_13.0 | all-reduce | flops 512 | bytes 4096 | tf_op jit(solution)/shard_map/psum | solution.py:86
  286.0 2.1 multiply_convert_fusion.6
  290.1 123.9 %all-reduce.6.cloned.1.call-done = (f32[512,512]{0,1:T(8,128)}, f32[512,512]{0,1:T(8,128)}, f32[512,512]{0,1:T(8,128)}) async-done(((f32[512,512]{0,1:T(8,128)}, f32[512,512]{0,1:T(8,128)}, f32[512,512]{0,1:T(8,128)}), (f32[512,512]{0,1:T(8,128)}, f32[512,512]{0,1:T(8,128)}, f32[512,512]{0,1:T(8,128)})) %all-reduce.6.cloned.1.call-update) | async-done | bytes 3145744 | tf_op jit(solution)/shard_map/psum | solution.py:177
  414.0 3.3 convolution_add_fusion.13
  418.8 2.6 copy.72
  425.4 2.6 copy.73
  428.0 2.7 fusion.30
  436.8 2.5 copy.80
  443.3 2.5 copy.81
  445.9 2.7 fusion.32
  454.6 2.6 copy.91
  461.2 2.6 copy.92
  463.7 2.7 fusion.34
  469.5 2.6 copy.76
  476.0 2.5 copy.77
  478.5 2.6 copy.84
  485.1 2.6 copy.85
  487.7 4.1 fusion.45
  492.5 4.5 fusion.48
  497.7 3.0 fusion.44
  502.5 2.6 copy.95
  509.1 3.8 fusion.51
  519.3 2.5 copy.128
  524.3 2.6 copy.130
  541.8 42.7 %reduce-scatter.10.cloned.1.call-done = f32[64,512]{1,0:T(8,128)} async-done(((f32[512,512]{1,0:T(8,128)}), f32[64,512]{1,0:T(8,128)}) %reduce-scatter.10.cloned.1.call-update) | async-done | bytes 131088
  587.4 63.3 %reduce-scatter.12.cloned.1.call-done = f32[64,512]{1,0:T(8,128)} async-done(((f32[512,512]{1,0:T(8,128)}), f32[64,512]{1,0:T(8,128)}) %reduce-scatter.12.cloned.1.call-update) | async-done | bytes 131088
  653.5 62.9 %reduce-scatter.14.cloned.1.call-done = f32[64,512]{1,0:T(8,128)} async-done(((f32[512,512]{1,0:T(8,128)}), f32[64,512]{1,0:T(8,128)}) %reduce-scatter.14.cloned.1.call-update) | async-done | bytes 131088
  (331 shorter events, 118.9 us)
Async XLA Ops:
  7.2 96.5 %copy-start = (bf16[128,512]{1,0:T(8,128)(2,1)S(1)}, bf16[128,512]{1,0:T(8,128)(2,1)}, u32[]{:S(2)}) copy-start(bf16[128,512]{1,0:T(8,128)(2,1)} %param.9) | copy-start | bytes 393220
  7.2 33.4 %copy-start.105 = (bf16[1,64,512]{2,1,0:T(8,128)(2,1)S(1)}, bf16[1,64,512]{2,1,0:T(8,128)(2,1)}, u32[]{:S(2)}) copy-start(bf16[1,64,512]{2,1,0:T(8,128)(2,1)} %param.15) | copy-start | bytes 196612
  7.2 234.5 %all-reduce.8.cloned.1.call-start = ((), (), s32[]{:S(2)}) async-start(), calls=%async_computation.7 | async-start | bytes 6291456 | tf_op jit(solution)/shard_map/psum | solution.py:158
  40.6 31.5 %copy-start.106 = (bf16[1,64,512]{2,1,0:T(8,128)(2,1)S(1)}, bf16[1,64,512]{2,1,0:T(8,128)(2,1)}, u32[]{:S(2)}) copy-start(bf16[1,64,512]{2,1,0:T(8,128)(2,1)} %param.14) | copy-start | bytes 196612
  103.6 10.1 %copy-start.5 = (bf16[1,512,512]{2,1,0:T(8,128)(2,1)}, bf16[1,512,512]{2,1,0:T(8,128)(2,1)S(1)}, u32[]{:S(2)}) copy-start(bf16[1,512,512]{2,1,0:T(8,128)(2,1)S(1)} %all-gather.1) | copy-start | bytes 1572868
  106.3 2.7 copy-start.48
  110.3 303.6 %all-reduce.6.cloned.1.call-start = ((), (), s32[]{:S(2)}) async-start(), calls=%async_computation.6 | async-start | bytes 6291456 | tf_op jit(solution)/shard_map/psum | solution.py:177
  241.7 2.9 copy-start.2
  246.8 1.7 copy-start.31
  249.1 2.6 copy-start.3
  263.0 4.8 copy-start.26
  265.6 2.2 copy-start.41
  268.5 2.7 copy-start.60
  269.0 2.2 copy-start.40
  279.4 2.0 copy-start.59
  285.8 298.7 %reduce-scatter.10.cloned.1.call-start = ((), (), s32[]{:S(2)}) async-start(), calls=%async_computation.3 | async-start | bytes 1179648
  414.0 3.3 copy-start.9
  414.0 3.3 copy-start.32
  421.4 2.5 copy-start.84
  428.0 2.7 copy-start.80
  439.3 2.5 copy-start.82
  445.9 2.7 copy-start.76
  457.2 2.6 copy-start.78
  463.7 2.8 copy-start.74
  472.0 2.5 copy-start.70
  481.1 2.6 copy-start.72
  502.5 2.6 copy-start.4
  505.1 2.3 copy-start.68
  516.1 1.8 copy-start.24
  517.3 5.7 copy-start.91
  521.8 128.8 %reduce-scatter.12.cloned.1.call-start = ((), (), s32[]{:S(2)}) async-start(), calls=%async_computation.4 | async-start | bytes 1179648
  526.9 189.5 %reduce-scatter.14.cloned.1.call-start = ((), (), s32[]{:S(2)}) async-start(), calls=%async_computation.5 | async-start | bytes 1179648
  (84 other events, 91.9 us)
Sparse Core Ops, SparseCore 0:
  110.4 131.2 all-reduce.7
  285.9 128.0 all-reduce.5
  521.9 62.4 reduce-scatter.9
  588.1 62.4 reduce-scatter.11
  653.9 62.4 reduce-scatter.13
where the time goes:
time: 728 us; the launch traced here: 726 us
  waiting for transfers between devices  420 us (58%)
  blocking collectives  104 us (14%)
  matrix products  86.9 us (12%)
  local copies, waits for them, and re-layouts  71.2 us (10%)
  other arithmetic  24.7 us (3%)
  between operations  18.8 us (3%)
    unnamed x8, waiting for transfers between devices  169 us
    psum x1, waiting for transfers between devices, per_device(): totals = lax.psum((fast[0], fast[1], fast[2]), 'tok')  127 us
    psum x1, waiting for transfers between devices, per_device(): lax.psum((partial_second[0], partial_second[1], partial_second[2]), 'tok')  124 us
    dot_general x42, matrix products, product(): return jnp.dot(left, right, preferred_element_type=jnp.float32)  55.1 us
    unnamed x230, local copies, waits for them, and re-layouts  38.6 us
    all_gather x1, blocking collectives, per_device(): lax.all_gather(own_rows[0], 'tok', axis=0, tiled=True)  33.4 us
    all_gather x1, blocking collectives, per_device(): lax.all_gather(own_rows[2], 'tok', axis=0, tiled=True)  31.5 us
    all_gather x1, blocking collectives, per_device(): lax.all_gather(own_rows[1], 'tok', axis=0, tiled=True)  31.5 us
  transfers between devices with their start and end apart: 5, of which 5 were waited for; matrix products, arithmetic and copies ran while one was open for 3% of the time, Pallas kernels for 0%

commit v1 on v0

--- a/solution.py
+++ b/solution.py
@@ -1,8 +1,11 @@
+import functools
 import math
 
 import jax
 import jax.numpy as jnp
 from jax import lax
+from jax.experimental import pallas as pl
+from jax.experimental.pallas import tpu as pltpu
 from jax.sharding import PartitionSpec as P
 
 NS_STEPS = 2
@@ -13,6 +16,10 @@
 fifth_coef = 2.0315
 rms_eps = 1e-06
 fro_eps = 1e-07
+
+bf16 = jnp.bfloat16
+f32 = jnp.float32
+ROWS = 256
 
 
 def product(left, right):
@@ -138,18 +145,14 @@
     return current
 
 
-def per_device(queries, keys, values, upstream, out_gain, gate_weight, up_weight, down_weight):
+def split_tokens(queries, keys, values, upstream, out_gain, gate_weight, up_weight, down_weight):
     shards = lax.axis_size("tok")
     owner = lax.axis_index("tok")
     width = out_gain.shape[0] * lax.axis_size("head")
     scale = 1.0 / math.sqrt(queries.shape[1] * shards)
     own_rows = (gate_weight[0], up_weight[0], down_weight[0])
     starts = [owner * own_rows[which].shape[0] for which in range(3)]
-    first = (
-        lax.all_gather(own_rows[0], "tok", axis=0, tiled=True),
-        lax.all_gather(own_rows[1], "tok", axis=0, tiled=True),
-        lax.all_gather(own_rows[2], "tok", axis=0, tiled=True),
-    )
+    first = tuple(lax.all_gather(rows, "tok", axis=0, tiled=True) for rows in own_rows)
     fast, saved_keys = fast_forward(keys, values, first)
     apply_first = apply_forward(queries[0], first)
     grad_first, partial_first = apply_backward(
@@ -161,14 +164,11 @@
         schulz_forward((totals[which] / (roots[which] + fro_eps)).astype(jnp.bfloat16))
         for which in range(3)
     ]
-    finals = [forward[which][0] for which in range(3)]
     second = tuple(
-        (
-            (first[which].astype(jnp.float32) - finals[which].astype(jnp.float32)).astype(
-                jnp.bfloat16
-            )
-            for which in range(3)
-        )
+        (first[which].astype(jnp.float32) - forward[which][0].astype(jnp.float32)).astype(
+            jnp.bfloat16
+        )
+        for which in range(3)
     )
     apply_second = apply_forward(queries[1], second)
     grad_second, partial_second = apply_backward(
@@ -189,27 +189,424 @@
                 - totals[which] * (inner / (norm * norm * roots[which]))
             ).astype(jnp.bfloat16)
         )
-    rate_rows = [
-        lax.dynamic_slice_in_dim(rates[which], starts[which], own_rows[which].shape[0], 0)
-        for which in range(3)
+    grad_keys, grad_values, second_order = fast_second(keys, values, first, saved_keys, cots)
+    grads = []
+    for which in range(3):
+        rate_rows = lax.dynamic_slice_in_dim(
+            rates[which], starts[which], own_rows[which].shape[0], 0
+        )
+        summed = lax.psum_scatter(
+            partial_first[which] + second_order[which], "tok", scatter_dimension=0, tiled=True
+        )
+        grads.append(((summed + rate_rows) * scale)[None])
+    grad_queries = jnp.stack([grad_first, grad_second])
+    return (grad_queries, grad_keys, grad_values, *grads)
+
+
+def shift(array, ring, step):
+    pairs = [
+        (o * 2 + i, ((o + step) % ring) * 2 + i) for o in range(ring) for i in range(2)
     ]
-    grad_keys, grad_values, second_order = fast_second(keys, values, first, saved_keys, cots)
-    sums = (
-        lax.psum_scatter(
-            partial_first[0] + second_order[0], "tok", scatter_dimension=0, tiled=True
+    return lax.ppermute(array, "tok", pairs)
+
+
+def swap(array, ring):
+    return lax.ppermute(array, "tok", [(i, i ^ 1) for i in range(2 * ring)])
+
+
+def gather_pieces(own, ring):
+    rows = own.shape[0]
+    found = [(0, 0, own)]
+    up = down = own
+    for step in range(1, ring // 2 + 1):
+        if 2 * step < ring:
+            up, down = shift(up, ring, 1), shift(down, ring, -1)
+            found += [(-step, 0, up), (step, 0, down)]
+        else:
+            half = rows // 2
+            found.append((-step, 0, shift(up[:half], ring, 1)))
+            found.append((-step, half, shift(down[half:], ring, -1)))
+    pieces = [(outer, 0, first, array) for outer, first, array in found]
+    pieces += [(outer, 1, first, swap(array, ring)) for outer, first, array in found]
+    return pieces
+
+
+def head_sums(stats):
+    heads = lax.axis_size("head")
+    others = [
+        lax.ppermute(stats, "head", [(i, (i + k) % heads) for i in range(heads)])
+        for k in range(1, heads)
+    ]
+    return jnp.stack([stats, *others])
+
+
+def unpack_copies(layout, segments, ring, me, refs, targets, sems):
+    copies = []
+    outer_me, inner_me = me // 2, me % 2
+    slots = {}
+    for (outer, flip, first, rows), ref in zip(layout, refs):
+        slot = slots.setdefault((outer, flip), len(slots))
+        owner = ((outer_me + outer + ring) % ring) * 2 + (inner_me + flip) % 2
+        begin = 0
+        for (count, by_slot), target in zip(segments, targets):
+            low, high = max(begin, first), min(begin + count, first + rows)
+            if low < high:
+                place = slot * count + low - begin
+                if not by_slot:
+                    place = pl.multiple_of(owner * count, 16) + (low - begin)
+                copies.append(
+                    pltpu.make_async_copy(
+                        ref.at[pl.ds(low - first, high - low)],
+                        target.at[pl.ds(place, high - low)],
+                        sems.at[len(copies)],
+                    )
+                )
+            begin += count
+    return copies
+
+
+def chunks_of(tokens):
+    step = min(ROWS, tokens)
+    return [slice(i, i + step) for i in range(0, tokens, step)]
+
+
+def fast_kernel(layout, segments, ring, me_ref, *refs):
+    count = len(layout)
+    pieces, refs = refs[:count], refs[count:]
+    (wg, wu, wd, keys, values, gk_ref, uk_ref, back_ref) = refs[:8]
+    xs, grams, blends, nexts, totals, roots = refs[8:14]
+    d_gate, d_up, hidden, sems = refs[14:]
+    copies = unpack_copies(
+        layout, segments, ring, me_ref[0], pieces, (wg, wu, wd, keys, values), sems
+    )
+    for copy in copies:
+        copy.start()
+    for copy in copies:
+        copy.wait()
+    for part in chunks_of(keys.shape[0]):
+        gk = product(keys[part], wg[...])
+        uk = product(keys[part], wu[...])
+        back = -against(values[part], wd[...])
+        sigma = jax.nn.sigmoid(gk)
+        active = gk * sigma
+        slope = sigma * (1.0 + gk * (1.0 - sigma))
+        hidden[part] = (active * uk).astype(bf16)
+        d_gate[part] = (back * uk * slope).astype(bf16)
+        d_up[part] = (back * active).astype(bf16)
+        gk_ref[part], uk_ref[part], back_ref[part] = gk, uk, back
+    totals[0] = across(keys[...], d_gate[...])
+    totals[1] = across(keys[...], d_up[...])
+    totals[2] = -across(hidden[...], values[...])
+    for which, weight in enumerate((wg, wu, wd)):
+        total = totals[which]
+        root = jnp.sqrt(jnp.sum(total * total, keepdims=True))
+        roots[which] = jnp.broadcast_to(root, roots.shape[1:])
+        xs[which, 0] = (total / (root + fro_eps)).astype(bf16)
+        for sweep in range(NS_STEPS):
+            current = xs[which, sweep]
+            gram = against(current, current).astype(bf16)
+            blend = (cube_coef * gram.astype(f32) + fifth_coef * product(gram, gram)).astype(bf16)
+            following = (lin_coef * current.astype(f32) + product(blend, current)).astype(bf16)
+            grams[which, sweep] = gram
+            blends[which, sweep] = blend
+            if sweep + 1 < NS_STEPS:
+                xs[which, sweep + 1] = following
+        nexts[which] = (weight[...].astype(f32) - following.astype(f32)).astype(bf16)
+
+
+def row_sums(columns, tokens):
+    lanes = lax.broadcasted_iota(jnp.int32, (tokens, 128), 1)
+    spread = jnp.where(lanes == 0, columns[0], jnp.where(lanes == 1, columns[1], 0.0))
+    return spread.T[:8]
+
+
+def forward_part(queries, upstream, gain, wg, wu, wd, gq_ref, uq_ref, hidden_ref, out_ref, stats):
+    for part in chunks_of(queries.shape[0]):
+        gq = product(queries[part], wg[...])
+        uq = product(queries[part], wu[...])
+        hidden = (gq * jax.nn.sigmoid(gq) * uq).astype(bf16)
+        output = product(hidden, wd[...])
+        weighted = gain[...] * upstream[part].astype(f32)
+        sums = (
+            jnp.sum(output * output, axis=1, keepdims=True),
+            jnp.sum(weighted * output, axis=1, keepdims=True),
+        )
+        stats[:, part] = row_sums(sums, output.shape[0])
+        gq_ref[part], uq_ref[part], hidden_ref[part], out_ref[part] = gq, uq, hidden, output
+
+
+def backward_part(
+    width, queries, upstream, gain, wg, wu, wd, gq_ref, uq_ref, hidden, out_ref, sums,
+    grad_ref, d_gate, d_up, d_out, own,
+):
+    for part in chunks_of(queries.shape[0]):
+        total = jnp.sum(sums[:, :, part], axis=0)
+        tokens = total.shape[1]
+        square = total[0:1] / width
+        inverse = lax.rsqrt(square + rms_eps)
+        pull = inverse * inverse * inverse * (total[1:2] / width)
+        index = lax.broadcasted_iota(jnp.int32, (128, tokens), 0)
+        columns = jnp.where(index == 0, inverse, jnp.where(index == 1, pull, 0.0)).T
+        inverse, pull = columns[:, 0:1], columns[:, 1:2]
+        weighted = gain[...] * upstream[part].astype(f32)
+        d_output = (inverse * weighted - out_ref[part] * pull).astype(bf16)
+        back = against(d_output, wd[...])
+        gq, uq = gq_ref[part], uq_ref[part]
+        sigma = jax.nn.sigmoid(gq)
+        d_gate[part] = (back * uq * sigma * (1.0 + gq * (1.0 - sigma))).astype(bf16)
+        d_up[part] = (back * gq * sigma).astype(bf16)
+        d_out[part] = d_output
+    grad_ref[...] = (
+        against(d_gate[:own], wg[...]) + against(d_up[:own], wu[...])
+    ).astype(bf16)
+
+
+def first_forward_kernel(queries, upstream, gain, wg, wu, wd, gq, uq, hidden, out, stats):
+    forward_part(queries, upstream, gain, wg, wu, wd, gq, uq, hidden, out, stats)
+
+
+def first_backward_kernel(
+    width, queries, upstream, gain, wg, wu, wd, gq, uq, hidden, out, sums,
+    grad, partial, d_gate, d_up, d_out,
+):
+    backward_part(
+        width, queries, upstream, gain, wg, wu, wd, gq, uq, hidden, out, sums,
+        grad, d_gate, d_up, d_out, queries.shape[0],
+    )
+    partial[0] = across(queries[...], d_gate[...]).astype(bf16)
+    partial[1] = across(queries[...], d_up[...]).astype(bf16)
+    partial[2] = across(hidden[...], d_out[...]).astype(bf16)
+
+
+def second_forward_kernel(
+    layout, segments, ring, me_ref, gain, nexts, *refs
+):
+    count = len(layout)
+    pieces, refs = refs[:count], refs[count:]
+    queries, upstream, gq, uq, hidden, out, stats, sems = refs
+    copies = unpack_copies(layout, segments, ring, me_ref[0], pieces, (queries, upstream), sems)
+    for copy in copies:
+        copy.start()
+    for copy in copies:
+        copy.wait()
+    forward_part(
+        queries, upstream, gain, nexts.at[0], nexts.at[1], nexts.at[2], gq, uq, hidden, out, stats
+    )
+
+
+def last_kernel(
+    width, own, me_ref, queries, upstream, gain, nexts, gq, uq, hidden_q, out, sums,
+    wg, wu, wd, keys, values, gk_ref, uk_ref, back_ref, xs, grams, blends, totals, roots,
+    grad_queries, grad_keys, grad_values, grads,
+    d_gate, d_up, d_out, rates, cots, lower, upper, d_back, pk, rk, hk,
+):
+    backward_part(
+        width, queries, upstream, gain, nexts.at[0], nexts.at[1], nexts.at[2],
+        gq, uq, hidden_q, out, sums, grad_queries, d_gate, d_up, d_out, own,
+    )
+    rates[0] = across(queries[...], d_gate[...])
+    rates[1] = across(queries[...], d_up[...])
+    rates[2] = across(hidden_q[...], d_out[...])
+    for which in range(3):
+        current = (-rates[which]).astype(bf16)
+        for sweep in reversed(range(NS_STEPS)):
+            iterate, gram, blend = xs[which, sweep], grams[which, sweep], blends[which, sweep]
+            symmetric = (against(current, iterate) + against(iterate, current)).astype(bf16)
+            bent = product(symmetric, gram) + product(gram, symmetric)
+            mixed = (cube_coef * symmetric.astype(f32) + fifth_coef * bent).astype(bf16)
+            current = (
+                lin_coef * current.astype(f32) + product(blend, current) + product(mixed, iterate)
+            ).astype(bf16)
+        root = roots[which, 0:1, 0:1]
+        norm = root + fro_eps
+        total = totals[which]
+        bottom = current.astype(f32)
+        inner = jnp.sum(bottom * total, keepdims=True)
+        cots[which] = (bottom / norm - total * (inner / (norm * norm * root))).astype(bf16)
+    for part in chunks_of(keys.shape[0]):
+        gk, uk, back = gk_ref[part], uk_ref[part], back_ref[part]
+        sigma = jax.nn.sigmoid(gk)
+        active = gk * sigma
+        slope = sigma * (1.0 + gk * (1.0 - sigma))
+        curve = sigma * (1.0 - sigma) * (2.0 + gk * (1.0 - 2.0 * sigma))
+        ek = product(keys[part], cots[0])
+        fk = product(keys[part], cots[1])
+        hk_part = -against(values[part], cots[2])
+        d_back[part] = (ek * uk * slope + fk * active).astype(bf16)
+        upper[part] = (ek * back * slope + hk_part * active).astype(bf16)
+        lower[part] = (
+            ek * back * uk * curve + fk * back * slope + hk_part * uk * slope
+        ).astype(bf16)
+        if part.start == 0:
+            pk[...] = (back * uk * slope).astype(bf16)[:own]
+            rk[...] = (back * active).astype(bf16)[:own]
+            hk[...] = (active * uk).astype(bf16)[:own]
+    grad_keys[...] = (
+        against(pk[...], cots[0])
+        + against(rk[...], cots[1])
+        + against(lower[:own], wg[...])
+        + against(upper[:own], wu[...])
+    ).astype(bf16)
+    grad_values[...] = (-product(hk[...], cots[2]) - product(d_back[:own], wd[...])).astype(bf16)
+    rates[0] += across(keys[...], lower[...])
+    rates[1] += across(keys[...], upper[...])
+    rates[2] -= across(d_back[...], values[...])
+    rows = grads.shape[1]
+    start = pl.multiple_of(me_ref[0] * rows, 16)
+    for which in range(3):
+        grads[which] = rates[which, pl.ds(start, rows)]
+
+
+def vmem():
+    return pl.BlockSpec(memory_space=pltpu.VMEM)
+
+
+def smem():
+    return pl.BlockSpec(memory_space=pltpu.SMEM)
+
+
+def anywhere():
+    return pl.BlockSpec(memory_space=pl.ANY)
+
+
+def params(mib):
+    return pltpu.CompilerParams(vmem_limit_bytes=mib * 2**20)
+
+
+def reduce_first(partial, ring, me):
+    whole, height, depth = partial.shape
+    inner = me % 2
+    blocks = partial.reshape(whole, ring, 2, height // (2 * ring), depth)
+    kept = lax.dynamic_index_in_dim(blocks, inner, 2, keepdims=False)
+    sent = lax.dynamic_index_in_dim(blocks, 1 - inner, 2, keepdims=False)
+    pair = kept.astype(f32) + swap(sent, ring).astype(f32)
+    outer = me // 2
+    result = lax.dynamic_index_in_dim(pair, outer, 1, keepdims=False)
+    for step in range(1, ring):
+        block = lax.dynamic_index_in_dim(pair, (outer + step) % ring, 1, keepdims=False)
+        result = result + shift(block.astype(bf16), ring, step).astype(f32)
+    return result
+
+
+def gather_tokens(queries, keys, values, upstream, out_gain, gate_weight, up_weight, down_weight):
+    shards = lax.axis_size("tok")
+    ring = shards // 2
+    me = lax.axis_index("tok")
+    me_ref = jnp.reshape(me, (1,)).astype(jnp.int32)
+    own, depth = keys.shape
+    rows = gate_weight.shape[1]
+    hidden = gate_weight.shape[2]
+    tokens = own * shards
+    width = out_gain.shape[0] * lax.axis_size("head")
+    scale = 1.0 / math.sqrt(tokens)
+    gain = out_gain[None]
+    S = jax.ShapeDtypeStruct
+
+    packed = jnp.concatenate([gate_weight[0], up_weight[0], down_weight[0], keys, values])
+    pieces = gather_pieces(packed, ring)
+    segments = ((rows, False), (rows, False), (down_weight.shape[1], False), (own, True), (own, True))
+    layout = [(o, f, r, a.shape[0]) for o, f, r, a in pieces]
+    matrix = (depth, hidden)
+    (
+        wg, wu, wd, all_keys, all_values, gk, uk, back, xs, grams, blends, nexts, totals, roots
+    ) = pl.pallas_call(
+        functools.partial(fast_kernel, layout, segments, ring),
+        out_shape=(
+            S(matrix, bf16), S(matrix, bf16), S(matrix, bf16),
+            S((tokens, depth), bf16), S((tokens, depth), bf16),
+            S((tokens, hidden), f32), S((tokens, hidden), f32), S((tokens, hidden), f32),
+            S((3, NS_STEPS, *matrix), bf16), S((3, NS_STEPS, *matrix), bf16),
+            S((3, NS_STEPS, *matrix), bf16), S((3, *matrix), bf16),
+            S((3, *matrix), f32), S((3, 8, 128), f32),
         ),
-        lax.psum_scatter(
-            partial_first[1] + second_order[1], "tok", scatter_dimension=0, tiled=True
+        in_specs=[smem()] + [anywhere()] * len(pieces),
+        out_specs=[vmem()] * 14,
+        scratch_shapes=[
+            pltpu.VMEM((tokens, hidden), bf16),
+            pltpu.VMEM((tokens, hidden), bf16),
+            pltpu.VMEM((tokens, hidden), bf16),
+            pltpu.SemaphoreType.DMA((5 * len(pieces),)),
+        ],
+        compiler_params=params(56),
+    )(me_ref, *[piece[3] for piece in pieces])
+
+    gq0, uq0, hidden0, out0, stats0 = pl.pallas_call(
+        first_forward_kernel,
+        out_shape=(
+            S((own, hidden), f32), S((own, hidden), f32), S((own, hidden), bf16),
+            S((own, depth), f32), S((8, own), f32),
         ),
-        lax.psum_scatter(
-            partial_first[2] + second_order[2], "tok", scatter_dimension=0, tiled=True
+        in_specs=[vmem()] * 6,
+        out_specs=[vmem()] * 5,
+        compiler_params=params(16),
+    )(queries[0], upstream[0], gain, wg, wu, wd)
+    sums0 = head_sums(stats0)
+    grad_first, partial = pl.pallas_call(
+        functools.partial(first_backward_kernel, width),
+        out_shape=(S((own, depth), bf16), S((3, *matrix), bf16)),
+        in_specs=[vmem()] * 11,
+        out_specs=[vmem()] * 2,
+        scratch_shapes=[pltpu.VMEM((own, hidden), bf16)] * 2 + [pltpu.VMEM((own, depth), bf16)],
+        compiler_params=params(24),
+    )(queries[0], upstream[0], gain, wg, wu, wd, gq0, uq0, hidden0, out0, sums0)
+    first_rows = reduce_first(partial, ring, me)
+
+    packed = jnp.concatenate([queries[1], upstream[1]])
+    packed, _ = lax.optimization_barrier((packed, pieces[-1][3]))
+    pieces = gather_pieces(packed, ring)
+    segments = ((own, True), (own, True))
+    layout = [(o, f, r, a.shape[0]) for o, f, r, a in pieces]
+    all_queries, all_upstream, gq, uq, hidden_q, out, stats = pl.pallas_call(
+        functools.partial(second_forward_kernel, layout, segments, ring),
+        out_shape=(
+            S((tokens, depth), bf16), S((tokens, depth), bf16),
+            S((tokens, hidden), f32), S((tokens, hidden), f32), S((tokens, hidden), bf16),
+            S((tokens, depth), f32), S((8, tokens), f32),
         ),
-    )
-    grad_gate = ((sums[0] + rate_rows[0]) * scale)[None]
-    grad_up = ((sums[1] + rate_rows[1]) * scale)[None]
-    grad_down = ((sums[2] + rate_rows[2]) * scale)[None]
+        in_specs=[smem(), vmem(), vmem()] + [anywhere()] * len(pieces),
+        out_specs=[vmem()] * 7,
+        scratch_shapes=[pltpu.SemaphoreType.DMA((2 * len(pieces),))],
+        compiler_params=params(32),
+    )(me_ref, gain, nexts, *[piece[3] for piece in pieces])
+    sums = head_sums(stats)
+
+    grad_second, grad_keys, grad_values, last_rows = pl.pallas_call(
+        functools.partial(last_kernel, width, own),
+        out_shape=(
+            S((own, depth), bf16), S((own, depth), bf16), S((own, depth), bf16),
+            S((3, rows, hidden), f32),
+        ),
+        in_specs=[smem()] + [vmem()] * 22,
+        out_specs=[vmem()] * 4,
+        scratch_shapes=[
+            pltpu.VMEM((tokens, hidden), bf16),
+            pltpu.VMEM((tokens, hidden), bf16),
+            pltpu.VMEM((tokens, depth), bf16),
+            pltpu.VMEM((3, *matrix), f32),
+            pltpu.VMEM((3, *matrix), bf16),
+            pltpu.VMEM((tokens, hidden), bf16),
+            pltpu.VMEM((tokens, hidden), bf16),
+            pltpu.VMEM((tokens, hidden), bf16),
+            pltpu.VMEM((own, hidden), bf16),
+            pltpu.VMEM((own, hidden), bf16),
+            pltpu.VMEM((own, hidden), bf16),
+        ],
+        compiler_params=params(60),
+    )(
+        me_ref, all_queries, all_upstream, gain, nexts, gq, uq, hidden_q, out, sums,
+        wg, wu, wd, all_keys, all_values, gk, uk, back, xs, grams, blends, totals, roots,
+    )
+    grads = (last_rows + first_rows) * scale
     grad_queries = jnp.stack([grad_first, grad_second])
-    return (grad_queries, grad_keys, grad_values, grad_gate, grad_up, grad_down)
+    return (grad_queries, grad_keys, grad_values, grads[0:1], grads[1:2], grads[2:3])
+
+
+def per_device(queries, keys, values, upstream, out_gain, gate_weight, up_weight, down_weight):
+    shards = lax.axis_size("tok")
+    tokens = keys.shape[0] * shards
+    few = 4 * tokens <= 12 * gate_weight.shape[2] and shards % 2 == 0
+    plan = gather_tokens if few else split_tokens
+    return plan(queries, keys, values, upstream, out_gain, gate_weight, up_weight, down_weight)
 
 
 def solution(mesh):

time: 728 us -> 198 us (0.27)
  waiting for transfers between devices: 420 us -> 82.1 us
  blocking collectives: 104 us -> 0 us
  matrix products: 86.9 us -> 0 us
  Pallas kernels: 0 us -> 56.5 us
  local copies, waits for them, and re-layouts: 71.2 us -> 17.2 us
  starting transfers between devices: 0.39 us -> 35.9 us
  other arithmetic: 24.7 us -> 4.9 us
  between operations: 18.8 us -> 0.89 us
    psum x2 -> x0, waiting for transfers between devices: 251 us -> none  [the longest x1 127 us: per_device(): totals = lax.psum((fast[0], fast[1], fast[2]), 'tok')]
    unnamed x8 -> x0, waiting for transfers between devices: 169 us -> none
    all_gather x3 -> x0, blocking collectives: 96.4 us -> none  [the longest x1 33.4 us: per_device(): lax.all_gather(own_rows[0], 'tok', axis=0, tiled=True)]
    dot_general x78 -> x0, matrix products: 86.9 us -> none  [the longest x42 55.1 us: product(): return jnp.dot(left, right, preferred_element_type=jnp.float32)]
    ppermute x0 -> x28, waiting for transfers between devices: none -> 82.1 us  [the longest x11 47.9 us: swap(): return lax.ppermute(array, 'tok', [(i, i ^ 1) for i in range(2 * ring)])]
    pallas_call x0 -> x5, Pallas kernels: none -> 56.5 us  [the longest x1 31.8 us: gather_tokens(): pl.pallas_call(functools.partial(last_kernel, width, own), out_shape=(S((...]
    ppermute x0 -> x28, starting transfers between devices: none -> 35.9 us  [the longest x11 19.9 us: shift(): return lax.ppermute(array, 'tok', pairs)]
    dot_general x12 -> x0, local copies, waits for them, and re-layouts: 29.6 us -> none  [the longest x6 15.4 us: against(): lax.dot_general(left, right, (((1,), (1,)), ((), ())), preferred_element_...]
  transfers between devices with their start and end apart: 5 -> 28, of which waited for: 5 -> 16; matrix products, arithmetic and copies ran while one was open for 3% -> 3% of each run, Pallas kernels for 0% -> 19%
where the time goes in v1:
time: 198 us
  waiting for transfers between devices  82.1 us (41%)
  Pallas kernels  56.5 us (29%)
  starting transfers between devices  35.9 us (18%)
  local copies, waits for them, and re-layouts  17.2 us (9%)
  other arithmetic  4.9 us (2%)
    ppermute x11, waiting for transfers between devices, swap(): return lax.ppermute(array, 'tok', [(i, i ^ 1) for i in range(2 * ring)])  47.9 us
    pallas_call x1, Pallas kernels, gather_tokens(): pl.pallas_call(functools.partial(last_kernel, width, own), out_shape=(S((...  31.8 us
    ppermute x11, waiting for transfers between devices, shift(): return lax.ppermute(array, 'tok', pairs)  31.3 us
    ppermute x11, starting transfers between devices, shift(): return lax.ppermute(array, 'tok', pairs)  19.9 us
    pallas_call x1, Pallas kernels, gather_tokens(): pl.pallas_call(functools.partial(fast_kernel, layout, segments, ring), ou...  16.8 us
    ppermute x11, starting transfers between devices, swap(): return lax.ppermute(array, 'tok', [(i, i ^ 1) for i in range(2 * ring)])  12.5 us
    unnamed x54, local copies, waits for them, and re-layouts  12.3 us
    pallas_call x1, Pallas kernels, gather_tokens(): pl.pallas_call(functools.partial(second_forward_kernel, layout, segments,...  6.05 us
  transfers between devices with their start and end apart: 28, of which 16 were waited for; matrix products, arithmetic and copies ran while one was open for 3% of the time, Pallas kernels for 19%

profile of v1, /device:TPU:0, one launch (start us, length us, event | category | flops | bytes accessed | tf_op | source)
XLA Modules:
  0.0 197.5 jit_solution(6404684518810183548)
XLA Ops:
  5.0 3.1 %collective-permute-start = (bf16[448,512]{1,0:T(8,128)(2,1)S(1)}, bf16[448,512]{1,0:T(8,128)(2,1)S(1)}, u32[]{:S(2)}, u32[]{:S(2)}) collective-permute-start(bf16[448,512]{1,0:T(8,128)(2,1)S(1)} %constant_dynamic-update-slice_fusion.refs_0_), channel_id=1, source_target_pairs={{0,8},{4,12},{8,16},{12,20},{16,24},{20,28},{24,0},{28,4},{1,9},{5... | collective-permute-start | bytes 1376264 | tf_op jit(solution)/shard_map/ppermute | solution.py:210
  8.1 2.1 %collective-permute-start.1 = (bf16[448,512]{1,0:T(8,128)(2,1)S(1)}, bf16[448,512]{1,0:T(8,128)(2,1)S(1)}, u32[]{:S(2)}, u32[]{:S(2)}) collective-permute-start(bf16[448,512]{1,0:T(8,128)(2,1)S(1)} %constant_dynamic-update-slice_fusion.refs_0_), channel_id=1, source_target_pairs={{0,24},{4,28},{8,0},{12,4},{16,8},{20,12},{24,16},{28,20},{1,25},{... | collective-permute-start | bytes 1376264 | tf_op jit(solution)/shard_map/ppermute | solution.py:210
  10.2 11.3 %collective-permute-done.refs_1_ = bf16[448,512]{1,0:T(8,128)(2,1)S(1)} collective-permute-done((bf16[448,512]{1,0:T(8,128)(2,1)S(1)}, bf16[448,512]{1,0:T(8,128)(2,1)S(1)}, u32[]{:S(2)}, u32[]{:S(2)}) %collective-permute-start) | collective-permute-done | bytes 458784 | tf_op jit(solution)/shard_map/ppermute | solution.py:210
  21.6 8.5 %collective-permute-done.1.refs_2_ = bf16[448,512]{1,0:T(8,128)(2,1)S(1)} collective-permute-done((bf16[448,512]{1,0:T(8,128)(2,1)S(1)}, bf16[448,512]{1,0:T(8,128)(2,1)S(1)}, u32[]{:S(2)}, u32[]{:S(2)}) %collective-permute-start.1) | collective-permute-done | bytes 458784 | tf_op jit(solution)/shard_map/ppermute | solution.py:210
  30.1 3.1 %collective-permute-start.3 = (bf16[224,512]{1,0:T(8,128)(2,1)S(1)}, bf16[224,512]{1,0:T(8,128)(2,1)}, u32[]{:S(2)}, u32[]{:S(2)}) collective-permute-start(bf16[224,512]{1,0:T(8,128)(2,1)S(1)} %slice.47), channel_id=1, source_target_pairs={{0,24},{4,28},{8,0},{12,4},{16,8},{20,12},{24,16},{28,20},{1,25},{... | collective-permute-start | bytes 688136 | tf_op jit(solution)/shard_map/ppermute | solution.py:210
  33.2 1.5 collective-permute-start.4
  35.3 1.5 collective-permute-start.6
  37.9 1.5 collective-permute-start.7
  40.4 1.5 collective-permute-start.8
  43.1 3.6 %collective-permute-done.4.refs_5_ = bf16[448,512]{1,0:T(8,128)(2,1)S(1)} collective-permute-done((bf16[448,512]{1,0:T(8,128)(2,1)S(1)}, bf16[448,512]{1,0:T(8,128)(2,1)S(1)}, u32[]{:S(2)}, u32[]{:S(2)}) %collective-permute-start.4) | collective-permute-done | bytes 458784 | tf_op jit(solution)/shard_map/ppermute | solution.py:214
  46.7 9.8 %collective-permute-done.5.refs_6_ = bf16[448,512]{1,0:T(8,128)(2,1)S(1)} collective-permute-done((bf16[448,512]{1,0:T(8,128)(2,1)S(1)}, bf16[448,512]{1,0:T(8,128)(2,1)S(1)}, u32[]{:S(2)}, u32[]{:S(2)}) %collective-permute-start.5) | collective-permute-done | bytes 458784 | tf_op jit(solution)/shard_map/ppermute | solution.py:214
  56.5 9.8 %collective-permute-done.6.refs_7_ = bf16[448,512]{1,0:T(8,128)(2,1)S(1)} collective-permute-done((bf16[448,512]{1,0:T(8,128)(2,1)S(1)}, bf16[448,512]{1,0:T(8,128)(2,1)S(1)}, u32[]{:S(2)}, u32[]{:S(2)}) %collective-permute-start.6) | collective-permute-done | bytes 458784 | tf_op jit(solution)/shard_map/ppermute | solution.py:214
  66.4 3.9 %collective-permute-done.7.refs_8_ = bf16[224,512]{1,0:T(8,128)(2,1)S(1)} collective-permute-done((bf16[224,512]{1,0:T(8,128)(2,1)}, bf16[224,512]{1,0:T(8,128)(2,1)S(1)}, u32[]{:S(2)}, u32[]{:S(2)}) %collective-permute-start.7) | collective-permute-done | bytes 229408 | tf_op jit(solution)/shard_map/ppermute | solution.py:214
  70.2 2.5 %collective-permute-done.8.refs_9_ = bf16[224,512]{1,0:T(8,128)(2,1)S(1)} collective-permute-done((bf16[224,512]{1,0:T(8,128)(2,1)}, bf16[224,512]{1,0:T(8,128)(2,1)S(1)}, u32[]{:S(2)}, u32[]{:S(2)}) %collective-permute-start.8) | collective-permute-done | bytes 229408 | tf_op jit(solution)/shard_map/ppermute | solution.py:214
  73.4 16.8 %shard_map.127 = (bf16[512,512]{1,0:T(8,128)(2,1)}, bf16[512,512]{1,0:T(8,128)(2,1)}, bf16[512,512]{1,0:T(8,128)(2,1)}, bf16[1024,512]{1,0:T(8,128)(2,1)}, bf16[...) custom-call(s32[1]{0:T(128)} %bitcast.3.me_ref, ...), custom_call_target="tpu_custom_call" | custom-call | tf_op jit(solution)/shard_map/pallas_call | solution.py:512
  94.0 1.6 collective-permute-start.10
  95.7 1.9 collective-permute-done.10
  104.0 1.5 collective-permute-start.12
  105.5 2.4 %collective-permute-start.13 = (bf16[256,512]{1,0:T(8,128)(2,1)S(1)}, bf16[256,512]{1,0:T(8,128)(2,1)S(1)}, u32[]{:S(2)}, u32[]{:S(2)}) collective-permute-start(bf16[256,512]{1,0:T(8,128)(2,1)S(1)} %pad_maximum_fusion.refs_0_), channel_id=1, source_target_pairs={{0,24},{4,28},{8,0},{12,4},{16,8},{20,12},{24,16},{28,20},{1,25},{... | collective-permute-start | bytes 786440 | tf_op jit(solution)/shard_map/ppermute | solution.py:210
  108.4 6.7 %collective-permute-done.12.refs_1_ = bf16[256,512]{1,0:T(8,128)(2,1)S(1)} collective-permute-done((bf16[256,512]{1,0:T(8,128)(2,1)S(1)}, bf16[256,512]{1,0:T(8,128)(2,1)S(1)}, u32[]{:S(2)}, u32[]{:S(2)}) %collective-permute-start.12) | collective-permute-done | bytes 262176 | tf_op jit(solution)/shard_map/ppermute | solution.py:210
  116.0 2.6 %collective-permute-done.13.refs_2_ = bf16[256,512]{1,0:T(8,128)(2,1)S(1)} collective-permute-done((bf16[256,512]{1,0:T(8,128)(2,1)S(1)}, bf16[256,512]{1,0:T(8,128)(2,1)S(1)}, u32[]{:S(2)}, u32[]{:S(2)}) %collective-permute-start.13) | collective-permute-done | bytes 262176 | tf_op jit(solution)/shard_map/ppermute | solution.py:210
  118.6 2.2 %collective-permute-start.15 = (bf16[128,512]{1,0:T(8,128)(2,1)S(1)}, bf16[128,512]{1,0:T(8,128)(2,1)S(1)}, u32[]{:S(2)}, u32[]{:S(2)}) collective-permute-start(bf16[128,512]{1,0:T(8,128)(2,1)S(1)} %slice.49), channel_id=1, source_target_pairs={{0,24},{4,28},{8,0},{12,4},{16,8},{20,12},{24,16},{28,20},{1,25},{... | collective-permute-start | bytes 393224 | tf_op jit(solution)/shard_map/ppermute | solution.py:210
  121.3 7.6 %collective-permute-done.16.refs_5_ = bf16[256,512]{1,0:T(8,128)(2,1)S(1)} collective-permute-done((bf16[256,512]{1,0:T(8,128)(2,1)S(1)}, bf16[256,512]{1,0:T(8,128)(2,1)S(1)}, u32[]{:S(2)}, u32[]{:S(2)}) %collective-permute-start.16) | collective-permute-done | bytes 262176 | tf_op jit(solution)/shard_map/ppermute | solution.py:214
  130.9 1.5 collective-permute-start.20
  132.4 9.3 %collective-permute-done.19.refs_8_ = bf16[128,512]{1,0:T(8,128)(2,1)S(1)} collective-permute-done((bf16[128,512]{1,0:T(8,128)(2,1)S(1)}, bf16[128,512]{1,0:T(8,128)(2,1)S(1)}, u32[]{:S(2)}, u32[]{:S(2)}) %collective-permute-start.19) | collective-permute-done | bytes 131104 | tf_op jit(solution)/shard_map/ppermute | solution.py:214
  141.6 1.5 collective-permute-done.20.refs_9_
  143.1 6.1 %shard_map.130 = (bf16[1024,512]{1,0:T(8,128)(2,1)S(1)}, bf16[1024,512]{1,0:T(8,128)(2,1)S(1)}, f32[1024,512]{1,0:T(8,128)S(1)}, f32[1024,512]{1,0:T(8,128)S(1)}...) custom-call(s32[1]{0:T(128)} %bitcast.3.me_ref, f32[1,512]{1,0:T(1,128)S(1)} %bitcast.56, ...), custom_call_target="tpu_custom_call" | custom-call | tf_op jit(solution)/shard_map/pallas_call | solution.py:559
  153.6 1.5 collective-permute-start.22
  157.9 2.0 collective-permute-start.26
  159.8 1.7 collective-permute-start.25
  162.2 31.8 %shard_map.131 = (bf16[128,512]{1,0:T(8,128)(2,1)}, bf16[128,512]{1,0:T(8,128)(2,1)}, bf16[128,512]{1,0:T(8,128)(2,1)}, f32[3,64,512]{2,1,0:T(8,128)}) custom-call(s32[1]{0:T(128)} %bitcast.3.me_ref, bf16[1024,512]{1,0:T(8,128)(2,1)} %copy-done.10, bf16[1024,512]{1,0:T(8,128)(2,1)} %copy-done.11, f32[1,512]{1,0:T(1,128)} %bitcast.53, ...), custom_call_target="tpu_custom_call" | custom-call | tf_op jit(solution)/shard_map/pallas_call | solution.py:573
  194.0 1.6 pad_maximum_fusion.1
  (99 shorter events, 32.8 us)
Async XLA Ops:
  5.0 67.7 %copy-start.19 = (bf16[448,512]{1,0:T(8,128)(2,1)}, bf16[448,512]{1,0:T(8,128)(2,1)S(1)}, u32[]{:S(2)}) copy-start(bf16[448,512]{1,0:T(8,128)(2,1)S(1)} %constant_dynamic-update-slice_fusion.refs_0_) | copy-start | bytes 1376260
  5.0 16.5 %collective-permute-start = (bf16[448,512]{1,0:T(8,128)(2,1)S(1)}, bf16[448,512]{1,0:T(8,128)(2,1)S(1)}, u32[]{:S(2)}, u32[]{:S(2)}) collective-permute-start(bf16[448,512]{1,0:T(8,128)(2,1)S(1)} %constant_dynamic-update-slice_fusion.refs_0_), channel_id=1, source_target_pairs={{0,8},{4,12},{8,16},{12,20},{16,24},{20,28},{24,0},{28,4},{1,9},{5... | collective-permute-start | bytes 1376264 | tf_op jit(solution)/shard_map/ppermute | solution.py:210
  8.1 22.0 %collective-permute-start.1 = (bf16[448,512]{1,0:T(8,128)(2,1)S(1)}, bf16[448,512]{1,0:T(8,128)(2,1)S(1)}, u32[]{:S(2)}, u32[]{:S(2)}) collective-permute-start(bf16[448,512]{1,0:T(8,128)(2,1)S(1)} %constant_dynamic-update-slice_fusion.refs_0_), channel_id=1, source_target_pairs={{0,24},{4,28},{8,0},{12,4},{16,8},{20,12},{24,16},{28,20},{1,25},{... | collective-permute-start | bytes 1376264 | tf_op jit(solution)/shard_map/ppermute | solution.py:210
  21.5 51.2 %copy-start.17 = (bf16[448,512]{1,0:T(8,128)(2,1)}, bf16[448,512]{1,0:T(8,128)(2,1)S(1)}, u32[]{:S(2)}) copy-start(bf16[448,512]{1,0:T(8,128)(2,1)S(1)} %collective-permute-done.refs_1_) | copy-start | bytes 1376260
  21.5 16.4 %collective-permute-start.2 = (bf16[224,512]{1,0:T(8,128)(2,1)S(1)}, bf16[224,512]{1,0:T(8,128)(2,1)}, u32[]{:S(2)}, u32[]{:S(2)}) collective-permute-start(bf16[224,512]{1,0:T(8,128)(2,1)S(1)} %slice.46), channel_id=1, source_target_pairs={{0,8},{4,12},{8,16},{12,20},{16,24},{20,28},{24,0},{28,4},{1,9},{5... | collective-permute-start | bytes 688136 | tf_op jit(solution)/shard_map/ppermute | solution.py:210
  30.1 42.6 %copy-start.18 = (bf16[448,512]{1,0:T(8,128)(2,1)}, bf16[448,512]{1,0:T(8,128)(2,1)S(1)}, u32[]{:S(2)}) copy-start(bf16[448,512]{1,0:T(8,128)(2,1)S(1)} %collective-permute-done.1.refs_2_) | copy-start | bytes 1376260
  30.1 10.3 %collective-permute-start.3 = (bf16[224,512]{1,0:T(8,128)(2,1)S(1)}, bf16[224,512]{1,0:T(8,128)(2,1)}, u32[]{:S(2)}, u32[]{:S(2)}) collective-permute-start(bf16[224,512]{1,0:T(8,128)(2,1)S(1)} %slice.47), channel_id=1, source_target_pairs={{0,24},{4,28},{8,0},{12,4},{16,8},{20,12},{24,16},{28,20},{1,25},{... | collective-permute-start | bytes 688136 | tf_op jit(solution)/shard_map/ppermute | solution.py:210
  33.2 13.5 %collective-permute-start.4 = (bf16[448,512]{1,0:T(8,128)(2,1)S(1)}, bf16[448,512]{1,0:T(8,128)(2,1)S(1)}, u32[]{:S(2)}, u32[]{:S(2)}) collective-permute-start(bf16[448,512]{1,0:T(8,128)(2,1)S(1)} %constant_dynamic-update-slice_fusion.refs_0_), channel_id=1, source_target_pairs={{0,4},{4,0},{8,12},{12,8},{16,20},{20,16},{24,28},{28,24},{1,5},{5... | collective-permute-start | bytes 1376264 | tf_op jit(solution)/shard_map/ppermute | solution.py:214
  34.7 21.8 %collective-permute-start.5 = (bf16[448,512]{1,0:T(8,128)(2,1)S(1)}, bf16[448,512]{1,0:T(8,128)(2,1)S(1)}, u32[]{:S(2)}, u32[]{:S(2)}) collective-permute-start(bf16[448,512]{1,0:T(8,128)(2,1)S(1)} %collective-permute-done.refs_1_), channel_id=1, source_target_pairs={{0,4},{4,0},{8,12},{12,8},{16,20},{20,16},{24,28},{28,24},{1,5},{5... | collective-permute-start | bytes 1376264 | tf_op jit(solution)/shard_map/ppermute | solution.py:214
  35.3 31.1 %collective-permute-start.6 = (bf16[448,512]{1,0:T(8,128)(2,1)S(1)}, bf16[448,512]{1,0:T(8,128)(2,1)S(1)}, u32[]{:S(2)}, u32[]{:S(2)}) collective-permute-start(bf16[448,512]{1,0:T(8,128)(2,1)S(1)} %collective-permute-done.1.refs_2_), channel_id=1, source_target_pairs={{0,4},{4,0},{8,12},{12,8},{16,20},{20,16},{24,28},{28,24},{1,5},{5... | collective-permute-start | bytes 1376264 | tf_op jit(solution)/shard_map/ppermute | solution.py:214
  37.9 32.3 %collective-permute-start.7 = (bf16[224,512]{1,0:T(8,128)(2,1)}, bf16[224,512]{1,0:T(8,128)(2,1)S(1)}, u32[]{:S(2)}, u32[]{:S(2)}) collective-permute-start(bf16[224,512]{1,0:T(8,128)(2,1)} %collective-permute-done.2.refs_3_), channel_id=1, source_target_pairs={{0,4},{4,0},{8,12},{12,8},{16,20},{20,16},{24,28},{28,24},{1,5},{5... | collective-permute-start | bytes 688136 | tf_op jit(solution)/shard_map/ppermute | solution.py:214
  40.4 32.3 %collective-permute-start.8 = (bf16[224,512]{1,0:T(8,128)(2,1)}, bf16[224,512]{1,0:T(8,128)(2,1)S(1)}, u32[]{:S(2)}, u32[]{:S(2)}) collective-permute-start(bf16[224,512]{1,0:T(8,128)(2,1)} %collective-permute-done.3.refs_4_), channel_id=1, source_target_pairs={{0,4},{4,0},{8,12},{12,8},{16,20},{20,16},{24,28},{28,24},{1,5},{5... | collective-permute-start | bytes 688136 | tf_op jit(solution)/shard_map/ppermute | solution.py:214
  43.1 47.1 %copy-start.15 = (f32[512]{0:T(512)S(1)}, f32[512]{0:T(512)}, u32[]{:S(2)}) copy-start(f32[512]{0:T(512)} %param.12) | copy-start | bytes 6148
  94.0 1.8 collective-permute-start.11
  94.0 3.7 %collective-permute-start.10 = (f32[8,128]{1,0:T(8,128)S(1)}, f32[8,128]{1,0:T(8,128)S(1)}, u32[]{:S(2)}, u32[]{:S(2)}) collective-permute-start(f32[8,128]{1,0:T(8,128)S(1)} %get-tuple-element.46), channel_id=1, source_target_pairs={{0,2},{1,3},{2,0},{3,1},{4,6},{5,7},{6,4},{7,5},{8,10},{9,11},{10,... | collective-permute-start | bytes 12296 | tf_op jit(solution)/shard_map/ppermute | solution.py:237
  95.6 3.0 %collective-permute-start.9 = (f32[8,128]{1,0:T(8,128)S(1)}, f32[8,128]{1,0:T(8,128)S(1)}, u32[]{:S(2)}, u32[]{:S(2)}) collective-permute-start(f32[8,128]{1,0:T(8,128)S(1)} %get-tuple-element.46), channel_id=1, source_target_pairs={{0,1},{1,2},{2,3},{3,0},{4,5},{5,6},{6,7},{7,4},{8,9},{9,10},{10,1... | collective-permute-start | bytes 12296 | tf_op jit(solution)/shard_map/ppermute | solution.py:237
  102.5 52.8 %collective-permute-start.24 = (bf16[3,4,64,512]{3,2,0,1:T(8,128)(2,1)}, bf16[3,4,64,512]{3,2,0,1:T(8,128)(2,1)}, u32[]{:S(2)}, u32[]{:S(2)}) collective-permute-start(bf16[3,4,64,512]{3,2,0,1:T(8,128)(2,1)} %bitcast.50), channel_id=1, source_target_pairs={{0,4},{4,0},{8,12},{12,8},{16,20},{20,16},{24,28},{28,24},{1,5},{5... | collective-permute-start | bytes 2359304 | tf_op jit(solution)/shard_map/ppermute | solution.py:214
  104.0 11.1 %collective-permute-start.12 = (bf16[256,512]{1,0:T(8,128)(2,1)S(1)}, bf16[256,512]{1,0:T(8,128)(2,1)S(1)}, u32[]{:S(2)}, u32[]{:S(2)}) collective-permute-start(bf16[256,512]{1,0:T(8,128)(2,1)S(1)} %pad_maximum_fusion.refs_0_), channel_id=1, source_target_pairs={{0,8},{4,12},{8,16},{12,20},{16,24},{20,28},{24,0},{28,4},{1,9},{5... | collective-permute-start | bytes 786440 | tf_op jit(solution)/shard_map/ppermute | solution.py:210
  105.5 13.0 %collective-permute-start.13 = (bf16[256,512]{1,0:T(8,128)(2,1)S(1)}, bf16[256,512]{1,0:T(8,128)(2,1)S(1)}, u32[]{:S(2)}, u32[]{:S(2)}) collective-permute-start(bf16[256,512]{1,0:T(8,128)(2,1)S(1)} %pad_maximum_fusion.refs_0_), channel_id=1, source_target_pairs={{0,24},{4,28},{8,0},{12,4},{16,8},{20,12},{24,16},{28,20},{1,25},{... | collective-permute-start | bytes 786440 | tf_op jit(solution)/shard_map/ppermute | solution.py:210
  107.9 20.9 %collective-permute-start.16 = (bf16[256,512]{1,0:T(8,128)(2,1)S(1)}, bf16[256,512]{1,0:T(8,128)(2,1)S(1)}, u32[]{:S(2)}, u32[]{:S(2)}) collective-permute-start(bf16[256,512]{1,0:T(8,128)(2,1)S(1)} %pad_maximum_fusion.refs_0_), channel_id=1, source_target_pairs={{0,4},{4,0},{8,12},{12,8},{16,20},{20,16},{24,28},{28,24},{1,5},{5... | collective-permute-start | bytes 786440 | tf_op jit(solution)/shard_map/ppermute | solution.py:214
  115.2 15.2 %collective-permute-start.14 = (bf16[128,512]{1,0:T(8,128)(2,1)S(1)}, bf16[128,512]{1,0:T(8,128)(2,1)S(1)}, u32[]{:S(2)}, u32[]{:S(2)}) collective-permute-start(bf16[128,512]{1,0:T(8,128)(2,1)S(1)} %slice.48), channel_id=1, source_target_pairs={{0,8},{4,12},{8,16},{12,20},{16,24},{20,28},{24,0},{28,4},{1,9},{5... | collective-permute-start | bytes 393224 | tf_op jit(solution)/shard_map/ppermute | solution.py:210
  118.6 12.3 %collective-permute-start.15 = (bf16[128,512]{1,0:T(8,128)(2,1)S(1)}, bf16[128,512]{1,0:T(8,128)(2,1)S(1)}, u32[]{:S(2)}, u32[]{:S(2)}) collective-permute-start(bf16[128,512]{1,0:T(8,128)(2,1)S(1)} %slice.49), channel_id=1, source_target_pairs={{0,24},{4,28},{8,0},{12,4},{16,8},{20,12},{24,16},{28,20},{1,25},{... | collective-permute-start | bytes 393224 | tf_op jit(solution)/shard_map/ppermute | solution.py:210
  120.8 22.3 %collective-permute-start.17 = (bf16[256,512]{1,0:T(8,128)(2,1)S(1)}, bf16[256,512]{1,0:T(8,128)(2,1)S(1)}, u32[]{:S(2)}, u32[]{:S(2)}) collective-permute-start(bf16[256,512]{1,0:T(8,128)(2,1)S(1)} %collective-permute-done.12.refs_1_), channel_id=1, source_target_pairs={{0,4},{4,0},{8,12},{12,8},{16,20},{20,16},{24,28},{28,24},{1,5},{5... | collective-permute-start | bytes 786440 | tf_op jit(solution)/shard_map/ppermute | solution.py:214
  128.8 14.3 %collective-permute-start.18 = (bf16[256,512]{1,0:T(8,128)(2,1)S(1)}, bf16[256,512]{1,0:T(8,128)(2,1)S(1)}, u32[]{:S(2)}, u32[]{:S(2)}) collective-permute-start(bf16[256,512]{1,0:T(8,128)(2,1)S(1)} %collective-permute-done.13.refs_2_), channel_id=1, source_target_pairs={{0,4},{4,0},{8,12},{12,8},{16,20},{20,16},{24,28},{28,24},{1,5},{5... | collective-permute-start | bytes 786440 | tf_op jit(solution)/shard_map/ppermute | solution.py:214
  130.3 11.3 %collective-permute-start.19 = (bf16[128,512]{1,0:T(8,128)(2,1)S(1)}, bf16[128,512]{1,0:T(8,128)(2,1)S(1)}, u32[]{:S(2)}, u32[]{:S(2)}) collective-permute-start(bf16[128,512]{1,0:T(8,128)(2,1)S(1)} %collective-permute-done.14.refs_3_), channel_id=1, source_target_pairs={{0,4},{4,0},{8,12},{12,8},{16,20},{20,16},{24,28},{28,24},{1,5},{5... | collective-permute-start | bytes 393224 | tf_op jit(solution)/shard_map/ppermute | solution.py:214
  130.9 12.3 %collective-permute-start.20 = (bf16[128,512]{1,0:T(8,128)(2,1)S(1)}, bf16[128,512]{1,0:T(8,128)(2,1)}, u32[]{:S(2)}, u32[]{:S(2)}) collective-permute-start(bf16[128,512]{1,0:T(8,128)(2,1)S(1)} %collective-permute-done.15.refs_4_), channel_id=1, source_target_pairs={{0,4},{4,0},{8,12},{12,8},{16,20},{20,16},{24,28},{28,24},{1,5},{5... | collective-permute-start | bytes 393224 | tf_op jit(solution)/shard_map/ppermute | solution.py:214
  153.6 6.3 %collective-permute-start.23 = (f32[8,1024]{1,0:T(8,128)S(1)}, f32[8,1024]{1,0:T(8,128)S(1)}, u32[]{:S(2)}, u32[]{:S(2)}) collective-permute-start(f32[8,1024]{1,0:T(8,128)S(1)} %get-tuple-element.56), channel_id=1, source_target_pairs={{0,3},{1,0},{2,1},{3,2},{4,7},{5,4},{6,5},{7,6},{8,11},{9,8},{10,9... | collective-permute-start | bytes 98312 | tf_op jit(solution)/shard_map/ppermute | solution.py:237
  153.6 7.9 %collective-permute-start.22 = (f32[8,1024]{1,0:T(8,128)S(1)}, f32[8,1024]{1,0:T(8,128)S(1)}, u32[]{:S(2)}, u32[]{:S(2)}) collective-permute-start(f32[8,1024]{1,0:T(8,128)S(1)} %get-tuple-element.56), channel_id=1, source_target_pairs={{0,2},{1,3},{2,0},{3,1},{4,6},{5,7},{6,4},{7,5},{8,10},{9,11},{10,... | collective-permute-start | bytes 98312 | tf_op jit(solution)/shard_map/ppermute | solution.py:237
  155.1 6.4 %collective-permute-start.21 = (f32[8,1024]{1,0:T(8,128)S(1)}, f32[8,1024]{1,0:T(8,128)S(1)}, u32[]{:S(2)}, u32[]{:S(2)}) collective-permute-start(f32[8,1024]{1,0:T(8,128)S(1)} %get-tuple-element.56), channel_id=1, source_target_pairs={{0,1},{1,2},{2,3},{3,0},{4,5},{5,6},{6,7},{7,4},{8,9},{9,10},{10,1... | collective-permute-start | bytes 98312 | tf_op jit(solution)/shard_map/ppermute | solution.py:237
  156.9 38.7 %collective-permute-start.27 = (bf16[3,64,512]{2,1,0:T(8,128)(2,1)S(1)}, bf16[3,64,512]{2,1,0:T(8,128)(2,1)S(1)}, u32[]{:S(2)}, u32[]{:S(2)}) collective-permute-start(bf16[3,64,512]{2,1,0:T(8,128)(2,1)S(1)} %get-tuple-element.73), channel_id=1, source_target_pairs={{0,24},{4,28},{8,0},{12,4},{16,8},{20,12},{24,16},{28,20},{1,25},{... | collective-permute-start | bytes 589832 | tf_op jit(solution)/shard_map/ppermute | solution.py:210
  157.9 37.7 %collective-permute-start.26 = (bf16[3,64,512]{2,1,0:T(8,128)(2,1)S(1)}, bf16[3,64,512]{2,1,0:T(8,128)(2,1)S(1)}, u32[]{:S(2)}, u32[]{:S(2)}) collective-permute-start(bf16[3,64,512]{2,1,0:T(8,128)(2,1)S(1)} %get-tuple-element.74), channel_id=1, source_target_pairs={{0,16},{4,20},{8,24},{12,28},{16,0},{20,4},{24,8},{28,12},{1,17},{... | collective-permute-start | bytes 589832 | tf_op jit(solution)/shard_map/ppermute | solution.py:210
  159.8 35.8 %collective-permute-start.25 = (bf16[3,64,512]{2,1,0:T(8,128)(2,1)S(1)}, bf16[3,64,512]{2,1,0:T(8,128)(2,1)S(1)}, u32[]{:S(2)}, u32[]{:S(2)}) collective-permute-start(bf16[3,64,512]{2,1,0:T(8,128)(2,1)S(1)} %get-tuple-element.72), channel_id=1, source_target_pairs={{0,8},{4,12},{8,16},{12,20},{16,24},{20,28},{24,0},{28,4},{1,9},{5... | collective-permute-start | bytes 589832 | tf_op jit(solution)/shard_map/ppermute | solution.py:210
  (21 other events, 178.6 us)

commit v2 on v1

--- a/solution.py
+++ b/solution.py
@@ -214,75 +214,78 @@
     return lax.ppermute(array, "tok", [(i, i ^ 1) for i in range(2 * ring)])
 
 
-def gather_pieces(own, ring):
-    rows = own.shape[0]
-    found = [(0, 0, own)]
-    up = down = own
+def tie(array, *earlier):
+    return lax.optimization_barrier((array, *earlier))[0]
+
+
+def along_ring(own, ring, earlier):
+    found = [(0, own)]
+    up, down = own, tie(own, earlier)
     for step in range(1, ring // 2 + 1):
+        up = shift(up, ring, 1)
+        found.append((-step, up))
         if 2 * step < ring:
-            up, down = shift(up, ring, 1), shift(down, ring, -1)
-            found += [(-step, 0, up), (step, 0, down)]
-        else:
-            half = rows // 2
-            found.append((-step, 0, shift(up[:half], ring, 1)))
-            found.append((-step, half, shift(down[half:], ring, -1)))
-    pieces = [(outer, 0, first, array) for outer, first, array in found]
-    pieces += [(outer, 1, first, swap(array, ring)) for outer, first, array in found]
-    return pieces
-
-
-def head_sums(stats):
+            down = shift(down, ring, -1)
+            found.append((step, down))
+    return found
+
+
+def head_terms(stats):
     heads = lax.axis_size("head")
-    others = [
+    return [stats] + [
         lax.ppermute(stats, "head", [(i, (i + k) % heads) for i in range(heads)])
         for k in range(1, heads)
     ]
-    return jnp.stack([stats, *others])
-
-
-def unpack_copies(layout, segments, ring, me, refs, targets, sems):
+
+
+def unpack(layout, segments, ring, me, refs, targets, sems):
     copies = []
-    outer_me, inner_me = me // 2, me % 2
-    slots = {}
-    for (outer, flip, first, rows), ref in zip(layout, refs):
-        slot = slots.setdefault((outer, flip), len(slots))
-        owner = ((outer_me + outer + ring) % ring) * 2 + (inner_me + flip) % 2
+    for slot, ((outer, flip), ref) in enumerate(zip(layout, refs)):
+        owner = ((me // 2 + outer + ring) % ring) * 2 + (me % 2 + flip) % 2
         begin = 0
         for (count, by_slot), target in zip(segments, targets):
-            low, high = max(begin, first), min(begin + count, first + rows)
-            if low < high:
-                place = slot * count + low - begin
-                if not by_slot:
-                    place = pl.multiple_of(owner * count, 16) + (low - begin)
-                copies.append(
-                    pltpu.make_async_copy(
-                        ref.at[pl.ds(low - first, high - low)],
-                        target.at[pl.ds(place, high - low)],
-                        sems.at[len(copies)],
-                    )
+            place = slot * count if by_slot else pl.multiple_of(owner * count, 16)
+            copies.append(
+                pltpu.make_async_copy(
+                    ref.at[pl.ds(begin, count)],
+                    target.at[pl.ds(place, count)],
+                    sems.at[len(copies)],
                 )
+            )
             begin += count
-    return copies
-
-
-def chunks_of(tokens):
-    step = min(ROWS, tokens)
-    return [slice(i, i + step) for i in range(0, tokens, step)]
-
-
-def fast_kernel(layout, segments, ring, me_ref, *refs):
-    count = len(layout)
-    pieces, refs = refs[:count], refs[count:]
-    (wg, wu, wd, keys, values, gk_ref, uk_ref, back_ref) = refs[:8]
-    xs, grams, blends, nexts, totals, roots = refs[8:14]
-    d_gate, d_up, hidden, sems = refs[14:]
-    copies = unpack_copies(
-        layout, segments, ring, me_ref[0], pieces, (wg, wu, wd, keys, values), sems
-    )
     for copy in copies:
         copy.start()
     for copy in copies:
         copy.wait()
+
+
+def chunks_of(tokens):
+    step = min(ROWS, tokens)
+    return [slice(i, i + step) for i in range(0, tokens, step)]
+
+
+def pack_kernel(lead, *refs):
+    sources, target, sems = refs[:-2], refs[-2], refs[-1]
+    copies, begin = [], 0
+    for place, source in enumerate(sources):
+        source = source.at[lead[place]] if lead[place] is not None else source
+        rows = source.shape[0]
+        copies.append(
+            pltpu.make_async_copy(source, target.at[pl.ds(begin, rows)], sems.at[place])
+        )
+        begin += rows
+    for copy in copies:
+        copy.start()
+    for copy in copies:
+        copy.wait()
+
+
+def fast_kernel(layout, segments, ring, me_ref, *refs):
+    count = len(layout)
+    pieces, refs = refs[:count], refs[count:]
+    (wg, wu, wd, keys, values, gk_ref, uk_ref, back_ref, totals_g, totals_u, totals_d) = refs[:11]
+    d_gate, d_up, hidden, sems = refs[11:]
+    unpack(layout, segments, ring, me_ref[0], pieces, (wg, wu, wd, keys, values), sems)
     for part in chunks_of(keys.shape[0]):
         gk = product(keys[part], wg[...])
         uk = product(keys[part], wu[...])
@@ -294,24 +297,26 @@
         d_gate[part] = (back * uk * slope).astype(bf16)
         d_up[part] = (back * active).astype(bf16)
         gk_ref[part], uk_ref[part], back_ref[part] = gk, uk, back
-    totals[0] = across(keys[...], d_gate[...])
-    totals[1] = across(keys[...], d_up[...])
-    totals[2] = -across(hidden[...], values[...])
-    for which, weight in enumerate((wg, wu, wd)):
-        total = totals[which]
-        root = jnp.sqrt(jnp.sum(total * total, keepdims=True))
-        roots[which] = jnp.broadcast_to(root, roots.shape[1:])
-        xs[which, 0] = (total / (root + fro_eps)).astype(bf16)
-        for sweep in range(NS_STEPS):
-            current = xs[which, sweep]
-            gram = against(current, current).astype(bf16)
-            blend = (cube_coef * gram.astype(f32) + fifth_coef * product(gram, gram)).astype(bf16)
-            following = (lin_coef * current.astype(f32) + product(blend, current)).astype(bf16)
-            grams[which, sweep] = gram
-            blends[which, sweep] = blend
-            if sweep + 1 < NS_STEPS:
-                xs[which, sweep + 1] = following
-        nexts[which] = (weight[...].astype(f32) - following.astype(f32)).astype(bf16)
+    totals_g[...] = across(keys[...], d_gate[...])
+    totals_u[...] = across(keys[...], d_up[...])
+    totals_d[...] = -across(hidden[...], values[...])
+
+
+def schulz_kernel(total_ref, weight, xs, grams, blends, following_ref, root_ref):
+    total = total_ref[...]
+    root = jnp.sqrt(jnp.sum(total * total, keepdims=True))
+    root_ref[...] = jnp.broadcast_to(root, root_ref.shape)
+    xs[0] = (total / (root + fro_eps)).astype(bf16)
+    for sweep in range(NS_STEPS):
+        current = xs[sweep]
+        gram = against(current, current).astype(bf16)
+        blend = (cube_coef * gram.astype(f32) + fifth_coef * product(gram, gram)).astype(bf16)
+        following = (lin_coef * current.astype(f32) + product(blend, current)).astype(bf16)
+        grams[sweep] = gram
+        blends[sweep] = blend
+        if sweep + 1 < NS_STEPS:
+            xs[sweep + 1] = following
+    following_ref[...] = (weight[...].astype(f32) - following.astype(f32)).astype(bf16)
 
 
 def row_sums(columns, tokens):
@@ -340,7 +345,7 @@
     grad_ref, d_gate, d_up, d_out, own,
 ):
     for part in chunks_of(queries.shape[0]):
-        total = jnp.sum(sums[:, :, part], axis=0)
+        total = sum(term[:, part] for term in sums)
         tokens = total.shape[1]
         square = total[0:1] / width
         inverse = lax.rsqrt(square + rms_eps)
@@ -361,77 +366,101 @@
     ).astype(bf16)
 
 
-def first_forward_kernel(queries, upstream, gain, wg, wu, wd, gq, uq, hidden, out, stats):
+def first_forward_kernel(
+    queries_ref, upstream_ref, gain, wg, wu, wd, queries, upstream, gq, uq, hidden, out, stats
+):
+    queries[...], upstream[...] = queries_ref[0], upstream_ref[0]
     forward_part(queries, upstream, gain, wg, wu, wd, gq, uq, hidden, out, stats)
 
 
 def first_backward_kernel(
-    width, queries, upstream, gain, wg, wu, wd, gq, uq, hidden, out, sums,
-    grad, partial, d_gate, d_up, d_out,
+    width, ring, me_ref, queries, upstream, gain, wg, wu, wd, gq, uq, hidden, out, *refs
 ):
+    count = len(refs) - 7
+    sums = refs[:count]
+    grad, kept, sent, d_gate, d_up, d_out, partial = refs[count:]
     backward_part(
         width, queries, upstream, gain, wg, wu, wd, gq, uq, hidden, out, sums,
         grad, d_gate, d_up, d_out, queries.shape[0],
     )
-    partial[0] = across(queries[...], d_gate[...]).astype(bf16)
-    partial[1] = across(queries[...], d_up[...]).astype(bf16)
-    partial[2] = across(hidden[...], d_out[...]).astype(bf16)
-
-
-def second_forward_kernel(
-    layout, segments, ring, me_ref, gain, nexts, *refs
-):
+    inner = me_ref[0] % 2
+    rows = kept.shape[2]
+    for which, (left, right) in enumerate(((queries, d_gate), (queries, d_up), (hidden, d_out))):
+        partial[...] = across(left[...], right[...]).astype(bf16)
+        for outer in range(ring):
+            mine = pl.multiple_of((outer * 2 + inner) * rows, 16)
+            other = pl.multiple_of((outer * 2 + 1 - inner) * rows, 16)
+            kept[outer, which] = partial[pl.ds(mine, rows)]
+            sent[outer, which] = partial[pl.ds(other, rows)]
+
+
+def pair_kernel(ring, me_ref, kept, received, own, *others):
+    outer = me_ref[0] // 2
+    own[...] = kept[outer].astype(f32) + received[outer].astype(f32)
+    for step, target in enumerate(others, 1):
+        place = (outer + step) % ring
+        target[...] = (kept[place].astype(f32) + received[place].astype(f32)).astype(bf16)
+
+
+def second_forward_kernel(layout, segments, ring, me_ref, gain, wg, wu, wd, *refs):
     count = len(layout)
     pieces, refs = refs[:count], refs[count:]
     queries, upstream, gq, uq, hidden, out, stats, sems = refs
-    copies = unpack_copies(layout, segments, ring, me_ref[0], pieces, (queries, upstream), sems)
-    for copy in copies:
-        copy.start()
-    for copy in copies:
-        copy.wait()
-    forward_part(
-        queries, upstream, gain, nexts.at[0], nexts.at[1], nexts.at[2], gq, uq, hidden, out, stats
-    )
+    unpack(layout, segments, ring, me_ref[0], pieces, (queries, upstream), sems)
+    forward_part(queries, upstream, gain, wg, wu, wd, gq, uq, hidden, out, stats)
+
+
+def second_backward_kernel(
+    width, own, grad_first, queries, upstream, gain, wg, wu, wd, gq, uq, hidden, out, *refs
+):
+    count = len(refs) - 7
+    sums = refs[:count]
+    grad, rate_g, rate_u, rate_d, d_gate, d_up, d_out = refs[count:]
+    grad[0] = grad_first[...]
+    backward_part(
+        width, queries, upstream, gain, wg, wu, wd, gq, uq, hidden, out, sums,
+        grad.at[1], d_gate, d_up, d_out, own,
+    )
+    rate_g[...] = across(queries[...], d_gate[...])
+    rate_u[...] = across(queries[...], d_up[...])
+    rate_d[...] = across(hidden[...], d_out[...])
+
+
+def schulz_back_kernel(rate, total_ref, xs, grams, blends, root_ref, cot):
+    current = (-rate[...]).astype(bf16)
+    for sweep in reversed(range(NS_STEPS)):
+        iterate, gram, blend = xs[sweep], grams[sweep], blends[sweep]
+        symmetric = (against(current, iterate) + against(iterate, current)).astype(bf16)
+        bent = product(symmetric, gram) + product(gram, symmetric)
+        mixed = (cube_coef * symmetric.astype(f32) + fifth_coef * bent).astype(bf16)
+        current = (
+            lin_coef * current.astype(f32) + product(blend, current) + product(mixed, iterate)
+        ).astype(bf16)
+    root = root_ref[0:1, 0:1]
+    norm = root + fro_eps
+    total = total_ref[...]
+    bottom = current.astype(f32)
+    inner = jnp.sum(bottom * total, keepdims=True)
+    cot[...] = (bottom / norm - total * (inner / (norm * norm * root))).astype(bf16)
 
 
 def last_kernel(
-    width, own, me_ref, queries, upstream, gain, nexts, gq, uq, hidden_q, out, sums,
-    wg, wu, wd, keys, values, gk_ref, uk_ref, back_ref, xs, grams, blends, totals, roots,
-    grad_queries, grad_keys, grad_values, grads,
-    d_gate, d_up, d_out, rates, cots, lower, upper, d_back, pk, rk, hk,
+    own, scale, me_ref, keys, values, wg, wu, wd, gk_ref, uk_ref, back_ref,
+    cot_g, cot_u, cot_d, rate_g, rate_u, rate_d, *refs,
 ):
-    backward_part(
-        width, queries, upstream, gain, nexts.at[0], nexts.at[1], nexts.at[2],
-        gq, uq, hidden_q, out, sums, grad_queries, d_gate, d_up, d_out, own,
-    )
-    rates[0] = across(queries[...], d_gate[...])
-    rates[1] = across(queries[...], d_up[...])
-    rates[2] = across(hidden_q[...], d_out[...])
-    for which in range(3):
-        current = (-rates[which]).astype(bf16)
-        for sweep in reversed(range(NS_STEPS)):
-            iterate, gram, blend = xs[which, sweep], grams[which, sweep], blends[which, sweep]
-            symmetric = (against(current, iterate) + against(iterate, current)).astype(bf16)
-            bent = product(symmetric, gram) + product(gram, symmetric)
-            mixed = (cube_coef * symmetric.astype(f32) + fifth_coef * bent).astype(bf16)
-            current = (
-                lin_coef * current.astype(f32) + product(blend, current) + product(mixed, iterate)
-            ).astype(bf16)
-        root = roots[which, 0:1, 0:1]
-        norm = root + fro_eps
-        total = totals[which]
-        bottom = current.astype(f32)
-        inner = jnp.sum(bottom * total, keepdims=True)
-        cots[which] = (bottom / norm - total * (inner / (norm * norm * root))).astype(bf16)
+    count = len(refs) - 12
+    firsts = refs[:count]
+    grad_keys, grad_values, grad_g, grad_u, grad_d = refs[count:count + 5]
+    lower, upper, d_back, pk, rk, hk, total = refs[count + 5:]
     for part in chunks_of(keys.shape[0]):
         gk, uk, back = gk_ref[part], uk_ref[part], back_ref[part]
         sigma = jax.nn.sigmoid(gk)
         active = gk * sigma
         slope = sigma * (1.0 + gk * (1.0 - sigma))
         curve = sigma * (1.0 - sigma) * (2.0 + gk * (1.0 - 2.0 * sigma))
-        ek = product(keys[part], cots[0])
-        fk = product(keys[part], cots[1])
-        hk_part = -against(values[part], cots[2])
+        ek = product(keys[part], cot_g[...])
+        fk = product(keys[part], cot_u[...])
+        hk_part = -against(values[part], cot_d[...])
         d_back[part] = (ek * uk * slope + fk * active).astype(bf16)
         upper[part] = (ek * back * slope + hk_part * active).astype(bf16)
         lower[part] = (
@@ -442,19 +471,25 @@
             rk[...] = (back * active).astype(bf16)[:own]
             hk[...] = (active * uk).astype(bf16)[:own]
     grad_keys[...] = (
-        against(pk[...], cots[0])
-        + against(rk[...], cots[1])
+        against(pk[...], cot_g[...])
+        + against(rk[...], cot_u[...])
         + against(lower[:own], wg[...])
         + against(upper[:own], wu[...])
     ).astype(bf16)
-    grad_values[...] = (-product(hk[...], cots[2]) - product(d_back[:own], wd[...])).astype(bf16)
-    rates[0] += across(keys[...], lower[...])
-    rates[1] += across(keys[...], upper[...])
-    rates[2] -= across(d_back[...], values[...])
-    rows = grads.shape[1]
+    grad_values[...] = (
+        -product(hk[...], cot_d[...]) - product(d_back[:own], wd[...])
+    ).astype(bf16)
+    rows = grad_g.shape[1]
     start = pl.multiple_of(me_ref[0] * rows, 16)
-    for which in range(3):
-        grads[which] = rates[which, pl.ds(start, rows)]
+    for which, (left, right, rate, grad) in enumerate((
+        (keys, lower, rate_g, grad_g), (keys, upper, rate_u, grad_u), (d_back, values, rate_d, grad_d)
+    )):
+        total[...] = across(left[...], right[...])
+        second = total[pl.ds(start, rows)]
+        first = sum(ref[which].astype(f32) for ref in firsts)
+        rate_rows = rate[pl.ds(start, rows)]
+        both = first - second if which == 2 else first + second
+        grad[0] = (both + rate_rows) * scale
 
 
 def vmem():
@@ -469,23 +504,13 @@
     return pl.BlockSpec(memory_space=pl.ANY)
 
 
+def cost(rows, depth, columns, products):
+    flops = 2 * rows * depth * columns * products
+    return pl.CostEstimate(flops=flops, bytes_accessed=flops // 512, transcendentals=0)
+
+
 def params(mib):
     return pltpu.CompilerParams(vmem_limit_bytes=mib * 2**20)
-
-
-def reduce_first(partial, ring, me):
-    whole, height, depth = partial.shape
-    inner = me % 2
-    blocks = partial.reshape(whole, ring, 2, height // (2 * ring), depth)
-    kept = lax.dynamic_index_in_dim(blocks, inner, 2, keepdims=False)
-    sent = lax.dynamic_index_in_dim(blocks, 1 - inner, 2, keepdims=False)
-    pair = kept.astype(f32) + swap(sent, ring).astype(f32)
-    outer = me // 2
-    result = lax.dynamic_index_in_dim(pair, outer, 1, keepdims=False)
-    for step in range(1, ring):
-        block = lax.dynamic_index_in_dim(pair, (outer + step) % ring, 1, keepdims=False)
-        result = result + shift(block.astype(bf16), ring, step).astype(f32)
-    return result
 
 
 def gather_tokens(queries, keys, values, upstream, out_gain, gate_weight, up_weight, down_weight):
@@ -502,60 +527,99 @@
     gain = out_gain[None]
     S = jax.ShapeDtypeStruct
 
-    packed = jnp.concatenate([gate_weight[0], up_weight[0], down_weight[0], keys, values])
-    pieces = gather_pieces(packed, ring)
+    matrix = (depth, hidden)
+    wide, narrow = S(matrix, f32), S(matrix, bf16)
+
+    def pack(arrays, lead):
+        rows = sum(array.shape[-2] for array in arrays)
+        return pl.pallas_call(
+            functools.partial(pack_kernel, lead),
+            out_shape=S((rows, depth), bf16),
+            in_specs=[anywhere()] * len(arrays),
+            out_specs=anywhere(),
+            scratch_shapes=[pltpu.SemaphoreType.DMA((len(arrays),))],
+            compiler_params=params(4),
+        )(*arrays)
+
+    packed = pack((gate_weight, up_weight, down_weight, keys, values), (0, 0, 0, None, None))
+    packed_second = pack((queries, upstream), (1, 1))
+    swapped = [swap(packed, ring)]
+    outers = along_ring(packed, ring, swapped[0])
+    swapped += [swap(array, ring) for _, array in outers[1:]]
+    last = outers[-1][1]
+    near = swapped[max(ring - 2, 0)]
+    layout = [(outer, 0) for outer, _ in outers] + [(outer, 1) for outer, _ in outers]
+    pieces = [array for _, array in outers] + swapped
     segments = ((rows, False), (rows, False), (down_weight.shape[1], False), (own, True), (own, True))
-    layout = [(o, f, r, a.shape[0]) for o, f, r, a in pieces]
-    matrix = (depth, hidden)
-    (
-        wg, wu, wd, all_keys, all_values, gk, uk, back, xs, grams, blends, nexts, totals, roots
-    ) = pl.pallas_call(
+    (wg, wu, wd, all_keys, all_values, gk, uk, back, *totals) = pl.pallas_call(
         functools.partial(fast_kernel, layout, segments, ring),
         out_shape=(
-            S(matrix, bf16), S(matrix, bf16), S(matrix, bf16),
-            S((tokens, depth), bf16), S((tokens, depth), bf16),
+            narrow, narrow, narrow, S((tokens, depth), bf16), S((tokens, depth), bf16),
             S((tokens, hidden), f32), S((tokens, hidden), f32), S((tokens, hidden), f32),
-            S((3, NS_STEPS, *matrix), bf16), S((3, NS_STEPS, *matrix), bf16),
-            S((3, NS_STEPS, *matrix), bf16), S((3, *matrix), bf16),
-            S((3, *matrix), f32), S((3, 8, 128), f32),
+            wide, wide, wide,
         ),
         in_specs=[smem()] + [anywhere()] * len(pieces),
-        out_specs=[vmem()] * 14,
-        scratch_shapes=[
-            pltpu.VMEM((tokens, hidden), bf16),
-            pltpu.VMEM((tokens, hidden), bf16),
-            pltpu.VMEM((tokens, hidden), bf16),
-            pltpu.SemaphoreType.DMA((5 * len(pieces),)),
-        ],
-        compiler_params=params(56),
-    )(me_ref, *[piece[3] for piece in pieces])
-
-    gq0, uq0, hidden0, out0, stats0 = pl.pallas_call(
+        out_specs=[vmem()] * 11,
+        scratch_shapes=[pltpu.VMEM((tokens, hidden), bf16)] * 3
+        + [pltpu.SemaphoreType.DMA((5 * len(pieces),))],
+        cost_estimate=cost(tokens, depth, hidden, 6),
+        compiler_params=params(24),
+    )(me_ref, *pieces)
+
+    queries0, upstream0, gq0, uq0, hidden0, out0, stats0 = pl.pallas_call(
         first_forward_kernel,
         out_shape=(
+            S((own, depth), bf16), S((own, depth), bf16),
             S((own, hidden), f32), S((own, hidden), f32), S((own, hidden), bf16),
             S((own, depth), f32), S((8, own), f32),
         ),
         in_specs=[vmem()] * 6,
-        out_specs=[vmem()] * 5,
+        out_specs=[vmem()] * 7,
+        cost_estimate=cost(own, depth, hidden, 3),
         compiler_params=params(16),
-    )(queries[0], upstream[0], gain, wg, wu, wd)
-    sums0 = head_sums(stats0)
-    grad_first, partial = pl.pallas_call(
-        functools.partial(first_backward_kernel, width),
-        out_shape=(S((own, depth), bf16), S((3, *matrix), bf16)),
-        in_specs=[vmem()] * 11,
-        out_specs=[vmem()] * 2,
-        scratch_shapes=[pltpu.VMEM((own, hidden), bf16)] * 2 + [pltpu.VMEM((own, depth), bf16)],
-        compiler_params=params(24),
-    )(queries[0], upstream[0], gain, wg, wu, wd, gq0, uq0, hidden0, out0, sums0)
-    first_rows = reduce_first(partial, ring, me)
-
-    packed = jnp.concatenate([queries[1], upstream[1]])
-    packed, _ = lax.optimization_barrier((packed, pieces[-1][3]))
-    pieces = gather_pieces(packed, ring)
+    )(queries, upstream, gain, wg, wu, wd)
+
+    def schulz(which, total):
+        return pl.pallas_call(
+            schulz_kernel,
+            out_shape=(
+                S((NS_STEPS, *matrix), bf16), S((NS_STEPS, *matrix), bf16),
+                S((NS_STEPS, *matrix), bf16), narrow, S((8, 128), f32),
+            ),
+            in_specs=[vmem()] * 2,
+            out_specs=[vmem()] * 5,
+            cost_estimate=cost(depth, depth, hidden, 3 * NS_STEPS),
+            compiler_params=params(16),
+        )(total, (wg, wu, wd)[which])
+
+    terms0 = head_terms(stats0)
+    grad_first, kept, sent = pl.pallas_call(
+        functools.partial(first_backward_kernel, width, ring),
+        out_shape=(
+            S((own, depth), bf16), S((ring, 3, rows, hidden), bf16), S((ring, 3, rows, hidden), bf16),
+        ),
+        in_specs=[smem()] + [vmem()] * (10 + len(terms0)),
+        out_specs=[vmem()] * 3,
+        scratch_shapes=[pltpu.VMEM((own, hidden), bf16)] * 2
+        + [pltpu.VMEM((own, depth), bf16), pltpu.VMEM(matrix, bf16)],
+        cost_estimate=cost(own, depth, hidden, 6),
+        compiler_params=params(20),
+    )(me_ref, queries0, upstream0, gain, wg, wu, wd, gq0, uq0, hidden0, out0, *terms0)
+
+    forward = [
+        schulz(0, totals[0]), schulz(1, tie(totals[1], *terms0)), schulz(2, tie(totals[2], sent))
+    ]
+
+    outers = along_ring(tie(packed_second, last), ring, last)
+    after = (near, None, totals[0], forward[0][3])
+    swapped = []
+    for place, (_, array) in enumerate(outers):
+        earlier = after[min(place, 3)]
+        swapped.append(swap(array if earlier is None else tie(array, earlier), ring))
+    near = swapped[max(ring - 2, 0)]
+    pieces = [array for _, array in outers] + swapped
     segments = ((own, True), (own, True))
-    layout = [(o, f, r, a.shape[0]) for o, f, r, a in pieces]
+    seconds = [forward[which][3] for which in range(3)]
     all_queries, all_upstream, gq, uq, hidden_q, out, stats = pl.pallas_call(
         functools.partial(second_forward_kernel, layout, segments, ring),
         out_shape=(
@@ -563,42 +627,69 @@
             S((tokens, hidden), f32), S((tokens, hidden), f32), S((tokens, hidden), bf16),
             S((tokens, depth), f32), S((8, tokens), f32),
         ),
-        in_specs=[smem(), vmem(), vmem()] + [anywhere()] * len(pieces),
+        in_specs=[smem()] + [vmem()] * 4 + [anywhere()] * len(pieces),
         out_specs=[vmem()] * 7,
         scratch_shapes=[pltpu.SemaphoreType.DMA((2 * len(pieces),))],
-        compiler_params=params(32),
-    )(me_ref, gain, nexts, *[piece[3] for piece in pieces])
-    sums = head_sums(stats)
-
-    grad_second, grad_keys, grad_values, last_rows = pl.pallas_call(
-        functools.partial(last_kernel, width, own),
+        cost_estimate=cost(tokens, depth, hidden, 3),
+        compiler_params=params(24),
+    )(me_ref, gain, *seconds, *pieces)
+    terms = head_terms(stats)
+
+    block = S((3, rows, hidden), bf16)
+    summed = pl.pallas_call(
+        functools.partial(pair_kernel, ring),
+        out_shape=(S((3, rows, hidden), f32),) + (block,) * (ring - 1),
+        in_specs=[smem()] + [vmem()] * 2,
+        out_specs=[vmem()] * ring,
+        compiler_params=params(12),
+    )(me_ref, kept, swap(tie(sent, near), ring))
+    firsts = [summed[0]] + [shift(summed[step], ring, step) for step in range(1, ring)]
+
+    grad_queries, *rates = pl.pallas_call(
+        functools.partial(second_backward_kernel, width, own),
+        out_shape=(S((2, own, depth), bf16), wide, wide, wide),
+        in_specs=[vmem()] * (11 + len(terms)),
+        out_specs=[vmem()] * 4,
+        scratch_shapes=[pltpu.VMEM((tokens, hidden), bf16)] * 2
+        + [pltpu.VMEM((tokens, depth), bf16)],
+        cost_estimate=cost(tokens, depth, hidden, 4),
+        compiler_params=params(20),
+    )(grad_first, all_queries, all_upstream, gain, *seconds, gq, uq, hidden_q, out, *terms)
+
+    cots = [
+        pl.pallas_call(
+            schulz_back_kernel,
+            out_shape=narrow,
+            in_specs=[vmem()] * 6,
+            out_specs=vmem(),
+            cost_estimate=cost(depth, depth, hidden, 6 * NS_STEPS),
+            compiler_params=params(16),
+        )(rates[which], totals[which], *forward[which][:3], forward[which][4])
+        for which in range(3)
+    ]
+
+    return (grad_queries, *pl.pallas_call(
+        functools.partial(last_kernel, own, scale),
         out_shape=(
-            S((own, depth), bf16), S((own, depth), bf16), S((own, depth), bf16),
-            S((3, rows, hidden), f32),
+            S((own, depth), bf16), S((own, depth), bf16),
+            S((1, rows, hidden), f32), S((1, rows, hidden), f32), S((1, rows, hidden), f32),
         ),
-        in_specs=[smem()] + [vmem()] * 22,
-        out_specs=[vmem()] * 4,
+        in_specs=[smem()] + [vmem()] * (14 + len(firsts)),
+        out_specs=[vmem()] * 5,
         scratch_shapes=[
-            pltpu.VMEM((tokens, hidden), bf16),
-            pltpu.VMEM((tokens, hidden), bf16),
-            pltpu.VMEM((tokens, depth), bf16),
-            pltpu.VMEM((3, *matrix), f32),
-            pltpu.VMEM((3, *matrix), bf16),
             pltpu.VMEM((tokens, hidden), bf16),
             pltpu.VMEM((tokens, hidden), bf16),
             pltpu.VMEM((tokens, hidden), bf16),
             pltpu.VMEM((own, hidden), bf16),
             pltpu.VMEM((own, hidden), bf16),
             pltpu.VMEM((own, hidden), bf16),
+            pltpu.VMEM(matrix, f32),
         ],
-        compiler_params=params(60),
+        cost_estimate=cost(tokens, depth, hidden, 7),
+        compiler_params=params(24),
     )(
-        me_ref, all_queries, all_upstream, gain, nexts, gq, uq, hidden_q, out, sums,
-        wg, wu, wd, all_keys, all_values, gk, uk, back, xs, grams, blends, totals, roots,
-    )
-    grads = (last_rows + first_rows) * scale
-    grad_queries = jnp.stack([grad_first, grad_second])
-    return (grad_queries, grad_keys, grad_values, grads[0:1], grads[1:2], grads[2:3])
+        me_ref, all_keys, all_values, wg, wu, wd, gk, uk, back, *cots, *rates, *firsts,
+    ))
 
 
 def per_device(queries, keys, values, upstream, out_gain, gate_weight, up_weight, down_weight):

time: 198 us -> 153 us (0.77); the launches traced: 198 us -> 150 us
  waiting for transfers between devices: 82.1 us -> 63 us
  local copies, waits for them, and re-layouts: 17.2 us -> 6.24 us
  starting transfers between devices: 35.9 us -> 29.4 us
  Pallas kernels: 56.5 us -> 50.9 us
  other arithmetic: 4.9 us -> 0 us
    ppermute x11 -> x9, waiting for transfers between devices: 47.9 us -> 27.5 us  [swap(): return lax.ppermute(array, 'tok', [(i, i ^ 1) for i in range(2 * ring)])]
    pallas_call x1, Pallas kernels: 16.8 us -> 10.5 us  [gather_tokens(): pl.pallas_call(functools.partial(fast_kernel, layout, segments, ring), ou...]
    unnamed x54 -> x24, local copies, waits for them, and re-layouts: 12.3 us -> 6.24 us
    ppermute x11 -> x9, starting transfers between devices: 19.9 us -> 14.1 us  [shift(): return lax.ppermute(array, 'tok', pairs)]
    another operation x3 -> x0, other arithmetic: 2.3 us -> none  [the longest x1 1.63 us: gather_tokens(): grad_queries = jnp.stack([grad_first, grad_second])]
    pallas_call x3 -> x13, Pallas kernels: 33.6 us -> 35.5 us  [the longest x3 12.9 us: gather_tokens(): pl.pallas_call(schulz_back_kernel, out_shape=narrow, in_specs=[vmem()] *...]
    ppermute x11 -> x9, waiting for transfers between devices: 31.3 us -> 32.7 us  [shift(): return lax.ppermute(array, 'tok', pairs)]
    ppermute x11 -> x9, starting transfers between devices: 12.5 us -> 12.2 us  [swap(): return lax.ppermute(array, 'tok', [(i, i ^ 1) for i in range(2 * ring)])]
  transfers between devices with their start and end apart: 28 -> 24, of which waited for: 16 -> 13; matrix products, arithmetic and copies ran while one was open for 3% -> 0% of each run, Pallas kernels for 19% -> 25%
where the time goes in v2:
time: 153 us; the launch traced here: 150 us
  waiting for transfers between devices  63 us (41%)
  Pallas kernels  50.9 us (33%)
  starting transfers between devices  29.4 us (19%)
  local copies, waits for them, and re-layouts  6.24 us (4%)
    ppermute x9, waiting for transfers between devices, shift(): return lax.ppermute(array, 'tok', pairs)  32.7 us
    ppermute x9, waiting for transfers between devices, swap(): return lax.ppermute(array, 'tok', [(i, i ^ 1) for i in range(2 * ring)])  27.5 us
    ppermute x9, starting transfers between devices, shift(): return lax.ppermute(array, 'tok', pairs)  14.1 us
    pallas_call x3, Pallas kernels, gather_tokens(): pl.pallas_call(schulz_back_kernel, out_shape=narrow, in_specs=[vmem()] *...  12.9 us
    ppermute x9, starting transfers between devices, swap(): return lax.ppermute(array, 'tok', [(i, i ^ 1) for i in range(2 * ring)])  12.2 us
    pallas_call x1, Pallas kernels, gather_tokens(): pl.pallas_call(functools.partial(fast_kernel, layout, segments, ring), ou...  10.5 us
    pallas_call x3, Pallas kernels, schulz(): pl.pallas_call(schulz_kernel, out_shape=(S((NS_STEPS, *matrix), bf16), S(...  7.61 us
    pallas_call x1, Pallas kernels, gather_tokens(): pl.pallas_call(functools.partial(last_kernel, own, scale), out_shape=(S((...  7.32 us
  transfers between devices with their start and end apart: 24, of which 13 were waited for; matrix products, arithmetic and copies ran while one was open for 0% of the time, Pallas kernels for 25%

profile of v2, /device:TPU:0, one launch (start us, length us, event | category | flops | bytes accessed | tf_op | source)
XLA Modules:
  0.0 150.4 jit_solution(4976907070794720675)
XLA Ops:
  5.6 3.0 %collective-permute-start.1 = (bf16[448,512]{1,0:T(8,128)(2,1)S(1)}, bf16[448,512]{1,0:T(8,128)(2,1)S(1)}, u32[]{:S(2)}, u32[]{:S(2)}) collective-permute-start(bf16[448,512]{1,0:T(8,128)(2,1)S(1)} %shard_map.127.refs_0_), channel_id=1, source_target_pairs={{0,4},{4,0},{8,12},{12,8},{16,20},{20,16},{24,28},{28,24},{1,5},{5... | collective-permute-start | bytes 1376264 | tf_op jit(solution)/shard_map/ppermute | solution.py:214
  8.6 1.6 %collective-permute-start = (bf16[448,512]{1,0:T(8,128)(2,1)S(1)}, bf16[448,512]{1,0:T(8,128)(2,1)S(1)}, u32[]{:S(2)}, u32[]{:S(2)}) collective-permute-start(bf16[448,512]{1,0:T(8,128)(2,1)S(1)} %shard_map.127.refs_0_), channel_id=1, source_target_pairs={{0,8},{4,12},{8,16},{12,20},{16,24},{20,28},{24,0},{28,4},{1,9},{5... | collective-permute-start | bytes 1376264 | tf_op jit(solution)/shard_map/ppermute | solution.py:210
  10.2 8.9 %collective-permute-done.1.refs_4_ = bf16[448,512]{1,0:T(8,128)(2,1)S(1)} collective-permute-done((bf16[448,512]{1,0:T(8,128)(2,1)S(1)}, bf16[448,512]{1,0:T(8,128)(2,1)S(1)}, u32[]{:S(2)}, u32[]{:S(2)}) %collective-permute-start.1) | collective-permute-done | bytes 458784 | tf_op jit(solution)/shard_map/ppermute | solution.py:214
  19.1 3.9 %collective-permute-start.2 = (bf16[448,512]{1,0:T(8,128)(2,1)S(1)}, bf16[448,512]{1,0:T(8,128)(2,1)S(1)}, u32[]{:S(2)}, u32[]{:S(2)}) collective-permute-start(bf16[448,512]{1,0:T(8,128)(2,1)S(1)} %shard_map.127.refs_0_), channel_id=1, source_target_pairs={{0,24},{4,28},{8,0},{12,4},{16,8},{20,12},{24,16},{28,20},{1,25},{... | collective-permute-start | bytes 1376264 | tf_op jit(solution)/shard_map/ppermute | solution.py:210
  23.0 1.5 collective-permute-start.4
  24.5 9.5 %collective-permute-done.2.refs_2_ = bf16[448,512]{1,0:T(8,128)(2,1)S(1)} collective-permute-done((bf16[448,512]{1,0:T(8,128)(2,1)S(1)}, bf16[448,512]{1,0:T(8,128)(2,1)S(1)}, u32[]{:S(2)}, u32[]{:S(2)}) %collective-permute-start.2) | collective-permute-done | bytes 458784 | tf_op jit(solution)/shard_map/ppermute | solution.py:210
  35.4 7.2 %collective-permute-done.3.refs_3_ = bf16[448,512]{1,0:T(8,128)(2,1)S(1)} collective-permute-done((bf16[448,512]{1,0:T(8,128)(2,1)S(1)}, bf16[448,512]{1,0:T(8,128)(2,1)S(1)}, u32[]{:S(2)}, u32[]{:S(2)}) %collective-permute-start.3) | collective-permute-done | bytes 458784 | tf_op jit(solution)/shard_map/ppermute | solution.py:210
  42.6 1.5 collective-permute-start.6
  46.3 1.7 %collective-permute-start.10 = (bf16[256,512]{1,0:T(8,128)(2,1)S(1)}, bf16[256,512]{1,0:T(8,128)(2,1)}, u32[]{:S(2)}, u32[]{:S(2)}) collective-permute-start(bf16[256,512]{1,0:T(8,128)(2,1)S(1)} %shard_map.134.refs_0_), channel_id=1, source_target_pairs={{0,8},{4,12},{8,16},{12,20},{16,24},{20,28},{24,0},{28,4},{1,9},{5... | collective-permute-start | bytes 786440 | tf_op jit(solution)/shard_map/ppermute | solution.py:210
  48.0 2.2 %collective-permute-start.11 = (bf16[256,512]{1,0:T(8,128)(2,1)S(1)}, bf16[256,512]{1,0:T(8,128)(2,1)S(1)}, u32[]{:S(2)}, u32[]{:S(2)}) collective-permute-start(bf16[256,512]{1,0:T(8,128)(2,1)S(1)} %shard_map.134.refs_0_), channel_id=1, source_target_pairs={{0,24},{4,28},{8,0},{12,4},{16,8},{20,12},{24,16},{28,20},{1,25},{... | collective-permute-start | bytes 786440 | tf_op jit(solution)/shard_map/ppermute | solution.py:210
  50.2 7.4 %collective-permute-done.10.refs_1_ = bf16[256,512]{1,0:T(8,128)(2,1)} collective-permute-done((bf16[256,512]{1,0:T(8,128)(2,1)S(1)}, bf16[256,512]{1,0:T(8,128)(2,1)}, u32[]{:S(2)}, u32[]{:S(2)}) %collective-permute-start.10) | collective-permute-done | bytes 262176 | tf_op jit(solution)/shard_map/ppermute | solution.py:210
  57.7 10.5 %shard_map.128 = (bf16[512,512]{1,0:T(8,128)(2,1)S(1)}, bf16[512,512]{1,0:T(8,128)(2,1)S(1)}, bf16[512,512]{1,0:T(8,128)(2,1)S(1)}, bf16[1024,512]{1,0:T(8,128)(...) custom-call(s32[1]{0:T(128)} %bitcast.me_ref, ...), custom_call_target="tpu_custom_call" | custom-call | flops 3221225472 | bytes 6291456 | tf_op jit(solution)/shard_map/pallas_call | solution.py:554
  68.9 1.6 %collective-permute-start.8 = (f32[8,128]{1,0:T(8,128)S(1)}, f32[8,128]{1,0:T(8,128)S(1)}, u32[]{:S(2)}, u32[]{:S(2)}) collective-permute-start(f32[8,128]{1,0:T(8,128)S(1)} %get-tuple-element.81.refs_0_), channel_id=1, source_target_pairs={{0,2},{1,3},{2,0},{3,1},{4,6},{5,7},{6,4},{7,5},{8,10},{9,11},{10,... | collective-permute-start | bytes 12296 | tf_op jit(solution)/shard_map/ppermute | solution.py:236
  70.6 2.5 %shard_map.131 = (bf16[2,512,512]{2,1,0:T(8,128)(2,1)S(1)}, bf16[2,512,512]{2,1,0:T(8,128)(2,1)S(1)}, bf16[2,512,512]{2,1,0:T(8,128)(2,1)S(1)}, bf16[512,512]{1,0:T(8,128)(2,1)S(1)}, f32[8,128]{1,0:T(8,128)S(1)}) custom-call(f32[512,512]{1,0:T(8,128)S(1)} %get-tuple-element.83.total_ref, bf16[512,512]{1,0:T(8,128)(2,1)S(1)} %get-tuple-element.72.wg.weight), custom_call_target="tpu_custom_call" | custom-call | flops 1610612736 | bytes 3145728 | tf_op jit(solution)/shard_map/pallas_call | solution.py:583
  73.8 1.5 collective-permute-start.13
  75.8 1.6 %shard_map.130 = (bf16[128,512]{1,0:T(8,128)(2,1)S(1)}, bf16[4,3,64,512]{3,2,1,0:T(8,128)(2,1)S(1)}, bf16[4,3,64,512]{3,2,1,0:T(8,128)(2,1)S(1)}) custom-call(s32[1]{0:T(128)} %bitcast.me_ref, bf16[128,512]{1,0:T(8,128)(2,1)S(1)} %get-tuple-element.75.queries, bf16[128,512]{1,0:T(8,128)(2,1)S(1)} %get-tuple-element.76.upstream, f32[1,512]{1,0:T(1,128)S(1)} %bitcast.3, ...), custom_call_target="tpu_custom_call" | custom-call | flops 402653184 | bytes 786432 | tf_op jit(solution)/shard_map/pallas_call | solution.py:596
  77.4 1.6 %collective-permute-start.16 = (bf16[256,512]{1,0:T(8,128)(2,1)S(1)}, bf16[256,512]{1,0:T(8,128)(2,1)S(1)}, u32[]{:S(2)}, u32[]{:S(2)}) collective-permute-start(bf16[256,512]{1,0:T(8,128)(2,1)S(1)} %collective-permute-done.12.refs_3_), channel_id=1, source_target_pairs={{0,4},{4,0},{8,12},{12,8},{16,20},{20,16},{24,28},{28,24},{1,5},{5... | collective-permute-start | bytes 786440 | tf_op jit(solution)/shard_map/ppermute | solution.py:214
  79.0 2.5 %shard_map.133 = (bf16[2,512,512]{2,1,0:T(8,128)(2,1)S(1)}, bf16[2,512,512]{2,1,0:T(8,128)(2,1)S(1)}, bf16[2,512,512]{2,1,0:T(8,128)(2,1)S(1)}, bf16[512,512]{1,0:T(8,128)(2,1)S(1)}, f32[8,128]{1,0:T(8,128)S(1)}) custom-call(f32[512,512]{1,0:T(8,128)S(1)} %get-tuple-element.90.total_ref, bf16[512,512]{1,0:T(8,128)(2,1)S(1)} %get-tuple-element.74.wd.weight), custom_call_target="tpu_custom_call" | custom-call | flops 1610612736 | bytes 3145728 | tf_op jit(solution)/shard_map/pallas_call | solution.py:583
  81.5 2.5 %shard_map.132 = (bf16[2,512,512]{2,1,0:T(8,128)(2,1)S(1)}, bf16[2,512,512]{2,1,0:T(8,128)(2,1)S(1)}, bf16[2,512,512]{2,1,0:T(8,128)(2,1)S(1)}, bf16[512,512]{1,0:T(8,128)(2,1)S(1)}, f32[8,128]{1,0:T(8,128)S(1)}) custom-call(f32[512,512]{1,0:T(8,128)S(1)} %get-tuple-element.86.total_ref, bf16[512,512]{1,0:T(8,128)(2,1)S(1)} %get-tuple-element.73.wu.weight), custom_call_target="tpu_custom_call" | custom-call | flops 1610612736 | bytes 3145728 | tf_op jit(solution)/shard_map/pallas_call | solution.py:583
  84.1 4.1 %collective-permute-done.13.refs_4_ = bf16[256,512]{1,0:T(8,128)(2,1)S(1)} collective-permute-done((bf16[256,512]{1,0:T(8,128)(2,1)S(1)}, bf16[256,512]{1,0:T(8,128)(2,1)S(1)}, u32[]{:S(2)}, u32[]{:S(2)}) %collective-permute-start.13) | collective-permute-done | bytes 262176 | tf_op jit(solution)/shard_map/ppermute | solution.py:214
  88.2 5.6 %collective-permute-done.15.refs_6_ = bf16[256,512]{1,0:T(8,128)(2,1)S(1)} collective-permute-done((bf16[256,512]{1,0:T(8,128)(2,1)S(1)}, bf16[256,512]{1,0:T(8,128)(2,1)S(1)}, u32[]{:S(2)}, u32[]{:S(2)}) %collective-permute-start.15) | collective-permute-done | bytes 262176 | tf_op jit(solution)/shard_map/ppermute | solution.py:214
  93.8 5.2 %collective-permute-done.16.refs_7_ = bf16[256,512]{1,0:T(8,128)(2,1)S(1)} collective-permute-done((bf16[256,512]{1,0:T(8,128)(2,1)S(1)}, bf16[256,512]{1,0:T(8,128)(2,1)S(1)}, u32[]{:S(2)}, u32[]{:S(2)}) %collective-permute-start.16) | collective-permute-done | bytes 262176 | tf_op jit(solution)/shard_map/ppermute | solution.py:214
  99.0 4.8 %shard_map.135 = (bf16[1024,512]{1,0:T(8,128)(2,1)S(1)}, bf16[1024,512]{1,0:T(8,128)(2,1)S(1)}, f32[1024,512]{1,0:T(8,128)S(1)}, f32[1024,512]{1,0:T(8,128)S(1)}...) custom-call(s32[1]{0:T(128)} %bitcast.me_ref, f32[1,512]{1,0:T(1,128)S(1)} %bitcast.4, ...), custom_call_target="tpu_custom_call" | custom-call | flops 1610612736 | bytes 3145728 | tf_op jit(solution)/shard_map/pallas_call | solution.py:623
  105.9 2.4 %collective-permute-done.18.refs_2_ = f32[8,1024]{1,0:T(8,128)S(1)} collective-permute-done((f32[8,1024]{1,0:T(8,128)S(1)}, f32[8,1024]{1,0:T(8,128)S(1)}, u32[]{:S(2)}, u32[]{:S(2)}) %collective-permute-start.18) | collective-permute-done | bytes 32800 | tf_op jit(solution)/shard_map/ppermute | solution.py:236
  108.6 4.4 %shard_map.136 = (bf16[2,128,512]{2,1,0:T(8,128)(2,1)}, f32[512,512]{1,0:T(8,128)S(1)}, f32[512,512]{1,0:T(8,128)S(1)}, f32[512,512]{1,0:T(8,128)S(1)}) custom-call(bf16[128,512]{1,0:T(8,128)(2,1)S(1)} %get-tuple-element.82.grad_first, bf16[1024,512]{1,0:T(8,128)(2,1)S(1)} %get-tuple-element.97.queries, bf16[1024,512]{1,0:T(8,128)(2,1)S(1)} %get-tuple-element.98.upstream, ...), custom_call_target="tpu_custom_call" | custom-call | flops 2147483648 | bytes 4194304 | tf_op jit(solution)/shard_map/pallas_call | solution.py:648
  113.0 4.3 %shard_map.139.cot_d = bf16[512,512]{1,0:T(8,128)(2,1)S(1)} custom-call(f32[512,512]{1,0:T(8,128)S(1)} %get-tuple-element.120.rate.rate_d, f32[512,512]{1,0:T(8,128)S(1)} %get-tuple-element.90.total_ref, bf16[2,512,512]{2,1,0:T(8,128)(2,1)S(1)} %get-tuple-element.121.xs, bf16[2,512,512]{2,1,0:T(8,128)(2,1)S(1)} %get-tuple-element.122.grams, ...), custom_call_target="tpu_custom_call" | custom-call | flops 3221225472 | bytes 6291456 | tf_op jit(solution)/shard_map/pallas_call | solution.py:660
  117.3 4.3 %shard_map.138.cot_u = bf16[512,512]{1,0:T(8,128)(2,1)S(1)} custom-call(f32[512,512]{1,0:T(8,128)S(1)} %get-tuple-element.115.rate.rate_u, f32[512,512]{1,0:T(8,128)S(1)} %get-tuple-element.86.total_ref, bf16[2,512,512]{2,1,0:T(8,128)(2,1)S(1)} %get-tuple-element.116.xs, bf16[2,512,512]{2,1,0:T(8,128)(2,1)S(1)} %get-tuple-element.117.grams, ...), custom_call_target="tpu_custom_call" | custom-call | flops 3221225472 | bytes 6291456 | tf_op jit(solution)/shard_map/pallas_call | solution.py:660
  121.6 3.7 %collective-permute-done.20.received = bf16[4,3,64,512]{3,2,1,0:T(8,128)(2,1)S(1)} collective-permute-done((bf16[4,3,64,512]{3,2,1,0:T(8,128)(2,1)S(1)}, bf16[4,3,64,512]{3,2,1,0:T(8,128)(2,1)S(1)}, u32[]{:S(2)}, u32[]{:S(2)}) %collective-permute-start.20) | collective-permute-done | bytes 786464 | tf_op jit(solution)/shard_map/ppermute | solution.py:214
  126.1 3.8 %collective-permute-start.22 = (bf16[3,64,512]{2,1,0:T(8,128)(2,1)S(1)}, bf16[3,64,512]{2,1,0:T(8,128)(2,1)S(1)}, u32[]{:S(2)}, u32[]{:S(2)}) collective-permute-start(bf16[3,64,512]{2,1,0:T(8,128)(2,1)S(1)} %get-tuple-element.129), channel_id=1, source_target_pairs={{0,16},{4,20},{8,24},{12,28},{16,0},{20,4},{24,8},{28,12},{1,17},{... | collective-permute-start | bytes 589832 | tf_op jit(solution)/shard_map/ppermute | solution.py:210
  130.2 4.3 %shard_map.137.cot_g = bf16[512,512]{1,0:T(8,128)(2,1)S(1)} custom-call(f32[512,512]{1,0:T(8,128)S(1)} %get-tuple-element.110.rate.rate_g, f32[512,512]{1,0:T(8,128)S(1)} %get-tuple-element.83.total_ref, bf16[2,512,512]{2,1,0:T(8,128)(2,1)S(1)} %get-tuple-element.111.xs, bf16[2,512,512]{2,1,0:T(8,128)(2,1)S(1)} %get-tuple-element.112.grams, ...), custom_call_target="tpu_custom_call" | custom-call | flops 3221225472 | bytes 6291456 | tf_op jit(solution)/shard_map/pallas_call | solution.py:660
  135.2 7.9 %collective-permute-done.22.refs_2_ = bf16[3,64,512]{2,1,0:T(8,128)(2,1)S(1)} collective-permute-done((bf16[3,64,512]{2,1,0:T(8,128)(2,1)S(1)}, bf16[3,64,512]{2,1,0:T(8,128)(2,1)S(1)}, u32[]{:S(2)}, u32[]{:S(2)}) %collective-permute-start.22) | collective-permute-done | bytes 196640 | tf_op jit(solution)/shard_map/ppermute | solution.py:210
  143.1 7.3 %shard_map.141 = (bf16[128,512]{1,0:T(8,128)(2,1)}, bf16[128,512]{1,0:T(8,128)(2,1)}, f32[1,64,512]{2,1,0:T(8,128)}, f32[1,64,512]{2,1,0:T(8,128)}, f32[1,64,512]{2,1,0:T(8,128)}) custom-call(s32[1]{0:T(128)} %bitcast.me_ref, bf16[1024,512]{1,0:T(8,128)(2,1)S(1)} %get-tuple-element.105.keys, bf16[1024,512]{1,0:T(8,128)(2,1)S(1)} %get-tuple-element.106.values, ...), custom_call_target="tpu_custom_call" | custom-call | flops 3758096384 | bytes 7340032 | tf_op jit(solution)/shard_map/pallas_call | solution.py:671
  (55 shorter events, 14.8 us)
Async XLA Ops:
  0.6 0.9 copy-start.4
  5.6 13.5 %collective-permute-start.1 = (bf16[448,512]{1,0:T(8,128)(2,1)S(1)}, bf16[448,512]{1,0:T(8,128)(2,1)S(1)}, u32[]{:S(2)}, u32[]{:S(2)}) collective-permute-start(bf16[448,512]{1,0:T(8,128)(2,1)S(1)} %shard_map.127.refs_0_), channel_id=1, source_target_pairs={{0,4},{4,0},{8,12},{12,8},{16,20},{20,16},{24,28},{28,24},{1,5},{5... | collective-permute-start | bytes 1376264 | tf_op jit(solution)/shard_map/ppermute | solution.py:214
  8.6 14.4 %collective-permute-start = (bf16[448,512]{1,0:T(8,128)(2,1)S(1)}, bf16[448,512]{1,0:T(8,128)(2,1)S(1)}, u32[]{:S(2)}, u32[]{:S(2)}) collective-permute-start(bf16[448,512]{1,0:T(8,128)(2,1)S(1)} %shard_map.127.refs_0_), channel_id=1, source_target_pairs={{0,8},{4,12},{8,16},{12,20},{16,24},{20,28},{24,0},{28,4},{1,9},{5... | collective-permute-start | bytes 1376264 | tf_op jit(solution)/shard_map/ppermute | solution.py:210
  19.1 14.8 %collective-permute-start.2 = (bf16[448,512]{1,0:T(8,128)(2,1)S(1)}, bf16[448,512]{1,0:T(8,128)(2,1)S(1)}, u32[]{:S(2)}, u32[]{:S(2)}) collective-permute-start(bf16[448,512]{1,0:T(8,128)(2,1)S(1)} %shard_map.127.refs_0_), channel_id=1, source_target_pairs={{0,24},{4,28},{8,0},{12,4},{16,8},{20,12},{24,16},{28,20},{1,25},{... | collective-permute-start | bytes 1376264 | tf_op jit(solution)/shard_map/ppermute | solution.py:210
  23.0 19.6 %collective-permute-start.3 = (bf16[448,512]{1,0:T(8,128)(2,1)S(1)}, bf16[448,512]{1,0:T(8,128)(2,1)S(1)}, u32[]{:S(2)}, u32[]{:S(2)}) collective-permute-start(bf16[448,512]{1,0:T(8,128)(2,1)S(1)} %collective-permute-done.refs_1_), channel_id=1, source_target_pairs={{0,8},{4,12},{8,16},{12,20},{16,24},{20,28},{24,0},{28,4},{1,9},{5... | collective-permute-start | bytes 1376264 | tf_op jit(solution)/shard_map/ppermute | solution.py:210
  23.0 34.7 %collective-permute-start.4 = (bf16[448,512]{1,0:T(8,128)(2,1)S(1)}, bf16[448,512]{1,0:T(8,128)(2,1)S(1)}, u32[]{:S(2)}, u32[]{:S(2)}) collective-permute-start(bf16[448,512]{1,0:T(8,128)(2,1)S(1)} %collective-permute-done.refs_1_), channel_id=1, source_target_pairs={{0,4},{4,0},{8,12},{12,8},{16,20},{20,16},{24,28},{28,24},{1,5},{5... | collective-permute-start | bytes 1376264 | tf_op jit(solution)/shard_map/ppermute | solution.py:214
  33.9 23.7 %collective-permute-start.5 = (bf16[448,512]{1,0:T(8,128)(2,1)S(1)}, bf16[448,512]{1,0:T(8,128)(2,1)S(1)}, u32[]{:S(2)}, u32[]{:S(2)}) collective-permute-start(bf16[448,512]{1,0:T(8,128)(2,1)S(1)} %collective-permute-done.2.refs_2_), channel_id=1, source_target_pairs={{0,4},{4,0},{8,12},{12,8},{16,20},{20,16},{24,28},{28,24},{1,5},{5... | collective-permute-start | bytes 1376264 | tf_op jit(solution)/shard_map/ppermute | solution.py:214
  42.6 15.0 %collective-permute-start.6 = (bf16[448,512]{1,0:T(8,128)(2,1)S(1)}, bf16[448,512]{1,0:T(8,128)(2,1)}, u32[]{:S(2)}, u32[]{:S(2)}) collective-permute-start(bf16[448,512]{1,0:T(8,128)(2,1)S(1)} %collective-permute-done.3.refs_3_), channel_id=1, source_target_pairs={{0,4},{4,0},{8,12},{12,8},{16,20},{20,16},{24,28},{28,24},{1,5},{5... | collective-permute-start | bytes 1376264 | tf_op jit(solution)/shard_map/ppermute | solution.py:214
  44.1 0.9 copy-start
  45.0 0.9 copy-start.2
  46.3 11.3 %collective-permute-start.10 = (bf16[256,512]{1,0:T(8,128)(2,1)S(1)}, bf16[256,512]{1,0:T(8,128)(2,1)}, u32[]{:S(2)}, u32[]{:S(2)}) collective-permute-start(bf16[256,512]{1,0:T(8,128)(2,1)S(1)} %shard_map.134.refs_0_), channel_id=1, source_target_pairs={{0,8},{4,12},{8,16},{12,20},{16,24},{20,28},{24,0},{28,4},{1,9},{5... | collective-permute-start | bytes 786440 | tf_op jit(solution)/shard_map/ppermute | solution.py:210
  48.0 25.2 %collective-permute-start.11 = (bf16[256,512]{1,0:T(8,128)(2,1)S(1)}, bf16[256,512]{1,0:T(8,128)(2,1)S(1)}, u32[]{:S(2)}, u32[]{:S(2)}) collective-permute-start(bf16[256,512]{1,0:T(8,128)(2,1)S(1)} %shard_map.134.refs_0_), channel_id=1, source_target_pairs={{0,24},{4,28},{8,0},{12,4},{16,8},{20,12},{24,16},{28,20},{1,25},{... | collective-permute-start | bytes 786440 | tf_op jit(solution)/shard_map/ppermute | solution.py:210
  57.6 19.8 %collective-permute-start.12 = (bf16[256,512]{1,0:T(8,128)(2,1)}, bf16[256,512]{1,0:T(8,128)(2,1)S(1)}, u32[]{:S(2)}, u32[]{:S(2)}) collective-permute-start(bf16[256,512]{1,0:T(8,128)(2,1)} %collective-permute-done.10.refs_1_), channel_id=1, source_target_pairs={{0,8},{4,12},{8,16},{12,20},{16,24},{20,28},{24,0},{28,4},{1,9},{5... | collective-permute-start | bytes 786440 | tf_op jit(solution)/shard_map/ppermute | solution.py:210
  57.6 10.5 %copy-start.1 = (bf16[2,128,512]{2,1,0:T(8,128)(2,1)S(1)}, bf16[2,128,512]{2,1,0:T(8,128)(2,1)}, u32[]{:S(2)}) copy-start(bf16[2,128,512]{2,1,0:T(8,128)(2,1)} %refs_0_.3) | copy-start | bytes 786436
  57.6 10.5 %copy-start.3 = (bf16[2,128,512]{2,1,0:T(8,128)(2,1)S(1)}, bf16[2,128,512]{2,1,0:T(8,128)(2,1)}, u32[]{:S(2)}) copy-start(bf16[2,128,512]{2,1,0:T(8,128)(2,1)} %refs_1_.3) | copy-start | bytes 786436
  57.7 10.5 %copy-start.9 = (f32[512]{0:T(512)S(1)}, f32[512]{0:T(512)}, u32[]{:S(2)}) copy-start(f32[512]{0:T(512)} %param.12) | copy-start | bytes 6148
  68.8 4.9 %collective-permute-start.9 = (f32[8,128]{1,0:T(8,128)S(1)}, f32[8,128]{1,0:T(8,128)S(1)}, u32[]{:S(2)}, u32[]{:S(2)}) collective-permute-start(f32[8,128]{1,0:T(8,128)S(1)} %get-tuple-element.81.refs_0_), channel_id=1, source_target_pairs={{0,3},{1,0},{2,1},{3,2},{4,7},{5,4},{6,5},{7,6},{8,11},{9,8},{10,9... | collective-permute-start | bytes 12296 | tf_op jit(solution)/shard_map/ppermute | solution.py:236
  68.9 6.4 %collective-permute-start.8 = (f32[8,128]{1,0:T(8,128)S(1)}, f32[8,128]{1,0:T(8,128)S(1)}, u32[]{:S(2)}, u32[]{:S(2)}) collective-permute-start(f32[8,128]{1,0:T(8,128)S(1)} %get-tuple-element.81.refs_0_), channel_id=1, source_target_pairs={{0,2},{1,3},{2,0},{3,1},{4,6},{5,7},{6,4},{7,5},{8,10},{9,11},{10,... | collective-permute-start | bytes 12296 | tf_op jit(solution)/shard_map/ppermute | solution.py:236
  70.4 5.3 %collective-permute-start.7 = (f32[8,128]{1,0:T(8,128)S(1)}, f32[8,128]{1,0:T(8,128)S(1)}, u32[]{:S(2)}, u32[]{:S(2)}) collective-permute-start(f32[8,128]{1,0:T(8,128)S(1)} %get-tuple-element.81.refs_0_), channel_id=1, source_target_pairs={{0,1},{1,2},{2,3},{3,0},{4,5},{5,6},{6,7},{7,4},{8,9},{9,10},{10,1... | collective-permute-start | bytes 12296 | tf_op jit(solution)/shard_map/ppermute | solution.py:236
  73.2 10.9 %collective-permute-start.14 = (bf16[256,512]{1,0:T(8,128)(2,1)}, bf16[256,512]{1,0:T(8,128)(2,1)S(1)}, u32[]{:S(2)}, u32[]{:S(2)}) collective-permute-start(bf16[256,512]{1,0:T(8,128)(2,1)} %collective-permute-done.10.refs_1_), channel_id=1, source_target_pairs={{0,4},{4,0},{8,12},{12,8},{16,20},{20,16},{24,28},{28,24},{1,5},{5... | collective-permute-start | bytes 786440 | tf_op jit(solution)/shard_map/ppermute | solution.py:214
  73.8 14.4 %collective-permute-start.13 = (bf16[256,512]{1,0:T(8,128)(2,1)S(1)}, bf16[256,512]{1,0:T(8,128)(2,1)S(1)}, u32[]{:S(2)}, u32[]{:S(2)}) collective-permute-start(bf16[256,512]{1,0:T(8,128)(2,1)S(1)} %shard_map.134.refs_0_), channel_id=1, source_target_pairs={{0,4},{4,0},{8,12},{12,8},{16,20},{20,16},{24,28},{28,24},{1,5},{5... | collective-permute-start | bytes 786440 | tf_op jit(solution)/shard_map/ppermute | solution.py:214
  75.3 18.5 %collective-permute-start.15 = (bf16[256,512]{1,0:T(8,128)(2,1)S(1)}, bf16[256,512]{1,0:T(8,128)(2,1)S(1)}, u32[]{:S(2)}, u32[]{:S(2)}) collective-permute-start(bf16[256,512]{1,0:T(8,128)(2,1)S(1)} %collective-permute-done.11.refs_2_), channel_id=1, source_target_pairs={{0,4},{4,0},{8,12},{12,8},{16,20},{20,16},{24,28},{28,24},{1,5},{5... | collective-permute-start | bytes 786440 | tf_op jit(solution)/shard_map/ppermute | solution.py:214
  77.4 21.5 %collective-permute-start.16 = (bf16[256,512]{1,0:T(8,128)(2,1)S(1)}, bf16[256,512]{1,0:T(8,128)(2,1)S(1)}, u32[]{:S(2)}, u32[]{:S(2)}) collective-permute-start(bf16[256,512]{1,0:T(8,128)(2,1)S(1)} %collective-permute-done.12.refs_3_), channel_id=1, source_target_pairs={{0,4},{4,0},{8,12},{12,8},{16,20},{20,16},{24,28},{28,24},{1,5},{5... | collective-permute-start | bytes 786440 | tf_op jit(solution)/shard_map/ppermute | solution.py:214
  81.5 2.6 %copy-start.10 = (bf16[2,512,512]{2,1,0:T(8,128)(2,1)}, bf16[2,512,512]{2,1,0:T(8,128)(2,1)S(1)}, u32[]{:S(2)}) copy-start(bf16[2,512,512]{2,1,0:T(8,128)(2,1)S(1)} %get-tuple-element.123.blends) | copy-start | bytes 3145732
  103.8 2.1 %collective-permute-start.19 = (f32[8,1024]{1,0:T(8,128)S(1)}, f32[8,1024]{1,0:T(8,128)S(1)}, u32[]{:S(2)}, u32[]{:S(2)}) collective-permute-start(f32[8,1024]{1,0:T(8,128)S(1)} %get-tuple-element.103.refs_0_), channel_id=1, source_target_pairs={{0,3},{1,0},{2,1},{3,2},{4,7},{5,4},{6,5},{7,6},{8,11},{9,8},{10,9... | collective-permute-start | bytes 98312 | tf_op jit(solution)/shard_map/ppermute | solution.py:236
  104.3 4.0 %collective-permute-start.18 = (f32[8,1024]{1,0:T(8,128)S(1)}, f32[8,1024]{1,0:T(8,128)S(1)}, u32[]{:S(2)}, u32[]{:S(2)}) collective-permute-start(f32[8,1024]{1,0:T(8,128)S(1)} %get-tuple-element.103.refs_0_), channel_id=1, source_target_pairs={{0,2},{1,3},{2,0},{3,1},{4,6},{5,7},{6,4},{7,5},{8,10},{9,11},{10,... | collective-permute-start | bytes 98312 | tf_op jit(solution)/shard_map/ppermute | solution.py:236
  105.1 3.4 %collective-permute-start.17 = (f32[8,1024]{1,0:T(8,128)S(1)}, f32[8,1024]{1,0:T(8,128)S(1)}, u32[]{:S(2)}, u32[]{:S(2)}) collective-permute-start(f32[8,1024]{1,0:T(8,128)S(1)} %get-tuple-element.103.refs_0_), channel_id=1, source_target_pairs={{0,1},{1,2},{2,3},{3,0},{4,5},{5,6},{6,7},{7,4},{8,9},{9,10},{10,1... | collective-permute-start | bytes 98312 | tf_op jit(solution)/shard_map/ppermute | solution.py:236
  105.2 20.1 %collective-permute-start.20 = (bf16[4,3,64,512]{3,2,1,0:T(8,128)(2,1)S(1)}, bf16[4,3,64,512]{3,2,1,0:T(8,128)(2,1)S(1)}, u32[]{:S(2)}, u32[]{:S(2)}) collective-permute-start(bf16[4,3,64,512]{3,2,1,0:T(8,128)(2,1)S(1)} %get-tuple-element.126), channel_id=1, source_target_pairs={{0,4},{4,0},{8,12},{12,8},{16,20},{20,16},{24,28},{28,24},{1,5},{5... | collective-permute-start | bytes 2359304 | tf_op jit(solution)/shard_map/ppermute | solution.py:214
  108.6 4.4 %copy-start.11 = (bf16[2,512,512]{2,1,0:T(8,128)(2,1)S(1)}, bf16[2,512,512]{2,1,0:T(8,128)(2,1)}, u32[]{:S(2)}) copy-start(bf16[2,512,512]{2,1,0:T(8,128)(2,1)} %copy-done.10) | copy-start | bytes 3145732
  125.4 9.7 %collective-permute-start.21 = (bf16[3,64,512]{2,1,0:T(8,128)(2,1)S(1)}, bf16[3,64,512]{2,1,0:T(8,128)(2,1)S(1)}, u32[]{:S(2)}, u32[]{:S(2)}) collective-permute-start(bf16[3,64,512]{2,1,0:T(8,128)(2,1)S(1)} %get-tuple-element.128), channel_id=1, source_target_pairs={{0,8},{4,12},{8,16},{12,20},{16,24},{20,28},{24,0},{28,4},{1,9},{5... | collective-permute-start | bytes 589832 | tf_op jit(solution)/shard_map/ppermute | solution.py:210
  126.1 17.0 %collective-permute-start.22 = (bf16[3,64,512]{2,1,0:T(8,128)(2,1)S(1)}, bf16[3,64,512]{2,1,0:T(8,128)(2,1)S(1)}, u32[]{:S(2)}, u32[]{:S(2)}) collective-permute-start(bf16[3,64,512]{2,1,0:T(8,128)(2,1)S(1)} %get-tuple-element.129), channel_id=1, source_target_pairs={{0,16},{4,20},{8,24},{12,28},{16,0},{20,4},{24,8},{28,12},{1,17},{... | collective-permute-start | bytes 589832 | tf_op jit(solution)/shard_map/ppermute | solution.py:210
  129.9 13.2 %collective-permute-start.23 = (bf16[3,64,512]{2,1,0:T(8,128)(2,1)S(1)}, bf16[3,64,512]{2,1,0:T(8,128)(2,1)S(1)}, u32[]{:S(2)}, u32[]{:S(2)}) collective-permute-start(bf16[3,64,512]{2,1,0:T(8,128)(2,1)S(1)} %get-tuple-element.130), channel_id=1, source_target_pairs={{0,24},{4,28},{8,0},{12,4},{16,8},{20,12},{24,16},{28,20},{1,25},{... | collective-permute-start | bytes 589832 | tf_op jit(solution)/shard_map/ppermute | solution.py:210
  (4 other events, 3.4 us)

commit v3 on v2

--- a/solution.py
+++ b/solution.py
@@ -218,18 +218,6 @@
     return lax.optimization_barrier((array, *earlier))[0]
 
 
-def along_ring(own, ring, earlier):
-    found = [(0, own)]
-    up, down = own, tie(own, earlier)
-    for step in range(1, ring // 2 + 1):
-        up = shift(up, ring, 1)
-        found.append((-step, up))
-        if 2 * step < ring:
-            down = shift(down, ring, -1)
-            found.append((step, down))
-    return found
-
-
 def head_terms(stats):
     heads = lax.axis_size("head")
     return [stats] + [
@@ -238,21 +226,17 @@
     ]
 
 
-def unpack(layout, segments, ring, me, refs, targets, sems):
-    copies = []
-    for slot, ((outer, flip), ref) in enumerate(zip(layout, refs)):
-        owner = ((me // 2 + outer + ring) % ring) * 2 + (me % 2 + flip) % 2
-        begin = 0
-        for (count, by_slot), target in zip(segments, targets):
-            place = slot * count if by_slot else pl.multiple_of(owner * count, 16)
-            copies.append(
-                pltpu.make_async_copy(
-                    ref.at[pl.ds(begin, count)],
-                    target.at[pl.ds(place, count)],
-                    sems.at[len(copies)],
-                )
-            )
-            begin += count
+def owner_of(ring, me, outer, flip):
+    return ((me // 2 + outer + ring) % ring) * 2 + (me % 2 + flip) % 2
+
+
+def move(rows, sems):
+    copies = [
+        pltpu.make_async_copy(
+            source.at[pl.ds(begin, count)], target.at[pl.ds(place, count)], sems.at[index]
+        )
+        for index, (source, begin, target, place, count) in enumerate(rows)
+    ]
     for copy in copies:
         copy.start()
     for copy in copies:
@@ -264,28 +248,49 @@
     return [slice(i, i + step) for i in range(0, tokens, step)]
 
 
-def pack_kernel(lead, *refs):
-    sources, target, sems = refs[:-2], refs[-2], refs[-1]
-    copies, begin = [], 0
-    for place, source in enumerate(sources):
-        source = source.at[lead[place]] if lead[place] is not None else source
-        rows = source.shape[0]
-        copies.append(
-            pltpu.make_async_copy(source, target.at[pl.ds(begin, rows)], sems.at[place])
-        )
-        begin += rows
-    for copy in copies:
-        copy.start()
-    for copy in copies:
-        copy.wait()
-
-
-def fast_kernel(layout, segments, ring, me_ref, *refs):
-    count = len(layout)
-    pieces, refs = refs[:count], refs[count:]
+def pack_kernel(gate, up, down, keys, values, queries, upstream, first, second, sems):
+    rows = []
+    for target, sources in (
+        (first, (gate.at[0], up.at[0], down.at[0], keys, values)),
+        (second, (queries.at[1], upstream.at[1])),
+    ):
+        begin = 0
+        for source in sources:
+            rows.append((source, 0, target, begin, source.shape[0]))
+            begin += source.shape[0]
+    move(rows, sems)
+
+
+def place_rows(layout, ring, me, pieces, targets):
+    rows = []
+    for (outer, flip, slot), piece in zip(layout, pieces):
+        owner = owner_of(ring, me, outer, flip)
+        begin = 0
+        for index, target in enumerate(targets):
+            count = target.shape[0] // (2 * ring)
+            place = pl.multiple_of(owner * count, 16) if index < 3 else slot * count
+            rows.append((piece, begin, target, place, count))
+            begin += count
+    return rows
+
+
+def place_kernel(layout, ring, carried, me_ref, *refs):
+    sems = refs[-1]
+    refs = refs[:-1]
+    targets = refs[-6:-1] if carried else refs[-5:]
+    rows = place_rows(layout, ring, me_ref[0], refs, targets)
+    begin = 0
+    for source in refs[len(layout):len(layout) + carried]:
+        rows.append((source, 0, refs[-1], begin, source.shape[0]))
+        begin += source.shape[0]
+    move(rows, sems)
+
+
+def fast_kernel(layout, ring, me_ref, *refs):
+    pieces, refs = refs[:len(layout)], refs[len(layout) + 5:]
     (wg, wu, wd, keys, values, gk_ref, uk_ref, back_ref, totals_g, totals_u, totals_d) = refs[:11]
     d_gate, d_up, hidden, sems = refs[11:]
-    unpack(layout, segments, ring, me_ref[0], pieces, (wg, wu, wd, keys, values), sems)
+    move(place_rows(layout, ring, me_ref[0], pieces, (wg, wu, wd, keys, values)), sems)
     for part in chunks_of(keys.shape[0]):
         gk = product(keys[part], wg[...])
         uk = product(keys[part], wu[...])
@@ -402,11 +407,18 @@
         target[...] = (kept[place].astype(f32) + received[place].astype(f32)).astype(bf16)
 
 
-def second_forward_kernel(layout, segments, ring, me_ref, gain, wg, wu, wd, *refs):
-    count = len(layout)
+def second_forward_kernel(gain, wg, wu, wd, *refs):
+    count = len(refs) - 8
     pieces, refs = refs[:count], refs[count:]
     queries, upstream, gq, uq, hidden, out, stats, sems = refs
-    unpack(layout, segments, ring, me_ref[0], pieces, (queries, upstream), sems)
+    tokens = queries.shape[0] // (2 * count)
+    rows = []
+    for slot, piece in enumerate(pieces):
+        for half in range(2):
+            place = (2 * slot + half) * tokens
+            rows.append((piece, 2 * half * tokens, queries, place, tokens))
+            rows.append((piece, (2 * half + 1) * tokens, upstream, place, tokens))
+    move(rows, sems)
     forward_part(queries, upstream, gain, wg, wu, wd, gq, uq, hidden, out, stats)
 
 
@@ -500,13 +512,16 @@
     return pl.BlockSpec(memory_space=pltpu.SMEM)
 
 
+def hbm():
+    return pl.BlockSpec(memory_space=pltpu.HBM)
+
+
 def anywhere():
     return pl.BlockSpec(memory_space=pl.ANY)
 
 
-def cost(rows, depth, columns, products):
-    flops = 2 * rows * depth * columns * products
-    return pl.CostEstimate(flops=flops, bytes_accessed=flops // 512, transcendentals=0)
+def light():
+    return pl.CostEstimate(flops=1, bytes_accessed=1, transcendentals=0)
 
 
 def params(mib):
@@ -530,41 +545,67 @@
     matrix = (depth, hidden)
     wide, narrow = S(matrix, f32), S(matrix, bf16)
 
-    def pack(arrays, lead):
-        rows = sum(array.shape[-2] for array in arrays)
-        return pl.pallas_call(
-            functools.partial(pack_kernel, lead),
-            out_shape=S((rows, depth), bf16),
-            in_specs=[anywhere()] * len(arrays),
-            out_specs=anywhere(),
-            scratch_shapes=[pltpu.SemaphoreType.DMA((len(arrays),))],
+    packed, packed_second = pl.pallas_call(
+        pack_kernel,
+        out_shape=(
+            S((2 * rows + down_weight.shape[1] + 2 * own, depth), bf16), S((2 * own, depth), bf16),
+        ),
+        in_specs=[hbm()] * 7,
+        out_specs=[vmem()] * 2,
+        scratch_shapes=[pltpu.SemaphoreType.DMA((7,))],
+        compiler_params=params(60),
+    )(gate_weight, up_weight, down_weight, keys, values, queries, upstream)
+    buffers = (narrow, narrow, narrow, S((tokens, depth), bf16), S((tokens, depth), bf16))
+
+    def place(pieces, layout, state=(), carry=(), others=()):
+        out_shape = buffers
+        if carry:
+            out_shape += (S((sum(array.shape[0] for array in carry), depth), bf16),)
+        start = 1 + len(pieces) + len(carry) + len(others)
+        out = pl.pallas_call(
+            functools.partial(place_kernel, layout, ring, len(carry)),
+            out_shape=out_shape,
+            in_specs=[smem()] + [anywhere()] * (start - 1 + len(state)),
+            out_specs=[anywhere()] * len(out_shape),
+            scratch_shapes=[pltpu.SemaphoreType.DMA((5 * len(pieces) + len(carry),))],
+            input_output_aliases={start + index: index for index in range(len(state))},
+            cost_estimate=light(),
             compiler_params=params(4),
-        )(*arrays)
-
-    packed = pack((gate_weight, up_weight, down_weight, keys, values), (0, 0, 0, None, None))
-    packed_second = pack((queries, upstream), (1, 1))
-    swapped = [swap(packed, ring)]
-    outers = along_ring(packed, ring, swapped[0])
-    swapped += [swap(array, ring) for _, array in outers[1:]]
-    last = outers[-1][1]
-    near = swapped[max(ring - 2, 0)]
-    layout = [(outer, 0) for outer, _ in outers] + [(outer, 1) for outer, _ in outers]
-    pieces = [array for _, array in outers] + swapped
-    segments = ((rows, False), (rows, False), (down_weight.shape[1], False), (own, True), (own, True))
+        )(me_ref, *pieces, *carry, *others, *state)
+        return (out[:5], out[5]) if carry else (out, None)
+
+    crossed = swap(packed, ring)
+    crossed_second = swap(packed_second, ring)
+    up = shift(packed, ring, 1)
+    state, carried = place((packed, crossed), ((0, 0, 0), (0, 1, 1)), carry=(packed,))
+    down = shift(carried, ring, -1)
+    crossed_up = swap(up, ring)
+    crossed_down = swap(down, ring)
+    state, carried = place((up,), ((-1, 0, 2),), state, (up,), (crossed_second,))
+    far = shift(carried, ring, 1)
+    crossed_far = swap(far, ring)
+    state, pair = place(
+        (down, crossed_up), ((1, 0, 3), (-1, 1, 4)), state, (packed_second, crossed_second)
+    )
+    state, _ = place((far, crossed_down), ((-2, 0, 5), (1, 1, 6)), state)
+    layout = ((-2, 1, 7),)
     (wg, wu, wd, all_keys, all_values, gk, uk, back, *totals) = pl.pallas_call(
-        functools.partial(fast_kernel, layout, segments, ring),
+        functools.partial(fast_kernel, layout, ring),
         out_shape=(
             narrow, narrow, narrow, S((tokens, depth), bf16), S((tokens, depth), bf16),
             S((tokens, hidden), f32), S((tokens, hidden), f32), S((tokens, hidden), f32),
             wide, wide, wide,
         ),
-        in_specs=[smem()] + [anywhere()] * len(pieces),
+        in_specs=[smem(), anywhere()] + [anywhere()] * 5,
         out_specs=[vmem()] * 11,
-        scratch_shapes=[pltpu.VMEM((tokens, hidden), bf16)] * 3
-        + [pltpu.SemaphoreType.DMA((5 * len(pieces),))],
-        cost_estimate=cost(tokens, depth, hidden, 6),
+        scratch_shapes=[pltpu.VMEM((tokens, hidden), bf16)] * 3 + [pltpu.SemaphoreType.DMA((5,))],
+        input_output_aliases={2 + index: index for index in range(5)},
+        cost_estimate=light(),
         compiler_params=params(24),
-    )(me_ref, *pieces)
+    )(me_ref, crossed_far, *state)
+
+    up, down = shift(pair, ring, 1), shift(pair, ring, -1)
+    pairs = [pair, up, down, shift(tie(up, totals[0]), ring, 1)]
 
     queries0, upstream0, gq0, uq0, hidden0, out0, stats0 = pl.pallas_call(
         first_forward_kernel,
@@ -575,7 +616,7 @@
         ),
         in_specs=[vmem()] * 6,
         out_specs=[vmem()] * 7,
-        cost_estimate=cost(own, depth, hidden, 3),
+        cost_estimate=light(),
         compiler_params=params(16),
     )(queries, upstream, gain, wg, wu, wd)
 
@@ -588,11 +629,13 @@
             ),
             in_specs=[vmem()] * 2,
             out_specs=[vmem()] * 5,
-            cost_estimate=cost(depth, depth, hidden, 3 * NS_STEPS),
+            cost_estimate=light(),
             compiler_params=params(16),
         )(total, (wg, wu, wd)[which])
 
     terms0 = head_terms(stats0)
+    first_weight = schulz(0, totals[0])
+    terms0[0] = tie(terms0[0], first_weight[4])
     grad_first, kept, sent = pl.pallas_call(
         functools.partial(first_backward_kernel, width, ring),
         out_shape=(
@@ -602,37 +645,26 @@
         out_specs=[vmem()] * 3,
         scratch_shapes=[pltpu.VMEM((own, hidden), bf16)] * 2
         + [pltpu.VMEM((own, depth), bf16), pltpu.VMEM(matrix, bf16)],
-        cost_estimate=cost(own, depth, hidden, 6),
+        cost_estimate=light(),
         compiler_params=params(20),
     )(me_ref, queries0, upstream0, gain, wg, wu, wd, gq0, uq0, hidden0, out0, *terms0)
 
-    forward = [
-        schulz(0, totals[0]), schulz(1, tie(totals[1], *terms0)), schulz(2, tie(totals[2], sent))
-    ]
-
-    outers = along_ring(tie(packed_second, last), ring, last)
-    after = (near, None, totals[0], forward[0][3])
-    swapped = []
-    for place, (_, array) in enumerate(outers):
-        earlier = after[min(place, 3)]
-        swapped.append(swap(array if earlier is None else tie(array, earlier), ring))
-    near = swapped[max(ring - 2, 0)]
-    pieces = [array for _, array in outers] + swapped
-    segments = ((own, True), (own, True))
+    forward = [first_weight, schulz(1, totals[1]), schulz(2, tie(totals[2], down))]
+
     seconds = [forward[which][3] for which in range(3)]
     all_queries, all_upstream, gq, uq, hidden_q, out, stats = pl.pallas_call(
-        functools.partial(second_forward_kernel, layout, segments, ring),
+        second_forward_kernel,
         out_shape=(
             S((tokens, depth), bf16), S((tokens, depth), bf16),
             S((tokens, hidden), f32), S((tokens, hidden), f32), S((tokens, hidden), bf16),
             S((tokens, depth), f32), S((8, tokens), f32),
         ),
-        in_specs=[smem()] + [vmem()] * 4 + [anywhere()] * len(pieces),
+        in_specs=[vmem()] * 4 + [anywhere()] * len(pairs),
         out_specs=[vmem()] * 7,
-        scratch_shapes=[pltpu.SemaphoreType.DMA((2 * len(pieces),))],
-        cost_estimate=cost(tokens, depth, hidden, 3),
+        scratch_shapes=[pltpu.SemaphoreType.DMA((4 * len(pairs),))],
+        cost_estimate=light(),
         compiler_params=params(24),
-    )(me_ref, gain, *seconds, *pieces)
+    )(gain, *seconds, *pairs)
     terms = head_terms(stats)
 
     block = S((3, rows, hidden), bf16)
@@ -642,7 +674,7 @@
         in_specs=[smem()] + [vmem()] * 2,
         out_specs=[vmem()] * ring,
         compiler_params=params(12),
-    )(me_ref, kept, swap(tie(sent, near), ring))
+    )(me_ref, tie(kept, terms[1]), swap(tie(sent, down), ring))
     firsts = [summed[0]] + [shift(summed[step], ring, step) for step in range(1, ring)]
 
     grad_queries, *rates = pl.pallas_call(
@@ -652,7 +684,7 @@
         out_specs=[vmem()] * 4,
         scratch_shapes=[pltpu.VMEM((tokens, hidden), bf16)] * 2
         + [pltpu.VMEM((tokens, depth), bf16)],
-        cost_estimate=cost(tokens, depth, hidden, 4),
+        cost_estimate=light(),
         compiler_params=params(20),
     )(grad_first, all_queries, all_upstream, gain, *seconds, gq, uq, hidden_q, out, *terms)
 
@@ -662,7 +694,7 @@
             out_shape=narrow,
             in_specs=[vmem()] * 6,
             out_specs=vmem(),
-            cost_estimate=cost(depth, depth, hidden, 6 * NS_STEPS),
+            cost_estimate=light(),
             compiler_params=params(16),
         )(rates[which], totals[which], *forward[which][:3], forward[which][4])
         for which in range(3)
@@ -685,7 +717,7 @@
             pltpu.VMEM((own, hidden), bf16),
             pltpu.VMEM(matrix, f32),
         ],
-        cost_estimate=cost(tokens, depth, hidden, 7),
+        cost_estimate=light(),
         compiler_params=params(24),
     )(
         me_ref, all_keys, all_values, wg, wu, wd, gk, uk, back, *cots, *rates, *firsts,
@@ -695,7 +727,7 @@
 def per_device(queries, keys, values, upstream, out_gain, gate_weight, up_weight, down_weight):
     shards = lax.axis_size("tok")
     tokens = keys.shape[0] * shards
-    few = 4 * tokens <= 12 * gate_weight.shape[2] and shards % 2 == 0
+    few = 4 * tokens <= 12 * gate_weight.shape[2] and shards == 8
     plan = gather_tokens if few else split_tokens
     return plan(queries, keys, values, upstream, out_gain, gate_weight, up_weight, down_weight)
 

time: 153 us -> 130 us (0.85); the launches traced: 150 us -> 130 us
  waiting for transfers between devices: 63 us -> 44.1 us
  local copies, waits for them, and re-layouts: 6.24 us -> 2.27 us
    ppermute x9 -> x6, waiting for transfers between devices: 27.5 us -> 16.3 us  [swap(): return lax.ppermute(array, 'tok', [(i, i ^ 1) for i in range(2 * ring)])]
    ppermute x9, waiting for transfers between devices: 32.7 us -> 22 us  [shift(): return lax.ppermute(array, 'tok', pairs)]
    unnamed x24 -> x14, local copies, waits for them, and re-layouts: 6.24 us -> 2.27 us
    ppermute x6, waiting for transfers between devices: 2.86 us -> 5.84 us  [head_terms(): lax.ppermute(stats, 'head', [(i, (i + k) % heads) for i in range(heads)])]
    ppermute x9, starting transfers between devices: 14.1 us -> 16.9 us  [shift(): return lax.ppermute(array, 'tok', pairs)]
    ppermute x9 -> x6, starting transfers between devices: 12.2 us -> 9.58 us  [swap(): return lax.ppermute(array, 'tok', [(i, i ^ 1) for i in range(2 * ring)])]
    pallas_call x4 -> x7, Pallas kernels: 16.3 us -> 17.4 us  [the longest x1 5.18 us: gather_tokens(): pl.pallas_call(second_forward_kernel, out_shape=(S((tokens, depth), bf16)...]
  transfers between devices with their start and end apart: 24 -> 21, of which waited for: 13 -> 8; matrix products, arithmetic and copies ran while one was open for 0% -> 0% of each run, Pallas kernels for 25% -> 33%
where the time goes in v3:
time: 130 us
  Pallas kernels  52.3 us (40%)
  waiting for transfers between devices  44.1 us (34%)
  starting transfers between devices  30 us (23%)
  local copies, waits for them, and re-layouts  2.27 us (2%)
    ppermute x9, waiting for transfers between devices, shift(): return lax.ppermute(array, 'tok', pairs)  22 us
    ppermute x9, starting transfers between devices, shift(): return lax.ppermute(array, 'tok', pairs)  16.9 us
    ppermute x6, waiting for transfers between devices, swap(): return lax.ppermute(array, 'tok', [(i, i ^ 1) for i in range(2 * ring)])  16.3 us
    pallas_call x3, Pallas kernels, gather_tokens(): pl.pallas_call(schulz_back_kernel, out_shape=narrow, in_specs=[vmem()] *...  13.1 us
    ppermute x6, starting transfers between devices, swap(): return lax.ppermute(array, 'tok', [(i, i ^ 1) for i in range(2 * ring)])  9.58 us
    pallas_call x3, Pallas kernels, schulz(): pl.pallas_call(schulz_kernel, out_shape=(S((NS_STEPS, *matrix), bf16), S(...  7.6 us
    pallas_call x1, Pallas kernels, gather_tokens(): pl.pallas_call(functools.partial(last_kernel, own, scale), out_shape=(S((...  7.33 us
    ppermute x6, waiting for transfers between devices, head_terms(): lax.ppermute(stats, 'head', [(i, (i + k) % heads) for i in range(heads)])  5.84 us
  transfers between devices with their start and end apart: 21, of which 8 were waited for; matrix products, arithmetic and copies ran while one was open for 0% of the time, Pallas kernels for 33%

profile of v3, /device:TPU:0, one launch (start us, length us, event | category | flops | bytes accessed | tf_op | source)
XLA Modules:
  0.0 129.6 jit_solution(6036337798185020002)
XLA Ops:
  0.6 2.1 %shard_map.127 = (bf16[448,512]{1,0:T(8,128)(2,1)}, bf16[256,512]{1,0:T(8,128)(2,1)}) custom-call(bf16[1,64,512]{2,1,0:T(8,128)(2,1)} %gate.1, bf16[1,64,512]{2,1,0:T(8,128)(2,1)} %up.1, bf16[1,64,512]{2,1,0:T(8,128)(2,1)} %down.1, bf16[128,512]{1,0:T(8,128)(2,1)} %keys.1, bf16[128,512]{1,0:T(8,128)(2,1)} %values.1, bf16[2,128,512]{2,1,0:T(8,128)(2,1)} %queries_ref.1, ...), custom_call_target="tpu_custom_call" | custom-call | tf_op jit(solution)/shard_map/pallas_call | solution.py:548
  2.8 3.0 %collective-permute-start.2 = (bf16[448,512]{1,0:T(8,128)(2,1)}, bf16[448,512]{1,0:T(8,128)(2,1)S(1)}, u32[]{:S(2)}, u32[]{:S(2)}) collective-permute-start(bf16[448,512]{1,0:T(8,128)(2,1)} %get-tuple-element.92.refs_0_.refs_2_), channel_id=1, source_target_pairs={{0,4},{4,0},{8,12},{12,8},{16,20},{20,16},{24,28},{28,24},{1,5},{5... | collective-permute-start | bytes 1376264 | tf_op jit(solution)/shard_map/ppermute | solution.py:214
  5.8 1.6 %collective-permute-start = (bf16[448,512]{1,0:T(8,128)(2,1)}, bf16[448,512]{1,0:T(8,128)(2,1)S(1)}, u32[]{:S(2)}, u32[]{:S(2)}) collective-permute-start(bf16[448,512]{1,0:T(8,128)(2,1)} %get-tuple-element.92.refs_0_.refs_2_), channel_id=1, source_target_pairs={{0,8},{4,12},{8,16},{12,20},{16,24},{20,28},{24,0},{28,4},{1,9},{5... | collective-permute-start | bytes 1376264 | tf_op jit(solution)/shard_map/ppermute | solution.py:210
  7.9 9.4 %collective-permute-done.2.refs_1_ = bf16[448,512]{1,0:T(8,128)(2,1)S(1)} collective-permute-done((bf16[448,512]{1,0:T(8,128)(2,1)}, bf16[448,512]{1,0:T(8,128)(2,1)S(1)}, u32[]{:S(2)}, u32[]{:S(2)}) %collective-permute-start.2) | collective-permute-done | bytes 458784 | tf_op jit(solution)/shard_map/ppermute | solution.py:214
  18.3 1.5 %shard_map.128 = (bf16[512,512]{1,0:T(8,128)(2,1)S(1)}, bf16[512,512]{1,0:T(8,128)(2,1)S(1)}, bf16[512,512]{1,0:T(8,128)(2,1)S(1)}, bf16[1024,512]{1,0:T(8,128)(...) custom-call(s32[1]{0:T(128)} %bitcast.me_ref, bf16[448,512]{1,0:T(8,128)(2,1)S(1)} %copy-done, ...), custom_call_target="tpu_custom_call" | custom-call | flops 1 | bytes 1 | tf_op jit(solution)/shard_map/pallas_call | solution.py:565
  19.9 4.2 %collective-permute-start.5 = (bf16[448,512]{1,0:T(8,128)(2,1)S(1)}, bf16[448,512]{1,0:T(8,128)(2,1)S(1)}, u32[]{:S(2)}, u32[]{:S(2)}) collective-permute-start(bf16[448,512]{1,0:T(8,128)(2,1)S(1)} %get-tuple-element.100), channel_id=1, source_target_pairs={{0,24},{4,28},{8,0},{12,4},{16,8},{20,12},{24,16},{28,20},{1,25},{... | collective-permute-start | bytes 1376264 | tf_op jit(solution)/shard_map/ppermute | solution.py:210
  24.1 1.5 %collective-permute-start.7 = (bf16[448,512]{1,0:T(8,128)(2,1)S(1)}, bf16[448,512]{1,0:T(8,128)(2,1)S(1)}, u32[]{:S(2)}, u32[]{:S(2)}) collective-permute-start(bf16[448,512]{1,0:T(8,128)(2,1)S(1)} %collective-permute-done.refs_0_.refs_1_), channel_id=1, source_target_pairs={{0,4},{4,0},{8,12},{12,8},{16,20},{20,16},{24,28},{28,24},{1,5},{5... | collective-permute-start | bytes 1376264 | tf_op jit(solution)/shard_map/ppermute | solution.py:214
  26.6 8.5 %collective-permute-done.5.refs_0_ = bf16[448,512]{1,0:T(8,128)(2,1)S(1)} collective-permute-done((bf16[448,512]{1,0:T(8,128)(2,1)S(1)}, bf16[448,512]{1,0:T(8,128)(2,1)S(1)}, u32[]{:S(2)}, u32[]{:S(2)}) %collective-permute-start.5) | collective-permute-done | bytes 458784 | tf_op jit(solution)/shard_map/ppermute | solution.py:210
  36.5 4.3 %collective-permute-start.11 = (bf16[512,512]{1,0:T(8,128)(2,1)S(1)}, bf16[512,512]{1,0:T(8,128)(2,1)S(1)}, u32[]{:S(2)}, u32[]{:S(2)}) collective-permute-start(bf16[512,512]{1,0:T(8,128)(2,1)S(1)} %get-tuple-element.134.refs_0_), channel_id=1, source_target_pairs={{0,24},{4,28},{8,0},{12,4},{16,8},{20,12},{24,16},{28,20},{1,25},{... | collective-permute-start | bytes 1572872 | tf_op jit(solution)/shard_map/ppermute | solution.py:210
  40.8 1.5 %collective-permute-start.6 = (bf16[448,512]{1,0:T(8,128)(2,1)S(1)}, bf16[448,512]{1,0:T(8,128)(2,1)S(1)}, u32[]{:S(2)}, u32[]{:S(2)}) collective-permute-start(bf16[448,512]{1,0:T(8,128)(2,1)S(1)} %collective-permute-done.5.refs_0_), channel_id=1, source_target_pairs={{0,4},{4,0},{8,12},{12,8},{16,20},{20,16},{24,28},{28,24},{1,5},{5... | collective-permute-start | bytes 1376264 | tf_op jit(solution)/shard_map/ppermute | solution.py:214
  42.3 3.6 %collective-permute-done.3.refs_0_ = bf16[448,512]{1,0:T(8,128)(2,1)S(1)} collective-permute-done((bf16[448,512]{1,0:T(8,128)(2,1)S(1)}, bf16[448,512]{1,0:T(8,128)(2,1)S(1)}, u32[]{:S(2)}, u32[]{:S(2)}) %collective-permute-start.3) | collective-permute-done | bytes 458784 | tf_op jit(solution)/shard_map/ppermute | solution.py:210
  47.4 1.6 %collective-permute-start.12 = (bf16[512,512]{1,0:T(8,128)(2,1)S(1)}, bf16[512,512]{1,0:T(8,128)(2,1)S(1)}, u32[]{:S(2)}, u32[]{:S(2)}) collective-permute-start(bf16[512,512]{1,0:T(8,128)(2,1)S(1)} %get-tuple-element.134.refs_0_), channel_id=1, source_target_pairs={{0,8},{4,12},{8,16},{12,20},{16,24},{20,28},{24,0},{28,4},{1,9},{5... | collective-permute-start | bytes 1572872 | tf_op jit(solution)/shard_map/ppermute | solution.py:210
  48.9 3.2 %collective-permute-done.6.refs_1_ = bf16[448,512]{1,0:T(8,128)(2,1)S(1)} collective-permute-done((bf16[448,512]{1,0:T(8,128)(2,1)S(1)}, bf16[448,512]{1,0:T(8,128)(2,1)S(1)}, u32[]{:S(2)}, u32[]{:S(2)}) %collective-permute-start.6) | collective-permute-done | bytes 458784 | tf_op jit(solution)/shard_map/ppermute | solution.py:214
  53.4 3.6 %collective-permute-done.4.refs_0_ = bf16[448,512]{1,0:T(8,128)(2,1)S(1)} collective-permute-done((bf16[448,512]{1,0:T(8,128)(2,1)S(1)}, bf16[448,512]{1,0:T(8,128)(2,1)S(1)}, u32[]{:S(2)}, u32[]{:S(2)}) %collective-permute-start.4) | collective-permute-done | bytes 458784 | tf_op jit(solution)/shard_map/ppermute | solution.py:214
  57.0 5.1 %shard_map.132 = (bf16[512,512]{1,0:T(8,128)(2,1)S(1)}, bf16[512,512]{1,0:T(8,128)(2,1)S(1)}, bf16[512,512]{1,0:T(8,128)(2,1)S(1)}, bf16[1024,512]{1,0:T(8,128)(...) custom-call(s32[1]{0:T(128)} %bitcast.me_ref, ...), custom_call_target="tpu_custom_call", output_to_operand_aliasing={{0}: (2, {}), {1}: (3, {}), {2}: (4, {}), {3}: (5, {}), {4}... | custom-call | flops 1 | bytes 1 | tf_op jit(solution)/shard_map/pallas_call | solution.py:592
  63.3 1.5 %collective-permute-start.9 = (f32[8,128]{1,0:T(8,128)S(1)}, f32[8,128]{1,0:T(8,128)S(1)}, u32[]{:S(2)}, u32[]{:S(2)}) collective-permute-start(f32[8,128]{1,0:T(8,128)S(1)} %get-tuple-element.128.refs_0_), channel_id=1, source_target_pairs={{0,2},{1,3},{2,0},{3,1},{4,6},{5,7},{6,4},{7,5},{8,10},{9,11},{10,... | collective-permute-start | bytes 12296 | tf_op jit(solution)/shard_map/ppermute | solution.py:224
  64.8 2.5 %shard_map.134 = (bf16[2,512,512]{2,1,0:T(8,128)(2,1)S(1)}, bf16[2,512,512]{2,1,0:T(8,128)(2,1)S(1)}, bf16[2,512,512]{2,1,0:T(8,128)(2,1)S(1)}, bf16[512,512]{1,0:T(8,128)(2,1)S(1)}, f32[8,128]{1,0:T(8,128)S(1)}) custom-call(f32[512,512]{1,0:T(8,128)S(1)} %get-tuple-element.126.total_ref, bf16[512,512]{1,0:T(8,128)(2,1)S(1)} %get-tuple-element.116.wg.weight), custom_call_target="tpu_custom_call" | custom-call | flops 1 | bytes 1 | tf_op jit(solution)/shard_map/pallas_call | solution.py:624
  67.4 1.6 %shard_map.135 = (bf16[128,512]{1,0:T(8,128)(2,1)S(1)}, bf16[4,3,64,512]{3,2,1,0:T(8,128)(2,1)S(1)}, bf16[4,3,64,512]{3,2,1,0:T(8,128)(2,1)S(1)}) custom-call(s32[1]{0:T(128)} %bitcast.me_ref, bf16[128,512]{1,0:T(8,128)(2,1)S(1)} %get-tuple-element.119.queries, bf16[128,512]{1,0:T(8,128)(2,1)S(1)} %get-tuple-element.120.upstream, f32[1,512]{1,0:T(1,128)S(1)} %bitcast.3, ...), custom_call_target="tpu_custom_call" | custom-call | flops 1 | bytes 1 | tf_op jit(solution)/shard_map/pallas_call | solution.py:639
  69.1 1.6 %collective-permute-start.17 = (bf16[4,3,64,512]{3,2,1,0:T(8,128)(2,1)S(1)}, bf16[4,3,64,512]{3,2,1,0:T(8,128)(2,1)S(1)}, u32[]{:S(2)}, u32[]{:S(2)}) collective-permute-start(bf16[4,3,64,512]{3,2,1,0:T(8,128)(2,1)S(1)} %get-tuple-element.168), channel_id=1, source_target_pairs={{0,4},{4,0},{8,12},{12,8},{16,20},{20,16},{24,28},{28,24},{1,5},{5... | collective-permute-start | bytes 2359304 | tf_op jit(solution)/shard_map/ppermute | solution.py:214
  71.8 2.5 %shard_map.136 = (bf16[2,512,512]{2,1,0:T(8,128)(2,1)S(1)}, bf16[2,512,512]{2,1,0:T(8,128)(2,1)S(1)}, bf16[2,512,512]{2,1,0:T(8,128)(2,1)S(1)}, bf16[512,512]{1,0:T(8,128)(2,1)S(1)}, f32[8,128]{1,0:T(8,128)S(1)}) custom-call(f32[512,512]{1,0:T(8,128)S(1)} %get-tuple-element.131.total_ref, bf16[512,512]{1,0:T(8,128)(2,1)S(1)} %get-tuple-element.117.wu.weight), custom_call_target="tpu_custom_call" | custom-call | flops 1 | bytes 1 | tf_op jit(solution)/shard_map/pallas_call | solution.py:624
  74.3 2.5 %shard_map.137 = (bf16[2,512,512]{2,1,0:T(8,128)(2,1)S(1)}, bf16[2,512,512]{2,1,0:T(8,128)(2,1)S(1)}, bf16[2,512,512]{2,1,0:T(8,128)(2,1)S(1)}, bf16[512,512]{1,0:T(8,128)(2,1)S(1)}, f32[8,128]{1,0:T(8,128)S(1)}) custom-call(f32[512,512]{1,0:T(8,128)S(1)} %get-tuple-element.135.total_ref, bf16[512,512]{1,0:T(8,128)(2,1)S(1)} %get-tuple-element.118.wd.weight), custom_call_target="tpu_custom_call" | custom-call | flops 1 | bytes 1 | tf_op jit(solution)/shard_map/pallas_call | solution.py:624
  76.8 9.9 %collective-permute-done.13.refs_3_ = bf16[512,512]{1,0:T(8,128)(2,1)S(1)} collective-permute-done((bf16[512,512]{1,0:T(8,128)(2,1)S(1)}, bf16[512,512]{1,0:T(8,128)(2,1)S(1)}, u32[]{:S(2)}, u32[]{:S(2)}) %collective-permute-start.13) | collective-permute-done | bytes 524320 | tf_op jit(solution)/shard_map/ppermute | solution.py:210
  86.7 5.2 %shard_map.138 = (bf16[1024,512]{1,0:T(8,128)(2,1)S(1)}, bf16[1024,512]{1,0:T(8,128)(2,1)S(1)}, f32[1024,512]{1,0:T(8,128)S(1)}, f32[1024,512]{1,0:T(8,128)S(1)}...) custom-call(f32[1,512]{1,0:T(1,128)S(1)} %bitcast.4, ...), custom_call_target="tpu_custom_call" | custom-call | flops 1 | bytes 1 | tf_op jit(solution)/shard_map/pallas_call | solution.py:655
  92.0 3.3 %collective-permute-done.14.refs_1_ = f32[8,1024]{1,0:T(8,128)S(1)} collective-permute-done((f32[8,1024]{1,0:T(8,128)S(1)}, f32[8,1024]{1,0:T(8,128)S(1)}, u32[]{:S(2)}, u32[]{:S(2)}) %collective-permute-start.14) | collective-permute-done | bytes 32800 | tf_op jit(solution)/shard_map/ppermute | solution.py:224
  95.6 2.3 %collective-permute-start.19 = (bf16[3,64,512]{2,1,0:T(8,128)(2,1)S(1)}, bf16[3,64,512]{2,1,0:T(8,128)(2,1)S(1)}, u32[]{:S(2)}, u32[]{:S(2)}) collective-permute-start(bf16[3,64,512]{2,1,0:T(8,128)(2,1)S(1)} %get-tuple-element.171), channel_id=1, source_target_pairs={{0,16},{4,20},{8,24},{12,28},{16,0},{20,4},{24,8},{28,12},{1,17},{... | collective-permute-start | bytes 589832 | tf_op jit(solution)/shard_map/ppermute | solution.py:210
  97.9 1.6 %collective-permute-start.20 = (bf16[3,64,512]{2,1,0:T(8,128)(2,1)S(1)}, bf16[3,64,512]{2,1,0:T(8,128)(2,1)S(1)}, u32[]{:S(2)}, u32[]{:S(2)}) collective-permute-start(bf16[3,64,512]{2,1,0:T(8,128)(2,1)S(1)} %get-tuple-element.172), channel_id=1, source_target_pairs={{0,24},{4,28},{8,0},{12,4},{16,8},{20,12},{24,16},{28,20},{1,25},{... | collective-permute-start | bytes 589832 | tf_op jit(solution)/shard_map/ppermute | solution.py:210
  100.9 2.5 %collective-permute-done.15.refs_2_ = f32[8,1024]{1,0:T(8,128)S(1)} collective-permute-done((f32[8,1024]{1,0:T(8,128)S(1)}, f32[8,1024]{1,0:T(8,128)S(1)}, u32[]{:S(2)}, u32[]{:S(2)}) %collective-permute-start.15) | collective-permute-done | bytes 32800 | tf_op jit(solution)/shard_map/ppermute | solution.py:224
  104.6 4.4 %shard_map.139 = (bf16[2,128,512]{2,1,0:T(8,128)(2,1)}, f32[512,512]{1,0:T(8,128)S(1)}, f32[512,512]{1,0:T(8,128)S(1)}, f32[512,512]{1,0:T(8,128)S(1)}) custom-call(bf16[128,512]{1,0:T(8,128)(2,1)S(1)} %get-tuple-element.129.grad_first, bf16[1024,512]{1,0:T(8,128)(2,1)S(1)} %get-tuple-element.138.queries, bf16[1024,512]{1,0:T(8,128)(2,1)S(1)} %copy-done.2, ...), custom_call_target="tpu_custom_call" | custom-call | flops 1 | bytes 1 | tf_op jit(solution)/shard_map/pallas_call | solution.py:680
  109.0 4.3 %shard_map.140.cot_g = bf16[512,512]{1,0:T(8,128)(2,1)S(1)} custom-call(f32[512,512]{1,0:T(8,128)S(1)} %get-tuple-element.151.rate.rate_g, f32[512,512]{1,0:T(8,128)S(1)} %get-tuple-element.126.total_ref, bf16[2,512,512]{2,1,0:T(8,128)(2,1)S(1)} %get-tuple-element.152.xs, bf16[2,512,512]{2,1,0:T(8,128)(2,1)S(1)} %get-tuple-element.153.grams, ...), custom_call_target="tpu_custom_call" | custom-call | flops 1 | bytes 1 | tf_op jit(solution)/shard_map/pallas_call | solution.py:692
  113.3 4.3 %shard_map.142.cot_d = bf16[512,512]{1,0:T(8,128)(2,1)S(1)} custom-call(f32[512,512]{1,0:T(8,128)S(1)} %get-tuple-element.160.rate.rate_d, f32[512,512]{1,0:T(8,128)S(1)} %get-tuple-element.135.total_ref, bf16[2,512,512]{2,1,0:T(8,128)(2,1)S(1)} %get-tuple-element.161.xs, bf16[2,512,512]{2,1,0:T(8,128)(2,1)S(1)} %get-tuple-element.162.grams, ...), custom_call_target="tpu_custom_call" | custom-call | flops 1 | bytes 1 | tf_op jit(solution)/shard_map/pallas_call | solution.py:692
  117.6 4.6 %shard_map.141.cot_u = bf16[512,512]{1,0:T(8,128)(2,1)S(1)} custom-call(f32[512,512]{1,0:T(8,128)S(1)} %get-tuple-element.155.rate.rate_u, f32[512,512]{1,0:T(8,128)S(1)} %get-tuple-element.131.total_ref, bf16[2,512,512]{2,1,0:T(8,128)(2,1)S(1)} %get-tuple-element.156.xs, bf16[2,512,512]{2,1,0:T(8,128)(2,1)S(1)} %get-tuple-element.157.grams, ...), custom_call_target="tpu_custom_call" | custom-call | flops 1 | bytes 1 | tf_op jit(solution)/shard_map/pallas_call | solution.py:692
  122.2 7.3 %shard_map.144 = (bf16[128,512]{1,0:T(8,128)(2,1)}, bf16[128,512]{1,0:T(8,128)(2,1)}, f32[1,64,512]{2,1,0:T(8,128)}, f32[1,64,512]{2,1,0:T(8,128)}, f32[1,64,512]{2,1,0:T(8,128)}) custom-call(s32[1]{0:T(128)} %bitcast.me_ref, bf16[1024,512]{1,0:T(8,128)(2,1)S(1)} %get-tuple-element.146.keys, bf16[1024,512]{1,0:T(8,128)(2,1)S(1)} %get-tuple-element.147.values, ...), custom_call_target="tpu_custom_call" | custom-call | flops 1 | bytes 1 | tf_op jit(solution)/shard_map/pallas_call | solution.py:703
  (42 shorter events, 11.9 us)
Async XLA Ops:
  2.8 14.6 %collective-permute-start.2 = (bf16[448,512]{1,0:T(8,128)(2,1)}, bf16[448,512]{1,0:T(8,128)(2,1)S(1)}, u32[]{:S(2)}, u32[]{:S(2)}) collective-permute-start(bf16[448,512]{1,0:T(8,128)(2,1)} %get-tuple-element.92.refs_0_.refs_2_), channel_id=1, source_target_pairs={{0,4},{4,0},{8,12},{12,8},{16,20},{20,16},{24,28},{28,24},{1,5},{5... | collective-permute-start | bytes 1376264 | tf_op jit(solution)/shard_map/ppermute | solution.py:214
  5.8 18.3 %collective-permute-start = (bf16[448,512]{1,0:T(8,128)(2,1)}, bf16[448,512]{1,0:T(8,128)(2,1)S(1)}, u32[]{:S(2)}, u32[]{:S(2)}) collective-permute-start(bf16[448,512]{1,0:T(8,128)(2,1)} %get-tuple-element.92.refs_0_.refs_2_), channel_id=1, source_target_pairs={{0,8},{4,12},{8,16},{12,20},{16,24},{20,28},{24,0},{28,4},{1,9},{5... | collective-permute-start | bytes 1376264 | tf_op jit(solution)/shard_map/ppermute | solution.py:210
  7.3 18.3 %collective-permute-start.1 = (bf16[256,512]{1,0:T(8,128)(2,1)}, bf16[256,512]{1,0:T(8,128)(2,1)S(1)}, u32[]{:S(2)}, u32[]{:S(2)}) collective-permute-start(bf16[256,512]{1,0:T(8,128)(2,1)} %get-tuple-element.93.refs_2_), channel_id=1, source_target_pairs={{0,4},{4,0},{8,12},{12,8},{16,20},{20,16},{24,28},{28,24},{1,5},{5... | collective-permute-start | bytes 786440 | tf_op jit(solution)/shard_map/ppermute | solution.py:214
  17.3 1.0 copy-start
  19.9 15.2 %collective-permute-start.5 = (bf16[448,512]{1,0:T(8,128)(2,1)S(1)}, bf16[448,512]{1,0:T(8,128)(2,1)S(1)}, u32[]{:S(2)}, u32[]{:S(2)}) collective-permute-start(bf16[448,512]{1,0:T(8,128)(2,1)S(1)} %get-tuple-element.100), channel_id=1, source_target_pairs={{0,24},{4,28},{8,0},{12,4},{16,8},{20,12},{24,16},{28,20},{1,25},{... | collective-permute-start | bytes 1376264 | tf_op jit(solution)/shard_map/ppermute | solution.py:210
  24.1 11.0 %collective-permute-start.7 = (bf16[448,512]{1,0:T(8,128)(2,1)S(1)}, bf16[448,512]{1,0:T(8,128)(2,1)S(1)}, u32[]{:S(2)}, u32[]{:S(2)}) collective-permute-start(bf16[448,512]{1,0:T(8,128)(2,1)S(1)} %collective-permute-done.refs_0_.refs_1_), channel_id=1, source_target_pairs={{0,4},{4,0},{8,12},{12,8},{16,20},{20,16},{24,28},{28,24},{1,5},{5... | collective-permute-start | bytes 1376264 | tf_op jit(solution)/shard_map/ppermute | solution.py:214
  25.6 9.5 %copy-start.5 = (bf16[256,512]{1,0:T(8,128)(2,1)S(1)}, bf16[256,512]{1,0:T(8,128)(2,1)}, u32[]{:S(2)}) copy-start(bf16[256,512]{1,0:T(8,128)(2,1)} %get-tuple-element.93.refs_2_) | copy-start | bytes 786436
  26.5 19.3 %collective-permute-start.3 = (bf16[448,512]{1,0:T(8,128)(2,1)S(1)}, bf16[448,512]{1,0:T(8,128)(2,1)S(1)}, u32[]{:S(2)}, u32[]{:S(2)}) collective-permute-start(bf16[448,512]{1,0:T(8,128)(2,1)S(1)} %get-tuple-element.99), channel_id=1, source_target_pairs={{0,8},{4,12},{8,16},{12,20},{16,24},{20,28},{24,0},{28,4},{1,9},{5... | collective-permute-start | bytes 1376264 | tf_op jit(solution)/shard_map/ppermute | solution.py:210
  36.5 32.6 %collective-permute-start.11 = (bf16[512,512]{1,0:T(8,128)(2,1)S(1)}, bf16[512,512]{1,0:T(8,128)(2,1)S(1)}, u32[]{:S(2)}, u32[]{:S(2)}) collective-permute-start(bf16[512,512]{1,0:T(8,128)(2,1)S(1)} %get-tuple-element.134.refs_0_), channel_id=1, source_target_pairs={{0,24},{4,28},{8,0},{12,4},{16,8},{20,12},{24,16},{28,20},{1,25},{... | collective-permute-start | bytes 1572872 | tf_op jit(solution)/shard_map/ppermute | solution.py:210
  40.8 11.3 %collective-permute-start.6 = (bf16[448,512]{1,0:T(8,128)(2,1)S(1)}, bf16[448,512]{1,0:T(8,128)(2,1)S(1)}, u32[]{:S(2)}, u32[]{:S(2)}) collective-permute-start(bf16[448,512]{1,0:T(8,128)(2,1)S(1)} %collective-permute-done.5.refs_0_), channel_id=1, source_target_pairs={{0,4},{4,0},{8,12},{12,8},{16,20},{20,16},{24,28},{28,24},{1,5},{5... | collective-permute-start | bytes 1376264 | tf_op jit(solution)/shard_map/ppermute | solution.py:214
  45.9 11.2 %collective-permute-start.4 = (bf16[448,512]{1,0:T(8,128)(2,1)S(1)}, bf16[448,512]{1,0:T(8,128)(2,1)S(1)}, u32[]{:S(2)}, u32[]{:S(2)}) collective-permute-start(bf16[448,512]{1,0:T(8,128)(2,1)S(1)} %collective-permute-done.3.refs_0_), channel_id=1, source_target_pairs={{0,4},{4,0},{8,12},{12,8},{16,20},{20,16},{24,28},{28,24},{1,5},{5... | collective-permute-start | bytes 1376264 | tf_op jit(solution)/shard_map/ppermute | solution.py:214
  47.4 23.3 %collective-permute-start.12 = (bf16[512,512]{1,0:T(8,128)(2,1)S(1)}, bf16[512,512]{1,0:T(8,128)(2,1)S(1)}, u32[]{:S(2)}, u32[]{:S(2)}) collective-permute-start(bf16[512,512]{1,0:T(8,128)(2,1)S(1)} %get-tuple-element.134.refs_0_), channel_id=1, source_target_pairs={{0,8},{4,12},{8,16},{12,20},{16,24},{20,28},{24,0},{28,4},{1,9},{5... | collective-permute-start | bytes 1572872 | tf_op jit(solution)/shard_map/ppermute | solution.py:210
  53.4 8.8 %copy-start.3 = (bf16[2,128,512]{2,1,0:T(8,128)(2,1)S(1)}, bf16[2,128,512]{2,1,0:T(8,128)(2,1)}, u32[]{:S(2)}) copy-start(bf16[2,128,512]{2,1,0:T(8,128)(2,1)} %queries_ref.1) | copy-start | bytes 786436
  53.4 8.8 %copy-start.4 = (bf16[2,128,512]{2,1,0:T(8,128)(2,1)S(1)}, bf16[2,128,512]{2,1,0:T(8,128)(2,1)}, u32[]{:S(2)}) copy-start(bf16[2,128,512]{2,1,0:T(8,128)(2,1)} %upstream_ref.1) | copy-start | bytes 786436
  53.4 8.8 %copy-start.6 = (f32[512]{0:T(512)S(1)}, f32[512]{0:T(512)}, u32[]{:S(2)}) copy-start(f32[512]{0:T(512)} %param.12) | copy-start | bytes 6148
  62.8 4.6 %collective-permute-start.10 = (f32[8,128]{1,0:T(8,128)S(1)}, f32[8,128]{1,0:T(8,128)S(1)}, u32[]{:S(2)}, u32[]{:S(2)}) collective-permute-start(f32[8,128]{1,0:T(8,128)S(1)} %get-tuple-element.128.refs_0_), channel_id=1, source_target_pairs={{0,3},{1,0},{2,1},{3,2},{4,7},{5,4},{6,5},{7,6},{8,11},{9,8},{10,9... | collective-permute-start | bytes 12296 | tf_op jit(solution)/shard_map/ppermute | solution.py:224
  62.8 4.6 %collective-permute-start.8 = (f32[8,128]{1,0:T(8,128)S(1)}, f32[8,128]{1,0:T(8,128)S(1)}, u32[]{:S(2)}, u32[]{:S(2)}) collective-permute-start(f32[8,128]{1,0:T(8,128)S(1)} %get-tuple-element.128.refs_0_), channel_id=1, source_target_pairs={{0,1},{1,2},{2,3},{3,0},{4,5},{5,6},{6,7},{7,4},{8,9},{9,10},{10,1... | collective-permute-start | bytes 12296 | tf_op jit(solution)/shard_map/ppermute | solution.py:224
  63.3 4.1 %collective-permute-start.9 = (f32[8,128]{1,0:T(8,128)S(1)}, f32[8,128]{1,0:T(8,128)S(1)}, u32[]{:S(2)}, u32[]{:S(2)}) collective-permute-start(f32[8,128]{1,0:T(8,128)S(1)} %get-tuple-element.128.refs_0_), channel_id=1, source_target_pairs={{0,2},{1,3},{2,0},{3,1},{4,6},{5,7},{6,4},{7,5},{8,10},{9,11},{10,... | collective-permute-start | bytes 12296 | tf_op jit(solution)/shard_map/ppermute | solution.py:224
  69.1 26.3 %collective-permute-start.17 = (bf16[4,3,64,512]{3,2,1,0:T(8,128)(2,1)S(1)}, bf16[4,3,64,512]{3,2,1,0:T(8,128)(2,1)S(1)}, u32[]{:S(2)}, u32[]{:S(2)}) collective-permute-start(bf16[4,3,64,512]{3,2,1,0:T(8,128)(2,1)S(1)} %get-tuple-element.168), channel_id=1, source_target_pairs={{0,4},{4,0},{8,12},{12,8},{16,20},{20,16},{24,28},{28,24},{1,5},{5... | collective-permute-start | bytes 2359304 | tf_op jit(solution)/shard_map/ppermute | solution.py:214
  70.6 16.1 %collective-permute-start.13 = (bf16[512,512]{1,0:T(8,128)(2,1)S(1)}, bf16[512,512]{1,0:T(8,128)(2,1)S(1)}, u32[]{:S(2)}, u32[]{:S(2)}) collective-permute-start(bf16[512,512]{1,0:T(8,128)(2,1)S(1)} %collective-permute-done.12.refs_1_), channel_id=1, source_target_pairs={{0,8},{4,12},{8,16},{12,20},{16,24},{20,28},{24,0},{28,4},{1,9},{5... | collective-permute-start | bytes 1572872 | tf_op jit(solution)/shard_map/ppermute | solution.py:210
  91.9 11.5 %copy-start.1 = (bf16[1024,512]{1,0:T(8,128)(2,1)}, bf16[1024,512]{1,0:T(8,128)(2,1)S(1)}, u32[]{:S(2)}) copy-start(bf16[1024,512]{1,0:T(8,128)(2,1)S(1)} %get-tuple-element.139.upstream) | copy-start | bytes 3145732
  91.9 3.4 %collective-permute-start.14 = (f32[8,1024]{1,0:T(8,128)S(1)}, f32[8,1024]{1,0:T(8,128)S(1)}, u32[]{:S(2)}, u32[]{:S(2)}) collective-permute-start(f32[8,1024]{1,0:T(8,128)S(1)} %get-tuple-element.144.refs_0_), channel_id=1, source_target_pairs={{0,1},{1,2},{2,3},{3,0},{4,5},{5,6},{6,7},{7,4},{8,9},{9,10},{10,1... | collective-permute-start | bytes 98312 | tf_op jit(solution)/shard_map/ppermute | solution.py:224
  95.5 26.7 %collective-permute-start.18 = (bf16[3,64,512]{2,1,0:T(8,128)(2,1)S(1)}, bf16[3,64,512]{2,1,0:T(8,128)(2,1)S(1)}, u32[]{:S(2)}, u32[]{:S(2)}) collective-permute-start(bf16[3,64,512]{2,1,0:T(8,128)(2,1)S(1)} %get-tuple-element.170), channel_id=1, source_target_pairs={{0,8},{4,12},{8,16},{12,20},{16,24},{20,28},{24,0},{28,4},{1,9},{5... | collective-permute-start | bytes 589832 | tf_op jit(solution)/shard_map/ppermute | solution.py:210
  95.6 26.7 %collective-permute-start.19 = (bf16[3,64,512]{2,1,0:T(8,128)(2,1)S(1)}, bf16[3,64,512]{2,1,0:T(8,128)(2,1)S(1)}, u32[]{:S(2)}, u32[]{:S(2)}) collective-permute-start(bf16[3,64,512]{2,1,0:T(8,128)(2,1)S(1)} %get-tuple-element.171), channel_id=1, source_target_pairs={{0,16},{4,20},{8,24},{12,28},{16,0},{20,4},{24,8},{28,12},{1,17},{... | collective-permute-start | bytes 589832 | tf_op jit(solution)/shard_map/ppermute | solution.py:210
  97.9 24.4 %collective-permute-start.20 = (bf16[3,64,512]{2,1,0:T(8,128)(2,1)S(1)}, bf16[3,64,512]{2,1,0:T(8,128)(2,1)S(1)}, u32[]{:S(2)}, u32[]{:S(2)}) collective-permute-start(bf16[3,64,512]{2,1,0:T(8,128)(2,1)S(1)} %get-tuple-element.172), channel_id=1, source_target_pairs={{0,24},{4,28},{8,0},{12,4},{16,8},{20,12},{24,16},{28,20},{1,25},{... | collective-permute-start | bytes 589832 | tf_op jit(solution)/shard_map/ppermute | solution.py:210
  99.5 3.9 %collective-permute-start.15 = (f32[8,1024]{1,0:T(8,128)S(1)}, f32[8,1024]{1,0:T(8,128)S(1)}, u32[]{:S(2)}, u32[]{:S(2)}) collective-permute-start(f32[8,1024]{1,0:T(8,128)S(1)} %get-tuple-element.144.refs_0_), channel_id=1, source_target_pairs={{0,2},{1,3},{2,0},{3,1},{4,6},{5,7},{6,4},{7,5},{8,10},{9,11},{10,... | collective-permute-start | bytes 98312 | tf_op jit(solution)/shard_map/ppermute | solution.py:224
  100.9 2.5 %collective-permute-start.16 = (f32[8,1024]{1,0:T(8,128)S(1)}, f32[8,1024]{1,0:T(8,128)S(1)}, u32[]{:S(2)}, u32[]{:S(2)}) collective-permute-start(f32[8,1024]{1,0:T(8,128)S(1)} %get-tuple-element.144.refs_0_), channel_id=1, source_target_pairs={{0,3},{1,0},{2,1},{3,2},{4,7},{5,4},{6,5},{7,6},{8,11},{9,8},{10,9... | collective-permute-start | bytes 98312 | tf_op jit(solution)/shard_map/ppermute | solution.py:224
  103.4 1.2 copy-start.2

commit v4 on v3

--- a/solution.py
+++ b/solution.py
@@ -330,8 +330,10 @@
     return spread.T[:8]
 
 
-def forward_part(queries, upstream, gain, wg, wu, wd, gq_ref, uq_ref, hidden_ref, out_ref, stats):
-    for part in chunks_of(queries.shape[0]):
+def forward_part(
+    parts, queries, upstream, gain, wg, wu, wd, gq_ref, uq_ref, hidden_ref, out_ref, stats
+):
+    for part in parts:
         gq = product(queries[part], wg[...])
         uq = product(queries[part], wu[...])
         hidden = (gq * jax.nn.sigmoid(gq) * uq).astype(bf16)
@@ -375,7 +377,8 @@
     queries_ref, upstream_ref, gain, wg, wu, wd, queries, upstream, gq, uq, hidden, out, stats
 ):
     queries[...], upstream[...] = queries_ref[0], upstream_ref[0]
-    forward_part(queries, upstream, gain, wg, wu, wd, gq, uq, hidden, out, stats)
+    parts = chunks_of(queries.shape[0])
+    forward_part(parts, queries, upstream, gain, wg, wu, wd, gq, uq, hidden, out, stats)
 
 
 def first_backward_kernel(
@@ -407,19 +410,22 @@
         target[...] = (kept[place].astype(f32) + received[place].astype(f32)).astype(bf16)
 
 
-def second_forward_kernel(gain, wg, wu, wd, *refs):
-    count = len(refs) - 8
-    pieces, refs = refs[:count], refs[count:]
-    queries, upstream, gq, uq, hidden, out, stats, sems = refs
-    tokens = queries.shape[0] // (2 * count)
+def second_forward_kernel(first, count, gain, wg, wu, wd, *refs):
+    pieces = refs[:count]
+    queries, upstream, gq, uq, hidden, out, stats, sems = refs[-8:]
+    tokens = pieces[0].shape[0] // 4
     rows = []
     for slot, piece in enumerate(pieces):
         for half in range(2):
-            place = (2 * slot + half) * tokens
+            place = (2 * (first + slot) + half) * tokens
             rows.append((piece, 2 * half * tokens, queries, place, tokens))
             rows.append((piece, (2 * half + 1) * tokens, upstream, place, tokens))
     move(rows, sems)
-    forward_part(queries, upstream, gain, wg, wu, wd, gq, uq, hidden, out, stats)
+    parts = [
+        slice(part.start + 2 * first * tokens, part.stop + 2 * first * tokens)
+        for part in chunks_of(2 * count * tokens)
+    ]
+    forward_part(parts, queries, upstream, gain, wg, wu, wd, gq, uq, hidden, out, stats)
 
 
 def second_backward_kernel(
@@ -438,32 +444,43 @@
     rate_d[...] = across(hidden[...], d_out[...])
 
 
-def schulz_back_kernel(rate, total_ref, xs, grams, blends, root_ref, cot):
-    current = (-rate[...]).astype(bf16)
+def schulz_back_kernel(*refs):
+    rates, totals, xs, grams, blends, roots, cots = (refs[i:i + 3] for i in range(0, 21, 3))
+    symmetric, mixed = refs[21:]
+    for which in range(3):
+        cots[which][...] = (-rates[which][...]).astype(bf16)
     for sweep in reversed(range(NS_STEPS)):
-        iterate, gram, blend = xs[sweep], grams[sweep], blends[sweep]
-        symmetric = (against(current, iterate) + against(iterate, current)).astype(bf16)
-        bent = product(symmetric, gram) + product(gram, symmetric)
-        mixed = (cube_coef * symmetric.astype(f32) + fifth_coef * bent).astype(bf16)
-        current = (
-            lin_coef * current.astype(f32) + product(blend, current) + product(mixed, iterate)
-        ).astype(bf16)
-    root = root_ref[0:1, 0:1]
-    norm = root + fro_eps
-    total = total_ref[...]
-    bottom = current.astype(f32)
-    inner = jnp.sum(bottom * total, keepdims=True)
-    cot[...] = (bottom / norm - total * (inner / (norm * norm * root))).astype(bf16)
+        for which in range(3):
+            cross = against(cots[which][...], xs[which][sweep])
+            symmetric[which] = (cross + cross.T).astype(bf16)
+        for which in range(3):
+            bent = product(symmetric[which], grams[which][sweep])
+            mixed[which] = (
+                cube_coef * symmetric[which].astype(f32) + fifth_coef * (bent + bent.T)
+            ).astype(bf16)
+        for which in range(3):
+            cots[which][...] = (
+                lin_coef * cots[which][...].astype(f32)
+                + product(blends[which][sweep], cots[which][...])
+                + product(mixed[which], xs[which][sweep])
+            ).astype(bf16)
+    for which in range(3):
+        root = roots[which][0:1, 0:1]
+        norm = root + fro_eps
+        total = totals[which][...]
+        bottom = cots[which][...].astype(f32)
+        inner = jnp.sum(bottom * total, keepdims=True)
+        cots[which][...] = (bottom / norm - total * (inner / (norm * norm * root))).astype(bf16)
 
 
 def last_kernel(
     own, scale, me_ref, keys, values, wg, wu, wd, gk_ref, uk_ref, back_ref,
     cot_g, cot_u, cot_d, rate_g, rate_u, rate_d, *refs,
 ):
-    count = len(refs) - 12
+    count = len(refs) - 13
     firsts = refs[:count]
     grad_keys, grad_values, grad_g, grad_u, grad_d = refs[count:count + 5]
-    lower, upper, d_back, pk, rk, hk, total = refs[count + 5:]
+    lower, upper, d_back, pk, rk, hk, keys_t, back_t = refs[count + 5:]
     for part in chunks_of(keys.shape[0]):
         gk, uk, back = gk_ref[part], uk_ref[part], back_ref[part]
         sigma = jax.nn.sigmoid(gk)
@@ -473,7 +490,10 @@
         ek = product(keys[part], cot_g[...])
         fk = product(keys[part], cot_u[...])
         hk_part = -against(values[part], cot_d[...])
-        d_back[part] = (ek * uk * slope + fk * active).astype(bf16)
+        d_back_part = (ek * uk * slope + fk * active).astype(bf16)
+        d_back[part] = d_back_part
+        back_t[:, part] = d_back_part.T
+        keys_t[:, part] = keys[part].T
         upper[part] = (ek * back * slope + hk_part * active).astype(bf16)
         lower[part] = (
             ek * back * uk * curve + fk * back * slope + hk_part * uk * slope
@@ -494,14 +514,12 @@
     rows = grad_g.shape[1]
     start = pl.multiple_of(me_ref[0] * rows, 16)
     for which, (left, right, rate, grad) in enumerate((
-        (keys, lower, rate_g, grad_g), (keys, upper, rate_u, grad_u), (d_back, values, rate_d, grad_d)
+        (keys_t, lower, rate_g, grad_g), (keys_t, upper, rate_u, grad_u), (back_t, values, rate_d, grad_d)
     )):
-        total[...] = across(left[...], right[...])
-        second = total[pl.ds(start, rows)]
+        second = product(left[pl.ds(start, rows)], right[...])
         first = sum(ref[which].astype(f32) for ref in firsts)
-        rate_rows = rate[pl.ds(start, rows)]
         both = first - second if which == 2 else first + second
-        grad[0] = (both + rate_rows) * scale
+        grad[0] = (both + rate[pl.ds(start, rows)]) * scale
 
 
 def vmem():
@@ -652,19 +670,27 @@
     forward = [first_weight, schulz(1, totals[1]), schulz(2, tie(totals[2], down))]
 
     seconds = [forward[which][3] for which in range(3)]
-    all_queries, all_upstream, gq, uq, hidden_q, out, stats = pl.pallas_call(
-        second_forward_kernel,
-        out_shape=(
-            S((tokens, depth), bf16), S((tokens, depth), bf16),
-            S((tokens, hidden), f32), S((tokens, hidden), f32), S((tokens, hidden), bf16),
-            S((tokens, depth), f32), S((8, tokens), f32),
-        ),
-        in_specs=[vmem()] * 4 + [anywhere()] * len(pairs),
-        out_specs=[vmem()] * 7,
-        scratch_shapes=[pltpu.SemaphoreType.DMA((4 * len(pairs),))],
-        cost_estimate=light(),
-        compiler_params=params(24),
-    )(gain, *seconds, *pairs)
+    def second_forward(first, arrived, state=()):
+        start = 4 + len(arrived)
+        return pl.pallas_call(
+            functools.partial(second_forward_kernel, first, len(arrived)),
+            out_shape=(
+                S((tokens, depth), bf16), S((tokens, depth), bf16),
+                S((tokens, hidden), f32), S((tokens, hidden), f32), S((tokens, hidden), bf16),
+                S((tokens, depth), f32), S((8, tokens), f32),
+            ),
+            in_specs=[vmem()] * 4 + [anywhere()] * (len(arrived) + len(state)),
+            out_specs=[vmem()] * 7,
+            scratch_shapes=[pltpu.SemaphoreType.DMA((4 * len(arrived),))],
+            input_output_aliases={start + index: index for index in range(len(state))},
+            cost_estimate=light(),
+            compiler_params=params(24),
+        )(gain, *seconds, *arrived, *state)
+
+    state = second_forward(0, pairs[:-1])
+    all_queries, all_upstream, gq, uq, hidden_q, out, stats = second_forward(
+        len(pairs) - 1, pairs[-1:], state
+    )
     terms = head_terms(stats)
 
     block = S((3, rows, hidden), bf16)
@@ -688,17 +714,18 @@
         compiler_params=params(20),
     )(grad_first, all_queries, all_upstream, gain, *seconds, gq, uq, hidden_q, out, *terms)
 
-    cots = [
-        pl.pallas_call(
-            schulz_back_kernel,
-            out_shape=narrow,
-            in_specs=[vmem()] * 6,
-            out_specs=vmem(),
-            cost_estimate=light(),
-            compiler_params=params(16),
-        )(rates[which], totals[which], *forward[which][:3], forward[which][4])
-        for which in range(3)
-    ]
+    cots = pl.pallas_call(
+        schulz_back_kernel,
+        out_shape=(narrow,) * 3,
+        in_specs=[vmem()] * 18,
+        out_specs=[vmem()] * 3,
+        scratch_shapes=[pltpu.VMEM((3, *matrix), bf16)] * 2,
+        cost_estimate=light(),
+        compiler_params=params(20),
+    )(
+        *rates, *totals, *(forward[which][part] for part in (0, 1, 2) for which in range(3)),
+        *(forward[which][4] for which in range(3)),
+    )
 
     return (grad_queries, *pl.pallas_call(
         functools.partial(last_kernel, own, scale),
@@ -715,7 +742,8 @@
             pltpu.VMEM((own, hidden), bf16),
             pltpu.VMEM((own, hidden), bf16),
             pltpu.VMEM((own, hidden), bf16),
-            pltpu.VMEM(matrix, f32),
+            pltpu.VMEM((depth, tokens), bf16),
+            pltpu.VMEM((hidden, tokens), bf16),
         ],
         cost_estimate=light(),
         compiler_params=params(24),

time: 130 us -> 119 us (0.915)
  Pallas kernels: 52.3 us -> 47 us
  waiting for transfers between devices: 44.1 us -> 39.1 us
    ppermute x9, waiting for transfers between devices: 22 us -> 17 us  [shift(): return lax.ppermute(array, 'tok', pairs)]
    pallas_call x4 -> x3, Pallas kernels: 18.3 us -> 13.8 us  [the longest x1 8.34 us: gather_tokens(): pl.pallas_call(schulz_back_kernel, out_shape=(narrow,) * 3, in_specs=[vme...]
  transfers between devices with their start and end apart: 21 -> 21, of which waited for: 8 -> 8; matrix products, arithmetic and copies ran while one was open for 0% -> 0% of each run, Pallas kernels for 33% -> 32%
where the time goes in v4:
time: 119 us
  Pallas kernels  47 us (39%)
  waiting for transfers between devices  39.1 us (33%)
  starting transfers between devices  30 us (25%)
  local copies, waits for them, and re-layouts  2.02 us (2%)
    ppermute x9, waiting for transfers between devices, shift(): return lax.ppermute(array, 'tok', pairs)  17 us
    ppermute x9, starting transfers between devices, shift(): return lax.ppermute(array, 'tok', pairs)  16.9 us
    ppermute x6, waiting for transfers between devices, swap(): return lax.ppermute(array, 'tok', [(i, i ^ 1) for i in range(2 * ring)])  16.3 us
    ppermute x6, starting transfers between devices, swap(): return lax.ppermute(array, 'tok', [(i, i ^ 1) for i in range(2 * ring)])  9.58 us
    pallas_call x1, Pallas kernels, gather_tokens(): pl.pallas_call(schulz_back_kernel, out_shape=(narrow,) * 3, in_specs=[vme...  8.34 us
    pallas_call x3, Pallas kernels, schulz(): pl.pallas_call(schulz_kernel, out_shape=(S((NS_STEPS, *matrix), bf16), S(...  7.61 us
    pallas_call x1, Pallas kernels, gather_tokens(): pl.pallas_call(functools.partial(last_kernel, own, scale), out_shape=(S((...  6.51 us
    ppermute x6, waiting for transfers between devices, head_terms(): lax.ppermute(stats, 'head', [(i, (i + k) % heads) for i in range(heads)])  5.81 us
  transfers between devices with their start and end apart: 21, of which 8 were waited for; matrix products, arithmetic and copies ran while one was open for 0% of the time, Pallas kernels for 32%

profile of v4, /device:TPU:0, one launch (start us, length us, event | category | flops | bytes accessed | tf_op | source)
XLA Modules:
  0.0 119.0 jit_solution(2782575402864762322)
XLA Ops:
  0.6 2.1 %shard_map.127 = (bf16[448,512]{1,0:T(8,128)(2,1)}, bf16[256,512]{1,0:T(8,128)(2,1)}) custom-call(bf16[1,64,512]{2,1,0:T(8,128)(2,1)} %gate.1, bf16[1,64,512]{2,1,0:T(8,128)(2,1)} %up.1, bf16[1,64,512]{2,1,0:T(8,128)(2,1)} %down.1, bf16[128,512]{1,0:T(8,128)(2,1)} %keys.1, bf16[128,512]{1,0:T(8,128)(2,1)} %values.1, bf16[2,128,512]{2,1,0:T(8,128)(2,1)} %queries_ref.1, ...), custom_call_target="tpu_custom_call" | custom-call | tf_op jit(solution)/shard_map/pallas_call | solution.py:566
  2.8 3.0 %collective-permute-start.2 = (bf16[448,512]{1,0:T(8,128)(2,1)}, bf16[448,512]{1,0:T(8,128)(2,1)S(1)}, u32[]{:S(2)}, u32[]{:S(2)}) collective-permute-start(bf16[448,512]{1,0:T(8,128)(2,1)} %get-tuple-element.102.refs_0_.refs_2_), channel_id=1, source_target_pairs={{0,4},{4,0},{8,12},{12,8},{16,20},{20,16},{24,28},{28,24},{1,5},{5... | collective-permute-start | bytes 1376264 | tf_op jit(solution)/shard_map/ppermute | solution.py:214
  5.8 1.6 %collective-permute-start = (bf16[448,512]{1,0:T(8,128)(2,1)}, bf16[448,512]{1,0:T(8,128)(2,1)S(1)}, u32[]{:S(2)}, u32[]{:S(2)}) collective-permute-start(bf16[448,512]{1,0:T(8,128)(2,1)} %get-tuple-element.102.refs_0_.refs_2_), channel_id=1, source_target_pairs={{0,8},{4,12},{8,16},{12,20},{16,24},{20,28},{24,0},{28,4},{1,9},{5... | collective-permute-start | bytes 1376264 | tf_op jit(solution)/shard_map/ppermute | solution.py:210
  7.9 9.4 %collective-permute-done.2.refs_1_ = bf16[448,512]{1,0:T(8,128)(2,1)S(1)} collective-permute-done((bf16[448,512]{1,0:T(8,128)(2,1)}, bf16[448,512]{1,0:T(8,128)(2,1)S(1)}, u32[]{:S(2)}, u32[]{:S(2)}) %collective-permute-start.2) | collective-permute-done | bytes 458784 | tf_op jit(solution)/shard_map/ppermute | solution.py:214
  18.3 1.5 %shard_map.128 = (bf16[512,512]{1,0:T(8,128)(2,1)S(1)}, bf16[512,512]{1,0:T(8,128)(2,1)S(1)}, bf16[512,512]{1,0:T(8,128)(2,1)S(1)}, bf16[1024,512]{1,0:T(8,128)(...) custom-call(s32[1]{0:T(128)} %bitcast.me_ref, bf16[448,512]{1,0:T(8,128)(2,1)S(1)} %copy-done, ...), custom_call_target="tpu_custom_call" | custom-call | flops 1 | bytes 1 | tf_op jit(solution)/shard_map/pallas_call | solution.py:583
  19.9 4.2 %collective-permute-start.5 = (bf16[448,512]{1,0:T(8,128)(2,1)S(1)}, bf16[448,512]{1,0:T(8,128)(2,1)S(1)}, u32[]{:S(2)}, u32[]{:S(2)}) collective-permute-start(bf16[448,512]{1,0:T(8,128)(2,1)S(1)} %get-tuple-element.110), channel_id=1, source_target_pairs={{0,24},{4,28},{8,0},{12,4},{16,8},{20,12},{24,16},{28,20},{1,25},{... | collective-permute-start | bytes 1376264 | tf_op jit(solution)/shard_map/ppermute | solution.py:210
  24.1 1.5 %collective-permute-start.7 = (bf16[448,512]{1,0:T(8,128)(2,1)S(1)}, bf16[448,512]{1,0:T(8,128)(2,1)S(1)}, u32[]{:S(2)}, u32[]{:S(2)}) collective-permute-start(bf16[448,512]{1,0:T(8,128)(2,1)S(1)} %collective-permute-done.refs_0_.refs_1_), channel_id=1, source_target_pairs={{0,4},{4,0},{8,12},{12,8},{16,20},{20,16},{24,28},{28,24},{1,5},{5... | collective-permute-start | bytes 1376264 | tf_op jit(solution)/shard_map/ppermute | solution.py:214
  26.6 8.5 %collective-permute-done.5.refs_0_ = bf16[448,512]{1,0:T(8,128)(2,1)S(1)} collective-permute-done((bf16[448,512]{1,0:T(8,128)(2,1)S(1)}, bf16[448,512]{1,0:T(8,128)(2,1)S(1)}, u32[]{:S(2)}, u32[]{:S(2)}) %collective-permute-start.5) | collective-permute-done | bytes 458784 | tf_op jit(solution)/shard_map/ppermute | solution.py:210
  36.5 4.3 %collective-permute-start.11 = (bf16[512,512]{1,0:T(8,128)(2,1)S(1)}, bf16[512,512]{1,0:T(8,128)(2,1)S(1)}, u32[]{:S(2)}, u32[]{:S(2)}) collective-permute-start(bf16[512,512]{1,0:T(8,128)(2,1)S(1)} %get-tuple-element.144.refs_0_), channel_id=1, source_target_pairs={{0,24},{4,28},{8,0},{12,4},{16,8},{20,12},{24,16},{28,20},{1,25},{... | collective-permute-start | bytes 1572872 | tf_op jit(solution)/shard_map/ppermute | solution.py:210
  40.8 1.5 %collective-permute-start.6 = (bf16[448,512]{1,0:T(8,128)(2,1)S(1)}, bf16[448,512]{1,0:T(8,128)(2,1)S(1)}, u32[]{:S(2)}, u32[]{:S(2)}) collective-permute-start(bf16[448,512]{1,0:T(8,128)(2,1)S(1)} %collective-permute-done.5.refs_0_), channel_id=1, source_target_pairs={{0,4},{4,0},{8,12},{12,8},{16,20},{20,16},{24,28},{28,24},{1,5},{5... | collective-permute-start | bytes 1376264 | tf_op jit(solution)/shard_map/ppermute | solution.py:214
  42.3 3.6 %collective-permute-done.3.refs_0_ = bf16[448,512]{1,0:T(8,128)(2,1)S(1)} collective-permute-done((bf16[448,512]{1,0:T(8,128)(2,1)S(1)}, bf16[448,512]{1,0:T(8,128)(2,1)S(1)}, u32[]{:S(2)}, u32[]{:S(2)}) %collective-permute-start.3) | collective-permute-done | bytes 458784 | tf_op jit(solution)/shard_map/ppermute | solution.py:210
  45.9 1.5 %collective-permute-start.4 = (bf16[448,512]{1,0:T(8,128)(2,1)S(1)}, bf16[448,512]{1,0:T(8,128)(2,1)S(1)}, u32[]{:S(2)}, u32[]{:S(2)}) collective-permute-start(bf16[448,512]{1,0:T(8,128)(2,1)S(1)} %collective-permute-done.3.refs_0_), channel_id=1, source_target_pairs={{0,4},{4,0},{8,12},{12,8},{16,20},{20,16},{24,28},{28,24},{1,5},{5... | collective-permute-start | bytes 1376264 | tf_op jit(solution)/shard_map/ppermute | solution.py:214
  47.4 1.6 %collective-permute-start.12 = (bf16[512,512]{1,0:T(8,128)(2,1)S(1)}, bf16[512,512]{1,0:T(8,128)(2,1)S(1)}, u32[]{:S(2)}, u32[]{:S(2)}) collective-permute-start(bf16[512,512]{1,0:T(8,128)(2,1)S(1)} %get-tuple-element.144.refs_0_), channel_id=1, source_target_pairs={{0,8},{4,12},{8,16},{12,20},{16,24},{20,28},{24,0},{28,4},{1,9},{5... | collective-permute-start | bytes 1572872 | tf_op jit(solution)/shard_map/ppermute | solution.py:210
  48.9 3.2 %collective-permute-done.6.refs_1_ = bf16[448,512]{1,0:T(8,128)(2,1)S(1)} collective-permute-done((bf16[448,512]{1,0:T(8,128)(2,1)S(1)}, bf16[448,512]{1,0:T(8,128)(2,1)S(1)}, u32[]{:S(2)}, u32[]{:S(2)}) %collective-permute-start.6) | collective-permute-done | bytes 458784 | tf_op jit(solution)/shard_map/ppermute | solution.py:214
  53.4 3.6 %collective-permute-done.4.refs_0_ = bf16[448,512]{1,0:T(8,128)(2,1)S(1)} collective-permute-done((bf16[448,512]{1,0:T(8,128)(2,1)S(1)}, bf16[448,512]{1,0:T(8,128)(2,1)S(1)}, u32[]{:S(2)}, u32[]{:S(2)}) %collective-permute-start.4) | collective-permute-done | bytes 458784 | tf_op jit(solution)/shard_map/ppermute | solution.py:214
  57.0 5.1 %shard_map.132 = (bf16[512,512]{1,0:T(8,128)(2,1)S(1)}, bf16[512,512]{1,0:T(8,128)(2,1)S(1)}, bf16[512,512]{1,0:T(8,128)(2,1)S(1)}, bf16[1024,512]{1,0:T(8,128)(...) custom-call(s32[1]{0:T(128)} %bitcast.me_ref, ...), custom_call_target="tpu_custom_call", output_to_operand_aliasing={{0}: (2, {}), {1}: (3, {}), {2}: (4, {}), {3}: (5, {}), {4}... | custom-call | flops 1 | bytes 1 | tf_op jit(solution)/shard_map/pallas_call | solution.py:610
  63.3 1.5 %collective-permute-start.9 = (f32[8,128]{1,0:T(8,128)S(1)}, f32[8,128]{1,0:T(8,128)S(1)}, u32[]{:S(2)}, u32[]{:S(2)}) collective-permute-start(f32[8,128]{1,0:T(8,128)S(1)} %get-tuple-element.138.refs_0_), channel_id=1, source_target_pairs={{0,2},{1,3},{2,0},{3,1},{4,6},{5,7},{6,4},{7,5},{8,10},{9,11},{10,... | collective-permute-start | bytes 12296 | tf_op jit(solution)/shard_map/ppermute | solution.py:224
  64.8 2.5 %shard_map.134 = (bf16[2,512,512]{2,1,0:T(8,128)(2,1)S(1)}, bf16[2,512,512]{2,1,0:T(8,128)(2,1)S(1)}, bf16[2,512,512]{2,1,0:T(8,128)(2,1)S(1)}, bf16[512,512]{1,0:T(8,128)(2,1)S(1)}, f32[8,128]{1,0:T(8,128)S(1)}) custom-call(f32[512,512]{1,0:T(8,128)S(1)} %get-tuple-element.136.total_ref.refs_3_, bf16[512,512]{1,0:T(8,128)(2,1)S(1)} %get-tuple-element.126.wg.weight), custom_call_target="tpu_custom_call" | custom-call | flops 1 | bytes 1 | tf_op jit(solution)/shard_map/pallas_call | solution.py:642
  67.4 1.6 %shard_map.135 = (bf16[128,512]{1,0:T(8,128)(2,1)S(1)}, bf16[4,3,64,512]{3,2,1,0:T(8,128)(2,1)S(1)}, bf16[4,3,64,512]{3,2,1,0:T(8,128)(2,1)S(1)}) custom-call(s32[1]{0:T(128)} %bitcast.me_ref, bf16[128,512]{1,0:T(8,128)(2,1)S(1)} %get-tuple-element.129.queries, bf16[128,512]{1,0:T(8,128)(2,1)S(1)} %get-tuple-element.130.upstream, f32[1,512]{1,0:T(1,128)S(1)} %bitcast.3, ...), custom_call_target="tpu_custom_call" | custom-call | flops 1 | bytes 1 | tf_op jit(solution)/shard_map/pallas_call | solution.py:657
  69.1 1.6 %collective-permute-start.17 = (bf16[4,3,64,512]{3,2,1,0:T(8,128)(2,1)S(1)}, bf16[4,3,64,512]{3,2,1,0:T(8,128)(2,1)S(1)}, u32[]{:S(2)}, u32[]{:S(2)}) collective-permute-start(bf16[4,3,64,512]{3,2,1,0:T(8,128)(2,1)S(1)} %get-tuple-element.188), channel_id=1, source_target_pairs={{0,4},{4,0},{8,12},{12,8},{16,20},{20,16},{24,28},{28,24},{1,5},{5... | collective-permute-start | bytes 2359304 | tf_op jit(solution)/shard_map/ppermute | solution.py:214
  71.8 2.5 %shard_map.136 = (bf16[2,512,512]{2,1,0:T(8,128)(2,1)S(1)}, bf16[2,512,512]{2,1,0:T(8,128)(2,1)S(1)}, bf16[2,512,512]{2,1,0:T(8,128)(2,1)S(1)}, bf16[512,512]{1,0:T(8,128)(2,1)S(1)}, f32[8,128]{1,0:T(8,128)S(1)}) custom-call(f32[512,512]{1,0:T(8,128)S(1)} %get-tuple-element.141.total_ref.refs_4_, bf16[512,512]{1,0:T(8,128)(2,1)S(1)} %get-tuple-element.127.wu.weight), custom_call_target="tpu_custom_call" | custom-call | flops 1 | bytes 1 | tf_op jit(solution)/shard_map/pallas_call | solution.py:642
  74.3 2.5 %shard_map.137 = (bf16[2,512,512]{2,1,0:T(8,128)(2,1)S(1)}, bf16[2,512,512]{2,1,0:T(8,128)(2,1)S(1)}, bf16[2,512,512]{2,1,0:T(8,128)(2,1)S(1)}, bf16[512,512]{1,0:T(8,128)(2,1)S(1)}, f32[8,128]{1,0:T(8,128)S(1)}) custom-call(f32[512,512]{1,0:T(8,128)S(1)} %get-tuple-element.145.total_ref.refs_5_, bf16[512,512]{1,0:T(8,128)(2,1)S(1)} %get-tuple-element.128.wd.weight), custom_call_target="tpu_custom_call" | custom-call | flops 1 | bytes 1 | tf_op jit(solution)/shard_map/pallas_call | solution.py:642
  77.8 3.9 %shard_map.138 = (bf16[1024,512]{1,0:T(8,128)(2,1)S(1)}, bf16[1024,512]{1,0:T(8,128)(2,1)S(1)}, f32[1024,512]{1,0:T(8,128)S(1)}, f32[1024,512]{1,0:T(8,128)S(1)}...) custom-call(f32[1,512]{1,0:T(1,128)S(1)} %bitcast.4, ...), custom_call_target="tpu_custom_call" | custom-call | flops 1 | bytes 1 | tf_op jit(solution)/shard_map/pallas_call | solution.py:675
  81.8 4.9 %collective-permute-done.13.refs_0_ = bf16[512,512]{1,0:T(8,128)(2,1)S(1)} collective-permute-done((bf16[512,512]{1,0:T(8,128)(2,1)S(1)}, bf16[512,512]{1,0:T(8,128)(2,1)S(1)}, u32[]{:S(2)}, u32[]{:S(2)}) %collective-permute-start.13) | collective-permute-done | bytes 524320 | tf_op jit(solution)/shard_map/ppermute | solution.py:210
  86.7 1.5 %shard_map.139 = (bf16[1024,512]{1,0:T(8,128)(2,1)S(1)}, bf16[1024,512]{1,0:T(8,128)(2,1)S(1)}, f32[1024,512]{1,0:T(8,128)S(1)}, f32[1024,512]{1,0:T(8,128)S(1)}...) custom-call(f32[1,512]{1,0:T(1,128)S(1)} %bitcast.5, ...), custom_call_target="tpu_custom_call", output_to_operand_aliasing={{0}: (5, {}), {1}: (6, {}), {2}: (7, {}), {3}: (8, {}), {4}... | custom-call | flops 1 | bytes 1 | tf_op jit(solution)/shard_map/pallas_call | solution.py:675
  88.3 3.3 %collective-permute-done.14.refs_1_ = f32[8,1024]{1,0:T(8,128)S(1)} collective-permute-done((f32[8,1024]{1,0:T(8,128)S(1)}, f32[8,1024]{1,0:T(8,128)S(1)}, u32[]{:S(2)}, u32[]{:S(2)}) %collective-permute-start.14) | collective-permute-done | bytes 32800 | tf_op jit(solution)/shard_map/ppermute | solution.py:224
  91.9 2.3 %collective-permute-start.19 = (bf16[3,64,512]{2,1,0:T(8,128)(2,1)S(1)}, bf16[3,64,512]{2,1,0:T(8,128)(2,1)S(1)}, u32[]{:S(2)}, u32[]{:S(2)}) collective-permute-start(bf16[3,64,512]{2,1,0:T(8,128)(2,1)S(1)} %get-tuple-element.191), channel_id=1, source_target_pairs={{0,16},{4,20},{8,24},{12,28},{16,0},{20,4},{24,8},{28,12},{1,17},{... | collective-permute-start | bytes 589832 | tf_op jit(solution)/shard_map/ppermute | solution.py:210
  94.2 1.6 %collective-permute-start.20 = (bf16[3,64,512]{2,1,0:T(8,128)(2,1)S(1)}, bf16[3,64,512]{2,1,0:T(8,128)(2,1)S(1)}, u32[]{:S(2)}, u32[]{:S(2)}) collective-permute-start(bf16[3,64,512]{2,1,0:T(8,128)(2,1)S(1)} %get-tuple-element.192), channel_id=1, source_target_pairs={{0,24},{4,28},{8,0},{12,4},{16,8},{20,12},{24,16},{28,20},{1,25},{... | collective-permute-start | bytes 589832 | tf_op jit(solution)/shard_map/ppermute | solution.py:210
  97.2 2.5 %collective-permute-done.15.refs_2_ = f32[8,1024]{1,0:T(8,128)S(1)} collective-permute-done((f32[8,1024]{1,0:T(8,128)S(1)}, f32[8,1024]{1,0:T(8,128)S(1)}, u32[]{:S(2)}, u32[]{:S(2)}) %collective-permute-start.15) | collective-permute-done | bytes 32800 | tf_op jit(solution)/shard_map/ppermute | solution.py:224
  99.7 4.4 %shard_map.140 = (bf16[2,128,512]{2,1,0:T(8,128)(2,1)}, f32[512,512]{1,0:T(8,128)S(1)}, f32[512,512]{1,0:T(8,128)S(1)}, f32[512,512]{1,0:T(8,128)S(1)}) custom-call(bf16[128,512]{1,0:T(8,128)(2,1)S(1)} %get-tuple-element.139.grad_first, bf16[1024,512]{1,0:T(8,128)(2,1)S(1)} %get-tuple-element.155.queries, bf16[1024,512]{1,0:T(8,128)(2,1)S(1)} %get-tuple-element.156.upstream, ...), custom_call_target="tpu_custom_call" | custom-call | flops 1 | bytes 1 | tf_op jit(solution)/shard_map/pallas_call | solution.py:706
  104.1 8.3 %shard_map.141 = (bf16[512,512]{1,0:T(8,128)(2,1)S(1)}, bf16[512,512]{1,0:T(8,128)(2,1)S(1)}, bf16[512,512]{1,0:T(8,128)(2,1)S(1)}) custom-call(f32[512,512]{1,0:T(8,128)S(1)} %get-tuple-element.168.refs_0_.rate_g, f32[512,512]{1,0:T(8,128)S(1)} %get-tuple-element.169.refs_1_.rate_u, f32[512,512]{1,0:T(8,128)S(1)} %get-tuple-element.170.refs_2_.rate_d, ...), custom_call_target="tpu_custom_call" | custom-call | flops 1 | bytes 1 | tf_op jit(solution)/shard_map/pallas_call | solution.py:717
  112.5 6.5 %shard_map.143 = (bf16[128,512]{1,0:T(8,128)(2,1)}, bf16[128,512]{1,0:T(8,128)(2,1)}, f32[1,64,512]{2,1,0:T(8,128)}, f32[1,64,512]{2,1,0:T(8,128)}, f32[1,64,512]{2,1,0:T(8,128)}) custom-call(s32[1]{0:T(128)} %bitcast.me_ref, bf16[1024,512]{1,0:T(8,128)(2,1)S(1)} %get-tuple-element.163.keys, bf16[1024,512]{1,0:T(8,128)(2,1)S(1)} %get-tuple-element.164.values, ...), custom_call_target="tpu_custom_call" | custom-call | flops 1 | bytes 1 | tf_op jit(solution)/shard_map/pallas_call | solution.py:730
  (41 shorter events, 10.2 us)
Async XLA Ops:
  2.8 14.6 %collective-permute-start.2 = (bf16[448,512]{1,0:T(8,128)(2,1)}, bf16[448,512]{1,0:T(8,128)(2,1)S(1)}, u32[]{:S(2)}, u32[]{:S(2)}) collective-permute-start(bf16[448,512]{1,0:T(8,128)(2,1)} %get-tuple-element.102.refs_0_.refs_2_), channel_id=1, source_target_pairs={{0,4},{4,0},{8,12},{12,8},{16,20},{20,16},{24,28},{28,24},{1,5},{5... | collective-permute-start | bytes 1376264 | tf_op jit(solution)/shard_map/ppermute | solution.py:214
  5.8 18.3 %collective-permute-start = (bf16[448,512]{1,0:T(8,128)(2,1)}, bf16[448,512]{1,0:T(8,128)(2,1)S(1)}, u32[]{:S(2)}, u32[]{:S(2)}) collective-permute-start(bf16[448,512]{1,0:T(8,128)(2,1)} %get-tuple-element.102.refs_0_.refs_2_), channel_id=1, source_target_pairs={{0,8},{4,12},{8,16},{12,20},{16,24},{20,28},{24,0},{28,4},{1,9},{5... | collective-permute-start | bytes 1376264 | tf_op jit(solution)/shard_map/ppermute | solution.py:210
  7.3 18.3 %collective-permute-start.1 = (bf16[256,512]{1,0:T(8,128)(2,1)}, bf16[256,512]{1,0:T(8,128)(2,1)S(1)}, u32[]{:S(2)}, u32[]{:S(2)}) collective-permute-start(bf16[256,512]{1,0:T(8,128)(2,1)} %get-tuple-element.103.refs_2_), channel_id=1, source_target_pairs={{0,4},{4,0},{8,12},{12,8},{16,20},{20,16},{24,28},{28,24},{1,5},{5... | collective-permute-start | bytes 786440 | tf_op jit(solution)/shard_map/ppermute | solution.py:214
  17.3 1.0 copy-start
  19.9 15.2 %collective-permute-start.5 = (bf16[448,512]{1,0:T(8,128)(2,1)S(1)}, bf16[448,512]{1,0:T(8,128)(2,1)S(1)}, u32[]{:S(2)}, u32[]{:S(2)}) collective-permute-start(bf16[448,512]{1,0:T(8,128)(2,1)S(1)} %get-tuple-element.110), channel_id=1, source_target_pairs={{0,24},{4,28},{8,0},{12,4},{16,8},{20,12},{24,16},{28,20},{1,25},{... | collective-permute-start | bytes 1376264 | tf_op jit(solution)/shard_map/ppermute | solution.py:210
  24.1 11.0 %collective-permute-start.7 = (bf16[448,512]{1,0:T(8,128)(2,1)S(1)}, bf16[448,512]{1,0:T(8,128)(2,1)S(1)}, u32[]{:S(2)}, u32[]{:S(2)}) collective-permute-start(bf16[448,512]{1,0:T(8,128)(2,1)S(1)} %collective-permute-done.refs_0_.refs_1_), channel_id=1, source_target_pairs={{0,4},{4,0},{8,12},{12,8},{16,20},{20,16},{24,28},{28,24},{1,5},{5... | collective-permute-start | bytes 1376264 | tf_op jit(solution)/shard_map/ppermute | solution.py:214
  25.6 9.5 %copy-start.5 = (bf16[256,512]{1,0:T(8,128)(2,1)S(1)}, bf16[256,512]{1,0:T(8,128)(2,1)}, u32[]{:S(2)}) copy-start(bf16[256,512]{1,0:T(8,128)(2,1)} %get-tuple-element.103.refs_2_) | copy-start | bytes 786436
  26.5 19.3 %collective-permute-start.3 = (bf16[448,512]{1,0:T(8,128)(2,1)S(1)}, bf16[448,512]{1,0:T(8,128)(2,1)S(1)}, u32[]{:S(2)}, u32[]{:S(2)}) collective-permute-start(bf16[448,512]{1,0:T(8,128)(2,1)S(1)} %get-tuple-element.109), channel_id=1, source_target_pairs={{0,8},{4,12},{8,16},{12,20},{16,24},{20,28},{24,0},{28,4},{1,9},{5... | collective-permute-start | bytes 1376264 | tf_op jit(solution)/shard_map/ppermute | solution.py:210
  36.5 32.6 %collective-permute-start.11 = (bf16[512,512]{1,0:T(8,128)(2,1)S(1)}, bf16[512,512]{1,0:T(8,128)(2,1)S(1)}, u32[]{:S(2)}, u32[]{:S(2)}) collective-permute-start(bf16[512,512]{1,0:T(8,128)(2,1)S(1)} %get-tuple-element.144.refs_0_), channel_id=1, source_target_pairs={{0,24},{4,28},{8,0},{12,4},{16,8},{20,12},{24,16},{28,20},{1,25},{... | collective-permute-start | bytes 1572872 | tf_op jit(solution)/shard_map/ppermute | solution.py:210
  40.8 11.3 %collective-permute-start.6 = (bf16[448,512]{1,0:T(8,128)(2,1)S(1)}, bf16[448,512]{1,0:T(8,128)(2,1)S(1)}, u32[]{:S(2)}, u32[]{:S(2)}) collective-permute-start(bf16[448,512]{1,0:T(8,128)(2,1)S(1)} %collective-permute-done.5.refs_0_), channel_id=1, source_target_pairs={{0,4},{4,0},{8,12},{12,8},{16,20},{20,16},{24,28},{28,24},{1,5},{5... | collective-permute-start | bytes 1376264 | tf_op jit(solution)/shard_map/ppermute | solution.py:214
  45.9 11.2 %collective-permute-start.4 = (bf16[448,512]{1,0:T(8,128)(2,1)S(1)}, bf16[448,512]{1,0:T(8,128)(2,1)S(1)}, u32[]{:S(2)}, u32[]{:S(2)}) collective-permute-start(bf16[448,512]{1,0:T(8,128)(2,1)S(1)} %collective-permute-done.3.refs_0_), channel_id=1, source_target_pairs={{0,4},{4,0},{8,12},{12,8},{16,20},{20,16},{24,28},{28,24},{1,5},{5... | collective-permute-start | bytes 1376264 | tf_op jit(solution)/shard_map/ppermute | solution.py:214
  47.4 23.3 %collective-permute-start.12 = (bf16[512,512]{1,0:T(8,128)(2,1)S(1)}, bf16[512,512]{1,0:T(8,128)(2,1)S(1)}, u32[]{:S(2)}, u32[]{:S(2)}) collective-permute-start(bf16[512,512]{1,0:T(8,128)(2,1)S(1)} %get-tuple-element.144.refs_0_), channel_id=1, source_target_pairs={{0,8},{4,12},{8,16},{12,20},{16,24},{20,28},{24,0},{28,4},{1,9},{5... | collective-permute-start | bytes 1572872 | tf_op jit(solution)/shard_map/ppermute | solution.py:210
  53.4 8.8 %copy-start.3 = (bf16[2,128,512]{2,1,0:T(8,128)(2,1)S(1)}, bf16[2,128,512]{2,1,0:T(8,128)(2,1)}, u32[]{:S(2)}) copy-start(bf16[2,128,512]{2,1,0:T(8,128)(2,1)} %queries_ref.1) | copy-start | bytes 786436
  53.4 8.8 %copy-start.4 = (bf16[2,128,512]{2,1,0:T(8,128)(2,1)S(1)}, bf16[2,128,512]{2,1,0:T(8,128)(2,1)}, u32[]{:S(2)}) copy-start(bf16[2,128,512]{2,1,0:T(8,128)(2,1)} %upstream_ref.1) | copy-start | bytes 786436
  53.4 8.8 %copy-start.6 = (f32[512]{0:T(512)S(1)}, f32[512]{0:T(512)}, u32[]{:S(2)}) copy-start(f32[512]{0:T(512)} %param.12) | copy-start | bytes 6148
  62.8 4.6 %collective-permute-start.10 = (f32[8,128]{1,0:T(8,128)S(1)}, f32[8,128]{1,0:T(8,128)S(1)}, u32[]{:S(2)}, u32[]{:S(2)}) collective-permute-start(f32[8,128]{1,0:T(8,128)S(1)} %get-tuple-element.138.refs_0_), channel_id=1, source_target_pairs={{0,3},{1,0},{2,1},{3,2},{4,7},{5,4},{6,5},{7,6},{8,11},{9,8},{10,9... | collective-permute-start | bytes 12296 | tf_op jit(solution)/shard_map/ppermute | solution.py:224
  62.8 4.6 %collective-permute-start.8 = (f32[8,128]{1,0:T(8,128)S(1)}, f32[8,128]{1,0:T(8,128)S(1)}, u32[]{:S(2)}, u32[]{:S(2)}) collective-permute-start(f32[8,128]{1,0:T(8,128)S(1)} %get-tuple-element.138.refs_0_), channel_id=1, source_target_pairs={{0,1},{1,2},{2,3},{3,0},{4,5},{5,6},{6,7},{7,4},{8,9},{9,10},{10,1... | collective-permute-start | bytes 12296 | tf_op jit(solution)/shard_map/ppermute | solution.py:224
  63.3 4.1 %collective-permute-start.9 = (f32[8,128]{1,0:T(8,128)S(1)}, f32[8,128]{1,0:T(8,128)S(1)}, u32[]{:S(2)}, u32[]{:S(2)}) collective-permute-start(f32[8,128]{1,0:T(8,128)S(1)} %get-tuple-element.138.refs_0_), channel_id=1, source_target_pairs={{0,2},{1,3},{2,0},{3,1},{4,6},{5,7},{6,4},{7,5},{8,10},{9,11},{10,... | collective-permute-start | bytes 12296 | tf_op jit(solution)/shard_map/ppermute | solution.py:224
  69.1 22.5 %collective-permute-start.17 = (bf16[4,3,64,512]{3,2,1,0:T(8,128)(2,1)S(1)}, bf16[4,3,64,512]{3,2,1,0:T(8,128)(2,1)S(1)}, u32[]{:S(2)}, u32[]{:S(2)}) collective-permute-start(bf16[4,3,64,512]{3,2,1,0:T(8,128)(2,1)S(1)} %get-tuple-element.188), channel_id=1, source_target_pairs={{0,4},{4,0},{8,12},{12,8},{16,20},{20,16},{24,28},{28,24},{1,5},{5... | collective-permute-start | bytes 2359304 | tf_op jit(solution)/shard_map/ppermute | solution.py:214
  70.6 16.1 %collective-permute-start.13 = (bf16[512,512]{1,0:T(8,128)(2,1)S(1)}, bf16[512,512]{1,0:T(8,128)(2,1)S(1)}, u32[]{:S(2)}, u32[]{:S(2)}) collective-permute-start(bf16[512,512]{1,0:T(8,128)(2,1)S(1)} %collective-permute-done.12.refs_1_), channel_id=1, source_target_pairs={{0,8},{4,12},{8,16},{12,20},{16,24},{20,28},{24,0},{28,4},{1,9},{5... | collective-permute-start | bytes 1572872 | tf_op jit(solution)/shard_map/ppermute | solution.py:210
  76.9 1.0 copy-start.1
  88.2 3.4 %collective-permute-start.14 = (f32[8,1024]{1,0:T(8,128)S(1)}, f32[8,1024]{1,0:T(8,128)S(1)}, u32[]{:S(2)}, u32[]{:S(2)}) collective-permute-start(f32[8,1024]{1,0:T(8,128)S(1)} %get-tuple-element.161.refs_0_), channel_id=1, source_target_pairs={{0,1},{1,2},{2,3},{3,0},{4,5},{5,6},{6,7},{7,4},{8,9},{9,10},{10,1... | collective-permute-start | bytes 98312 | tf_op jit(solution)/shard_map/ppermute | solution.py:224
  91.8 20.7 %collective-permute-start.18 = (bf16[3,64,512]{2,1,0:T(8,128)(2,1)S(1)}, bf16[3,64,512]{2,1,0:T(8,128)(2,1)S(1)}, u32[]{:S(2)}, u32[]{:S(2)}) collective-permute-start(bf16[3,64,512]{2,1,0:T(8,128)(2,1)S(1)} %get-tuple-element.190), channel_id=1, source_target_pairs={{0,8},{4,12},{8,16},{12,20},{16,24},{20,28},{24,0},{28,4},{1,9},{5... | collective-permute-start | bytes 589832 | tf_op jit(solution)/shard_map/ppermute | solution.py:210
  91.9 20.6 %collective-permute-start.19 = (bf16[3,64,512]{2,1,0:T(8,128)(2,1)S(1)}, bf16[3,64,512]{2,1,0:T(8,128)(2,1)S(1)}, u32[]{:S(2)}, u32[]{:S(2)}) collective-permute-start(bf16[3,64,512]{2,1,0:T(8,128)(2,1)S(1)} %get-tuple-element.191), channel_id=1, source_target_pairs={{0,16},{4,20},{8,24},{12,28},{16,0},{20,4},{24,8},{28,12},{1,17},{... | collective-permute-start | bytes 589832 | tf_op jit(solution)/shard_map/ppermute | solution.py:210
  94.2 18.3 %collective-permute-start.20 = (bf16[3,64,512]{2,1,0:T(8,128)(2,1)S(1)}, bf16[3,64,512]{2,1,0:T(8,128)(2,1)S(1)}, u32[]{:S(2)}, u32[]{:S(2)}) collective-permute-start(bf16[3,64,512]{2,1,0:T(8,128)(2,1)S(1)} %get-tuple-element.192), channel_id=1, source_target_pairs={{0,24},{4,28},{8,0},{12,4},{16,8},{20,12},{24,16},{28,20},{1,25},{... | collective-permute-start | bytes 589832 | tf_op jit(solution)/shard_map/ppermute | solution.py:210
  95.8 3.9 %collective-permute-start.15 = (f32[8,1024]{1,0:T(8,128)S(1)}, f32[8,1024]{1,0:T(8,128)S(1)}, u32[]{:S(2)}, u32[]{:S(2)}) collective-permute-start(f32[8,1024]{1,0:T(8,128)S(1)} %get-tuple-element.161.refs_0_), channel_id=1, source_target_pairs={{0,2},{1,3},{2,0},{3,1},{4,6},{5,7},{6,4},{7,5},{8,10},{9,11},{10,... | collective-permute-start | bytes 98312 | tf_op jit(solution)/shard_map/ppermute | solution.py:224
  97.2 2.5 %collective-permute-start.16 = (f32[8,1024]{1,0:T(8,128)S(1)}, f32[8,1024]{1,0:T(8,128)S(1)}, u32[]{:S(2)}, u32[]{:S(2)}) collective-permute-start(f32[8,1024]{1,0:T(8,128)S(1)} %get-tuple-element.161.refs_0_), channel_id=1, source_target_pairs={{0,3},{1,0},{2,1},{3,2},{4,7},{5,4},{6,5},{7,6},{8,11},{9,8},{10,9... | collective-permute-start | bytes 98312 | tf_op jit(solution)/shard_map/ppermute | solution.py:224
  99.7 4.4 %copy-start.2 = (bf16[2,512,512]{2,1,0:T(8,128)(2,1)S(1)}, bf16[2,512,512]{2,1,0:T(8,128)(2,1)}, u32[]{:S(2)}) copy-start(bf16[2,512,512]{2,1,0:T(8,128)(2,1)} %copy-done.1) | copy-start | bytes 3145732

commit v5 on v4

--- a/solution.py
+++ b/solution.py
@@ -288,8 +288,8 @@
 
 def fast_kernel(layout, ring, me_ref, *refs):
     pieces, refs = refs[:len(layout)], refs[len(layout) + 5:]
-    (wg, wu, wd, keys, values, gk_ref, uk_ref, back_ref, totals_g, totals_u, totals_d) = refs[:11]
-    d_gate, d_up, hidden, sems = refs[11:]
+    wg, wu, wd, keys, values, by_gate, by_up, by_lower, by_upper = refs[:9]
+    totals_g, totals_u, totals_d, pk, rk, hk, d_gate, d_up, hidden, sems = refs[9:]
     move(place_rows(layout, ring, me_ref[0], pieces, (wg, wu, wd, keys, values)), sems)
     for part in chunks_of(keys.shape[0]):
         gk = product(keys[part], wg[...])
@@ -298,30 +298,45 @@
         sigma = jax.nn.sigmoid(gk)
         active = gk * sigma
         slope = sigma * (1.0 + gk * (1.0 - sigma))
+        curve = sigma * (1.0 - sigma) * (2.0 + gk * (1.0 - 2.0 * sigma))
+        along = uk * slope
         hidden[part] = (active * uk).astype(bf16)
-        d_gate[part] = (back * uk * slope).astype(bf16)
+        d_gate[part] = (back * along).astype(bf16)
         d_up[part] = (back * active).astype(bf16)
-        gk_ref[part], uk_ref[part], back_ref[part] = gk, uk, back
+        by_gate[part], by_up[part] = along, active
+        by_lower[part], by_upper[part] = back * uk * curve, back * slope
     totals_g[...] = across(keys[...], d_gate[...])
     totals_u[...] = across(keys[...], d_up[...])
     totals_d[...] = -across(hidden[...], values[...])
-
-
-def schulz_kernel(total_ref, weight, xs, grams, blends, following_ref, root_ref):
-    total = total_ref[...]
-    root = jnp.sqrt(jnp.sum(total * total, keepdims=True))
-    root_ref[...] = jnp.broadcast_to(root, root_ref.shape)
-    xs[0] = (total / (root + fro_eps)).astype(bf16)
+    own = pk.shape[0]
+    pk[...], rk[...], hk[...] = d_gate[:own], d_up[:own], hidden[:own]
+
+
+def schulz_kernel(count, *refs):
+    totals, weights = refs[:count], refs[count:2 * count]
+    outs = [refs[i:i + 5] for i in range(2 * count, 7 * count, 5)]
+    for total_ref, (xs, _, _, _, root_ref) in zip(totals, outs):
+        total = total_ref[...]
+        root = jnp.sqrt(jnp.sum(total * total, keepdims=True))
+        root_ref[...] = jnp.broadcast_to(root, root_ref.shape)
+        xs[0] = (total / (root + fro_eps)).astype(bf16)
     for sweep in range(NS_STEPS):
-        current = xs[sweep]
-        gram = against(current, current).astype(bf16)
-        blend = (cube_coef * gram.astype(f32) + fifth_coef * product(gram, gram)).astype(bf16)
-        following = (lin_coef * current.astype(f32) + product(blend, current)).astype(bf16)
-        grams[sweep] = gram
-        blends[sweep] = blend
-        if sweep + 1 < NS_STEPS:
-            xs[sweep + 1] = following
-    following_ref[...] = (weight[...].astype(f32) - following.astype(f32)).astype(bf16)
+        for xs, grams, _, _, _ in outs:
+            grams[sweep] = against(xs[sweep], xs[sweep]).astype(bf16)
+        for _, grams, blends, _, _ in outs:
+            gram = grams[sweep]
+            blends[sweep] = (
+                cube_coef * gram.astype(f32) + fifth_coef * product(gram, gram)
+            ).astype(bf16)
+        for weight, (xs, _, blends, following_ref, _) in zip(weights, outs):
+            current = xs[sweep]
+            following = (
+                lin_coef * current.astype(f32) + product(blends[sweep], current)
+            ).astype(bf16)
+            if sweep + 1 < NS_STEPS:
+                xs[sweep + 1] = following
+            else:
+                following_ref[...] = (weight[...].astype(f32) - following.astype(f32)).astype(bf16)
 
 
 def row_sums(columns, tokens):
@@ -331,12 +346,14 @@
 
 
 def forward_part(
-    parts, queries, upstream, gain, wg, wu, wd, gq_ref, uq_ref, hidden_ref, out_ref, stats
+    parts, queries, upstream, gain, wg, wu, wd, by_gate, by_up, hidden_ref, out_ref, stats
 ):
     for part in parts:
         gq = product(queries[part], wg[...])
         uq = product(queries[part], wu[...])
-        hidden = (gq * jax.nn.sigmoid(gq) * uq).astype(bf16)
+        sigma = jax.nn.sigmoid(gq)
+        active = gq * sigma
+        hidden = (active * uq).astype(bf16)
         output = product(hidden, wd[...])
         weighted = gain[...] * upstream[part].astype(f32)
         sums = (
@@ -344,11 +361,12 @@
             jnp.sum(weighted * output, axis=1, keepdims=True),
         )
         stats[:, part] = row_sums(sums, output.shape[0])
-        gq_ref[part], uq_ref[part], hidden_ref[part], out_ref[part] = gq, uq, hidden, output
+        by_gate[part], by_up[part] = uq * sigma * (1.0 + gq * (1.0 - sigma)), active
+        hidden_ref[part], out_ref[part] = hidden, output
 
 
 def backward_part(
-    width, queries, upstream, gain, wg, wu, wd, gq_ref, uq_ref, hidden, out_ref, sums,
+    width, queries, upstream, gain, wg, wu, wd, by_gate, by_up, hidden, out_ref, sums,
     grad_ref, d_gate, d_up, d_out, own,
 ):
     for part in chunks_of(queries.shape[0]):
@@ -363,10 +381,8 @@
         weighted = gain[...] * upstream[part].astype(f32)
         d_output = (inverse * weighted - out_ref[part] * pull).astype(bf16)
         back = against(d_output, wd[...])
-        gq, uq = gq_ref[part], uq_ref[part]
-        sigma = jax.nn.sigmoid(gq)
-        d_gate[part] = (back * uq * sigma * (1.0 + gq * (1.0 - sigma))).astype(bf16)
-        d_up[part] = (back * gq * sigma).astype(bf16)
+        d_gate[part] = (back * by_gate[part]).astype(bf16)
+        d_up[part] = (back * by_up[part]).astype(bf16)
         d_out[part] = d_output
     grad_ref[...] = (
         against(d_gate[:own], wg[...]) + against(d_up[:own], wu[...])
@@ -474,34 +490,24 @@
 
 
 def last_kernel(
-    own, scale, me_ref, keys, values, wg, wu, wd, gk_ref, uk_ref, back_ref,
+    own, scale, me_ref, keys, values, wg, wu, wd, by_gate, by_up, by_lower, by_upper, pk, rk, hk,
     cot_g, cot_u, cot_d, rate_g, rate_u, rate_d, *refs,
 ):
-    count = len(refs) - 13
+    count = len(refs) - 10
     firsts = refs[:count]
     grad_keys, grad_values, grad_g, grad_u, grad_d = refs[count:count + 5]
-    lower, upper, d_back, pk, rk, hk, keys_t, back_t = refs[count + 5:]
+    lower, upper, d_back, keys_t, back_t = refs[count + 5:]
     for part in chunks_of(keys.shape[0]):
-        gk, uk, back = gk_ref[part], uk_ref[part], back_ref[part]
-        sigma = jax.nn.sigmoid(gk)
-        active = gk * sigma
-        slope = sigma * (1.0 + gk * (1.0 - sigma))
-        curve = sigma * (1.0 - sigma) * (2.0 + gk * (1.0 - 2.0 * sigma))
+        along, active, bent = by_gate[part], by_up[part], by_upper[part]
         ek = product(keys[part], cot_g[...])
         fk = product(keys[part], cot_u[...])
         hk_part = -against(values[part], cot_d[...])
-        d_back_part = (ek * uk * slope + fk * active).astype(bf16)
+        d_back_part = (ek * along + fk * active).astype(bf16)
         d_back[part] = d_back_part
         back_t[:, part] = d_back_part.T
         keys_t[:, part] = keys[part].T
-        upper[part] = (ek * back * slope + hk_part * active).astype(bf16)
-        lower[part] = (
-            ek * back * uk * curve + fk * back * slope + hk_part * uk * slope
-        ).astype(bf16)
-        if part.start == 0:
-            pk[...] = (back * uk * slope).astype(bf16)[:own]
-            rk[...] = (back * active).astype(bf16)[:own]
-            hk[...] = (active * uk).astype(bf16)[:own]
+        upper[part] = (ek * bent + hk_part * active).astype(bf16)
+        lower[part] = (ek * by_lower[part] + fk * bent + hk_part * along).astype(bf16)
     grad_keys[...] = (
         against(pk[...], cot_g[...])
         + against(rk[...], cot_u[...])
@@ -595,8 +601,8 @@
     crossed = swap(packed, ring)
     crossed_second = swap(packed_second, ring)
     up = shift(packed, ring, 1)
-    state, carried = place((packed, crossed), ((0, 0, 0), (0, 1, 1)), carry=(packed,))
-    down = shift(carried, ring, -1)
+    down = shift(tie(packed, crossed), ring, -1)
+    state, _ = place((packed, crossed), ((0, 0, 0), (0, 1, 1)))
     crossed_up = swap(up, ring)
     crossed_down = swap(down, ring)
     state, carried = place((up,), ((-1, 0, 2),), state, (up,), (crossed_second,))
@@ -607,23 +613,23 @@
     )
     state, _ = place((far, crossed_down), ((-2, 0, 5), (1, 1, 6)), state)
     layout = ((-2, 1, 7),)
-    (wg, wu, wd, all_keys, all_values, gk, uk, back, *totals) = pl.pallas_call(
+    (wg, wu, wd, all_keys, all_values, *rest) = pl.pallas_call(
         functools.partial(fast_kernel, layout, ring),
         out_shape=(
             narrow, narrow, narrow, S((tokens, depth), bf16), S((tokens, depth), bf16),
-            S((tokens, hidden), f32), S((tokens, hidden), f32), S((tokens, hidden), f32),
-            wide, wide, wide,
+            *[S((tokens, hidden), f32)] * 4, wide, wide, wide, *[S((own, hidden), bf16)] * 3,
         ),
         in_specs=[smem(), anywhere()] + [anywhere()] * 5,
-        out_specs=[vmem()] * 11,
+        out_specs=[vmem()] * 15,
         scratch_shapes=[pltpu.VMEM((tokens, hidden), bf16)] * 3 + [pltpu.SemaphoreType.DMA((5,))],
         input_output_aliases={2 + index: index for index in range(5)},
         cost_estimate=light(),
         compiler_params=params(24),
     )(me_ref, crossed_far, *state)
+    slopes, totals, own_rows = rest[:4], rest[4:7], rest[7:]
 
     up, down = shift(pair, ring, 1), shift(pair, ring, -1)
-    pairs = [pair, up, down, shift(tie(up, totals[0]), ring, 1)]
+    pairs = [pair, up, down, shift(tie(down, totals[0]), ring, -1)]
 
     queries0, upstream0, gq0, uq0, hidden0, out0, stats0 = pl.pallas_call(
         first_forward_kernel,
@@ -638,21 +644,23 @@
         compiler_params=params(16),
     )(queries, upstream, gain, wg, wu, wd)
 
-    def schulz(which, total):
-        return pl.pallas_call(
-            schulz_kernel,
+    def schulz(begin, *sums):
+        count = len(sums)
+        out = pl.pallas_call(
+            functools.partial(schulz_kernel, count),
             out_shape=(
                 S((NS_STEPS, *matrix), bf16), S((NS_STEPS, *matrix), bf16),
                 S((NS_STEPS, *matrix), bf16), narrow, S((8, 128), f32),
-            ),
-            in_specs=[vmem()] * 2,
-            out_specs=[vmem()] * 5,
+            ) * count,
+            in_specs=[vmem()] * (2 * count),
+            out_specs=[vmem()] * (5 * count),
             cost_estimate=light(),
             compiler_params=params(16),
-        )(total, (wg, wu, wd)[which])
+        )(*sums, *(wg, wu, wd)[begin:begin + count])
+        return [out[i:i + 5] for i in range(0, 5 * count, 5)]
 
     terms0 = head_terms(stats0)
-    first_weight = schulz(0, totals[0])
+    first_weight = schulz(0, totals[0])[0]
     terms0[0] = tie(terms0[0], first_weight[4])
     grad_first, kept, sent = pl.pallas_call(
         functools.partial(first_backward_kernel, width, ring),
@@ -667,7 +675,7 @@
         compiler_params=params(20),
     )(me_ref, queries0, upstream0, gain, wg, wu, wd, gq0, uq0, hidden0, out0, *terms0)
 
-    forward = [first_weight, schulz(1, totals[1]), schulz(2, tie(totals[2], down))]
+    forward = [first_weight, *schulz(1, *totals[1:])]
 
     seconds = [forward[which][3] for which in range(3)]
     def second_forward(first, arrived, state=()):
@@ -684,7 +692,7 @@
             scratch_shapes=[pltpu.SemaphoreType.DMA((4 * len(arrived),))],
             input_output_aliases={start + index: index for index in range(len(state))},
             cost_estimate=light(),
-            compiler_params=params(24),
+            compiler_params=params(14),
         )(gain, *seconds, *arrived, *state)
 
     state = second_forward(0, pairs[:-1])
@@ -700,7 +708,7 @@
         in_specs=[smem()] + [vmem()] * 2,
         out_specs=[vmem()] * ring,
         compiler_params=params(12),
-    )(me_ref, tie(kept, terms[1]), swap(tie(sent, down), ring))
+    )(me_ref, tie(kept, *terms[1:]), swap(tie(sent, up), ring))
     firsts = [summed[0]] + [shift(summed[step], ring, step) for step in range(1, ring)]
 
     grad_queries, *rates = pl.pallas_call(
@@ -733,22 +741,19 @@
             S((own, depth), bf16), S((own, depth), bf16),
             S((1, rows, hidden), f32), S((1, rows, hidden), f32), S((1, rows, hidden), f32),
         ),
-        in_specs=[smem()] + [vmem()] * (14 + len(firsts)),
+        in_specs=[smem()] + [vmem()] * (18 + len(firsts)),
         out_specs=[vmem()] * 5,
         scratch_shapes=[
             pltpu.VMEM((tokens, hidden), bf16),
             pltpu.VMEM((tokens, hidden), bf16),
             pltpu.VMEM((tokens, hidden), bf16),
-            pltpu.VMEM((own, hidden), bf16),
-            pltpu.VMEM((own, hidden), bf16),
-            pltpu.VMEM((own, hidden), bf16),
             pltpu.VMEM((depth, tokens), bf16),
             pltpu.VMEM((hidden, tokens), bf16),
         ],
         cost_estimate=light(),
         compiler_params=params(24),
     )(
-        me_ref, all_keys, all_values, wg, wu, wd, gk, uk, back, *cots, *rates, *firsts,
+        me_ref, all_keys, all_values, wg, wu, wd, *slopes, *own_rows, *cots, *rates, *firsts,
     ))
 
 

time: 119 us -> 116 us (0.975); the launches traced: 119 us -> 114 us
  waiting for transfers between devices: 39.1 us -> 35.6 us
  Pallas kernels: 47 us -> 45.4 us
    ppermute x6, waiting for transfers between devices: 5.81 us -> 1.6 us  [head_terms(): lax.ppermute(stats, 'head', [(i, (i + k) % heads) for i in range(heads)])]
    ppermute x6, waiting for transfers between devices: 16.3 us -> 18.5 us  [swap(): return lax.ppermute(array, 'tok', [(i, i ^ 1) for i in range(2 * ring)])]
    ppermute x6, starting transfers between devices: 3.53 us -> 5.08 us  [head_terms(): lax.ppermute(stats, 'head', [(i, (i + k) % heads) for i in range(heads)])]
    ppermute x9, waiting for transfers between devices: 17 us -> 15.5 us  [shift(): return lax.ppermute(array, 'tok', pairs)]
    ppermute x9, starting transfers between devices: 16.9 us -> 15.5 us  [shift(): return lax.ppermute(array, 'tok', pairs)]
    pallas_call x1, Pallas kernels: 6.51 us -> 5.25 us  [gather_tokens(): pl.pallas_call(functools.partial(last_kernel, own, scale), out_shape=(S((...]
    pallas_call x3 -> x2, Pallas kernels: 7.61 us -> 6.69 us  [schulz(): pl.pallas_call(functools.partial(schulz_kernel, count), out_shape=(S((NS_...]
  transfers between devices with their start and end apart: 21 -> 21, of which waited for: 8 -> 10; matrix products, arithmetic and copies ran while one was open for 0% -> 0% of each run, Pallas kernels for 32% -> 33%
where the time goes in v5:
time: 116 us; the launch traced here: 114 us
  Pallas kernels  45.4 us (39%)
  waiting for transfers between devices  35.6 us (31%)
  starting transfers between devices  31 us (27%)
    ppermute x6, waiting for transfers between devices, swap(): return lax.ppermute(array, 'tok', [(i, i ^ 1) for i in range(2 * ring)])  18.5 us
    ppermute x9, starting transfers between devices, shift(): return lax.ppermute(array, 'tok', pairs)  15.5 us
    ppermute x9, waiting for transfers between devices, shift(): return lax.ppermute(array, 'tok', pairs)  15.5 us
    ppermute x6, starting transfers between devices, swap(): return lax.ppermute(array, 'tok', [(i, i ^ 1) for i in range(2 * ring)])  10.4 us
    pallas_call x1, Pallas kernels, gather_tokens(): pl.pallas_call(schulz_back_kernel, out_shape=(narrow,) * 3, in_specs=[vme...  8.33 us
    pallas_call x2, Pallas kernels, schulz(): pl.pallas_call(functools.partial(schulz_kernel, count), out_shape=(S((NS_...  6.69 us
    pallas_call x1, Pallas kernels, gather_tokens(): pl.pallas_call(functools.partial(fast_kernel, layout, ring), out_shape=(n...  6 us
    pallas_call x2, Pallas kernels, second_forward(): pl.pallas_call(functools.partial(second_forward_kernel, first, len(arrive...  5.85 us
  transfers between devices with their start and end apart: 21, of which 10 were waited for; matrix products, arithmetic and copies ran while one was open for 0% of the time, Pallas kernels for 33%

profile of v5, /device:TPU:0, one launch (start us, length us, event | category | flops | bytes accessed | tf_op | source)
XLA Modules:
  0.0 114.0 jit_solution(10708704157427954351)
XLA Ops:
  0.6 2.1 %shard_map.127 = (bf16[448,512]{1,0:T(8,128)(2,1)}, bf16[256,512]{1,0:T(8,128)(2,1)}) custom-call(bf16[1,64,512]{2,1,0:T(8,128)(2,1)} %gate.1, bf16[1,64,512]{2,1,0:T(8,128)(2,1)} %up.1, bf16[1,64,512]{2,1,0:T(8,128)(2,1)} %down.1, bf16[128,512]{1,0:T(8,128)(2,1)} %keys.1, bf16[128,512]{1,0:T(8,128)(2,1)} %values.1, bf16[2,128,512]{2,1,0:T(8,128)(2,1)} %queries_ref.1, ...), custom_call_target="tpu_custom_call" | custom-call | tf_op jit(solution)/shard_map/pallas_call | solution.py:572
  2.8 3.0 %collective-permute-start.2 = (bf16[448,512]{1,0:T(8,128)(2,1)}, bf16[448,512]{1,0:T(8,128)(2,1)S(1)}, u32[]{:S(2)}, u32[]{:S(2)}) collective-permute-start(bf16[448,512]{1,0:T(8,128)(2,1)} %get-tuple-element.113.refs_0_), channel_id=1, source_target_pairs={{0,4},{4,0},{8,12},{12,8},{16,20},{20,16},{24,28},{28,24},{1,5},{5... | collective-permute-start | bytes 1376264 | tf_op jit(solution)/shard_map/ppermute | solution.py:214
  5.8 1.6 %collective-permute-start = (bf16[448,512]{1,0:T(8,128)(2,1)}, bf16[448,512]{1,0:T(8,128)(2,1)S(1)}, u32[]{:S(2)}, u32[]{:S(2)}) collective-permute-start(bf16[448,512]{1,0:T(8,128)(2,1)} %get-tuple-element.113.refs_0_), channel_id=1, source_target_pairs={{0,8},{4,12},{8,16},{12,20},{16,24},{20,28},{24,0},{28,4},{1,9},{5... | collective-permute-start | bytes 1376264 | tf_op jit(solution)/shard_map/ppermute | solution.py:210
  7.9 9.4 %collective-permute-done.2.refs_1_ = bf16[448,512]{1,0:T(8,128)(2,1)S(1)} collective-permute-done((bf16[448,512]{1,0:T(8,128)(2,1)}, bf16[448,512]{1,0:T(8,128)(2,1)S(1)}, u32[]{:S(2)}, u32[]{:S(2)}) %collective-permute-start.2) | collective-permute-done | bytes 458784 | tf_op jit(solution)/shard_map/ppermute | solution.py:214
  17.3 4.2 %collective-permute-start.5 = (bf16[448,512]{1,0:T(8,128)(2,1)}, bf16[448,512]{1,0:T(8,128)(2,1)S(1)}, u32[]{:S(2)}, u32[]{:S(2)}) collective-permute-start(bf16[448,512]{1,0:T(8,128)(2,1)} %get-tuple-element.113.refs_0_), channel_id=1, source_target_pairs={{0,24},{4,28},{8,0},{12,4},{16,8},{20,12},{24,16},{28,20},{1,25},{... | collective-permute-start | bytes 1376264 | tf_op jit(solution)/shard_map/ppermute | solution.py:210
  21.5 1.5 %collective-permute-start.7 = (bf16[448,512]{1,0:T(8,128)(2,1)S(1)}, bf16[448,512]{1,0:T(8,128)(2,1)S(1)}, u32[]{:S(2)}, u32[]{:S(2)}) collective-permute-start(bf16[448,512]{1,0:T(8,128)(2,1)S(1)} %collective-permute-done.refs_0_.refs_1_), channel_id=1, source_target_pairs={{0,4},{4,0},{8,12},{12,8},{16,20},{20,16},{24,28},{28,24},{1,5},{5... | collective-permute-start | bytes 1376264 | tf_op jit(solution)/shard_map/ppermute | solution.py:214
  24.0 1.3 %shard_map.128 = (bf16[512,512]{1,0:T(8,128)(2,1)S(1)}, bf16[512,512]{1,0:T(8,128)(2,1)S(1)}, bf16[512,512]{1,0:T(8,128)(2,1)S(1)}, bf16[1024,512]{1,0:T(8,128)(2,1)S(1)}, bf16[1024,512]{1,0:T(8,128)(2,1)S(1)}) custom-call(s32[1]{0:T(128)} %bitcast.me_ref, bf16[448,512]{1,0:T(8,128)(2,1)S(1)} %copy-done.2, bf16[448,512]{1,0:T(8,128)(2,1)S(1)} %collective-permute-done.2.refs_1_), custom_call_target="tpu_custom_call" | custom-call | flops 1 | bytes 1 | tf_op jit(solution)/shard_map/pallas_call | solution.py:589
  26.3 6.5 %collective-permute-done.5.refs_0_ = bf16[448,512]{1,0:T(8,128)(2,1)S(1)} collective-permute-done((bf16[448,512]{1,0:T(8,128)(2,1)}, bf16[448,512]{1,0:T(8,128)(2,1)S(1)}, u32[]{:S(2)}, u32[]{:S(2)}) %collective-permute-start.5) | collective-permute-done | bytes 458784 | tf_op jit(solution)/shard_map/ppermute | solution.py:210
  32.8 1.3 %shard_map.130 = (bf16[512,512]{1,0:T(8,128)(2,1)S(1)}, bf16[512,512]{1,0:T(8,128)(2,1)S(1)}, bf16[512,512]{1,0:T(8,128)(2,1)S(1)}, bf16[1024,512]{1,0:T(8,128)(...) custom-call(s32[1]{0:T(128)} %bitcast.me_ref, ...), custom_call_target="tpu_custom_call", output_to_operand_aliasing={{0}: (5, {}), {1}: (6, {}), {2}: (7, {}), {3}: (8, {}), {4}... | custom-call | flops 1 | bytes 1 | tf_op jit(solution)/shard_map/pallas_call | solution.py:589
  35.2 1.5 %collective-permute-start.6 = (bf16[448,512]{1,0:T(8,128)(2,1)S(1)}, bf16[448,512]{1,0:T(8,128)(2,1)S(1)}, u32[]{:S(2)}, u32[]{:S(2)}) collective-permute-start(bf16[448,512]{1,0:T(8,128)(2,1)S(1)} %collective-permute-done.5.refs_0_), channel_id=1, source_target_pairs={{0,4},{4,0},{8,12},{12,8},{16,20},{20,16},{24,28},{28,24},{1,5},{5... | collective-permute-start | bytes 1376264 | tf_op jit(solution)/shard_map/ppermute | solution.py:214
  36.6 5.9 %collective-permute-done.3.refs_0_ = bf16[448,512]{1,0:T(8,128)(2,1)S(1)} collective-permute-done((bf16[448,512]{1,0:T(8,128)(2,1)S(1)}, bf16[448,512]{1,0:T(8,128)(2,1)S(1)}, u32[]{:S(2)}, u32[]{:S(2)}) %collective-permute-start.3) | collective-permute-done | bytes 458784 | tf_op jit(solution)/shard_map/ppermute | solution.py:210
  42.6 2.3 %collective-permute-start.4 = (bf16[448,512]{1,0:T(8,128)(2,1)S(1)}, bf16[448,512]{1,0:T(8,128)(2,1)S(1)}, u32[]{:S(2)}, u32[]{:S(2)}) collective-permute-start(bf16[448,512]{1,0:T(8,128)(2,1)S(1)} %collective-permute-done.3.refs_0_), channel_id=1, source_target_pairs={{0,4},{4,0},{8,12},{12,8},{16,20},{20,16},{24,28},{28,24},{1,5},{5... | collective-permute-start | bytes 1376264 | tf_op jit(solution)/shard_map/ppermute | solution.py:214
  45.7 2.9 %collective-permute-done.6.refs_1_ = bf16[448,512]{1,0:T(8,128)(2,1)S(1)} collective-permute-done((bf16[448,512]{1,0:T(8,128)(2,1)S(1)}, bf16[448,512]{1,0:T(8,128)(2,1)S(1)}, u32[]{:S(2)}, u32[]{:S(2)}) %collective-permute-start.6) | collective-permute-done | bytes 458784 | tf_op jit(solution)/shard_map/ppermute | solution.py:214
  48.6 1.3 %shard_map.131 = (bf16[512,512]{1,0:T(8,128)(2,1)S(1)}, bf16[512,512]{1,0:T(8,128)(2,1)S(1)}, bf16[512,512]{1,0:T(8,128)(2,1)S(1)}, bf16[1024,512]{1,0:T(8,128)(2,1)S(1)}, bf16[1024,512]{1,0:T(8,128)(2,1)S(1)}) custom-call(s32[1]{0:T(128)} %bitcast.me_ref, ...), custom_call_target="tpu_custom_call", output_to_operand_aliasing={{0}: (3, {}), {1}: (4, {}), {2}: (5, {}), {3}: (6, {}), {4}... | custom-call | flops 1 | bytes 1 | tf_op jit(solution)/shard_map/pallas_call | solution.py:589
  49.9 6.2 %collective-permute-done.4.refs_0_ = bf16[448,512]{1,0:T(8,128)(2,1)S(1)} collective-permute-done((bf16[448,512]{1,0:T(8,128)(2,1)S(1)}, bf16[448,512]{1,0:T(8,128)(2,1)S(1)}, u32[]{:S(2)}, u32[]{:S(2)}) %collective-permute-start.4) | collective-permute-done | bytes 458784 | tf_op jit(solution)/shard_map/ppermute | solution.py:214
  56.1 6.0 %shard_map.132 = (bf16[512,512]{1,0:T(8,128)(2,1)S(1)}, bf16[512,512]{1,0:T(8,128)(2,1)S(1)}, bf16[512,512]{1,0:T(8,128)(2,1)S(1)}, bf16[1024,512]{1,0:T(8,128)(...) custom-call(s32[1]{0:T(128)} %bitcast.me_ref, ...), custom_call_target="tpu_custom_call", output_to_operand_aliasing={{0}: (2, {}), {1}: (3, {}), {2}: (4, {}), {3}: (5, {}), {4}... | custom-call | flops 1 | bytes 1 | tf_op jit(solution)/shard_map/pallas_call | solution.py:616
  63.3 1.5 %collective-permute-start.9 = (f32[8,128]{1,0:T(8,128)S(1)}, f32[8,128]{1,0:T(8,128)S(1)}, u32[]{:S(2)}, u32[]{:S(2)}) collective-permute-start(f32[8,128]{1,0:T(8,128)S(1)} %get-tuple-element.141.refs_0_), channel_id=1, source_target_pairs={{0,2},{1,3},{2,0},{3,1},{4,6},{5,7},{6,4},{7,5},{8,10},{9,11},{10,... | collective-permute-start | bytes 12296 | tf_op jit(solution)/shard_map/ppermute | solution.py:224
  64.8 2.5 %shard_map.134 = (bf16[2,512,512]{2,1,0:T(8,128)(2,1)S(1)}, bf16[2,512,512]{2,1,0:T(8,128)(2,1)S(1)}, bf16[2,512,512]{2,1,0:T(8,128)(2,1)S(1)}, bf16[512,512]{1,0:T(8,128)(2,1)S(1)}, f32[8,128]{1,0:T(8,128)S(1)}) custom-call(f32[512,512]{1,0:T(8,128)S(1)} %get-tuple-element.139.refs_0_.refs_3_, bf16[512,512]{1,0:T(8,128)(2,1)S(1)} %get-tuple-element.129.wg.refs_1_), custom_call_target="tpu_custom_call" | custom-call | flops 1 | bytes 1 | tf_op jit(solution)/shard_map/pallas_call | solution.py:649
  67.4 1.5 %shard_map.135 = (bf16[128,512]{1,0:T(8,128)(2,1)S(1)}, bf16[4,3,64,512]{3,2,1,0:T(8,128)(2,1)S(1)}, bf16[4,3,64,512]{3,2,1,0:T(8,128)(2,1)S(1)}) custom-call(s32[1]{0:T(128)} %bitcast.me_ref, bf16[128,512]{1,0:T(8,128)(2,1)S(1)} %get-tuple-element.132.queries, bf16[128,512]{1,0:T(8,128)(2,1)S(1)} %get-tuple-element.133.upstream, f32[1,512]{1,0:T(1,128)S(1)} %bitcast.3, ...), custom_call_target="tpu_custom_call" | custom-call | flops 1 | bytes 1 | tf_op jit(solution)/shard_map/pallas_call | solution.py:665
  68.9 1.6 %collective-permute-start.17 = (bf16[4,3,64,512]{3,2,1,0:T(8,128)(2,1)S(1)}, bf16[4,3,64,512]{3,2,1,0:T(8,128)(2,1)S(1)}, u32[]{:S(2)}, u32[]{:S(2)}) collective-permute-start(bf16[4,3,64,512]{3,2,1,0:T(8,128)(2,1)S(1)} %get-tuple-element.194), channel_id=1, source_target_pairs={{0,4},{4,0},{8,12},{12,8},{16,20},{20,16},{24,28},{28,24},{1,5},{5... | collective-permute-start | bytes 2359304 | tf_op jit(solution)/shard_map/ppermute | solution.py:214
  70.5 2.4 %collective-permute-start.12 = (bf16[512,512]{1,0:T(8,128)(2,1)S(1)}, bf16[512,512]{1,0:T(8,128)(2,1)S(1)}, u32[]{:S(2)}, u32[]{:S(2)}) collective-permute-start(bf16[512,512]{1,0:T(8,128)(2,1)S(1)} %collective-permute-done.11.refs_2_), channel_id=1, source_target_pairs={{0,24},{4,28},{8,0},{12,4},{16,8},{20,12},{24,16},{28,20},{1,25},{... | collective-permute-start | bytes 1572872 | tf_op jit(solution)/shard_map/ppermute | solution.py:210
  72.9 4.2 %shard_map.136 = (bf16[2,512,512]{2,1,0:T(8,128)(2,1)S(1)}, bf16[2,512,512]{2,1,0:T(8,128)(2,1)S(1)}, bf16[2,512,512]{2,1,0:T(8,128)(2,1)S(1)}, bf16[512,512]{1,...) custom-call(f32[512,512]{1,0:T(8,128)S(1)} %get-tuple-element.144.re, ...), custom_call_target="tpu_custom_call" | custom-call | flops 1 | bytes 1 | tf_op jit(solution)/shard_map/pallas_call | solution.py:649
  77.0 4.3 %shard_map.137 = (bf16[1024,512]{1,0:T(8,128)(2,1)S(1)}, bf16[1024,512]{1,0:T(8,128)(2,1)S(1)}, f32[1024,512]{1,0:T(8,128)S(1)}, f32[1024,512]{1,0:T(8,128)S(1)}...) custom-call(f32[1,512]{1,0:T(1,128)S(1)} %bitcast.4, ...), custom_call_target="tpu_custom_call" | custom-call | flops 1 | bytes 1 | tf_op jit(solution)/shard_map/pallas_call | solution.py:683
  81.3 2.6 %collective-permute-done.12.refs_0_ = bf16[512,512]{1,0:T(8,128)(2,1)S(1)} collective-permute-done((bf16[512,512]{1,0:T(8,128)(2,1)S(1)}, bf16[512,512]{1,0:T(8,128)(2,1)S(1)}, u32[]{:S(2)}, u32[]{:S(2)}) %collective-permute-start.12) | collective-permute-done | bytes 524320 | tf_op jit(solution)/shard_map/ppermute | solution.py:210
  83.9 1.6 %shard_map.138 = (bf16[1024,512]{1,0:T(8,128)(2,1)S(1)}, bf16[1024,512]{1,0:T(8,128)(2,1)S(1)}, f32[1024,512]{1,0:T(8,128)S(1)}, f32[1024,512]{1,0:T(8,128)S(1)}...) custom-call(f32[1,512]{1,0:T(1,128)S(1)} %bitcast.5, ...), custom_call_target="tpu_custom_call", output_to_operand_aliasing={{0}: (5, {}), {1}: (6, {}), {2}: (7, {}), {3}: (8, {}), {4}... | custom-call | flops 1 | bytes 1 | tf_op jit(solution)/shard_map/pallas_call | solution.py:683
  85.6 1.6 %collective-permute-start.15 = (f32[8,1024]{1,0:T(8,128)S(1)}, f32[8,1024]{1,0:T(8,128)S(1)}, u32[]{:S(2)}, u32[]{:S(2)}) collective-permute-start(f32[8,1024]{1,0:T(8,128)S(1)} %get-tuple-element.163.refs_0_), channel_id=1, source_target_pairs={{0,2},{1,3},{2,0},{3,1},{4,6},{5,7},{6,4},{7,5},{8,10},{9,11},{10,... | collective-permute-start | bytes 98312 | tf_op jit(solution)/shard_map/ppermute | solution.py:224
  87.2 1.4 %collective-permute-start.16 = (f32[8,1024]{1,0:T(8,128)S(1)}, f32[8,1024]{1,0:T(8,128)S(1)}, u32[]{:S(2)}, u32[]{:S(2)}) collective-permute-start(f32[8,1024]{1,0:T(8,128)S(1)} %get-tuple-element.163.refs_0_), channel_id=1, source_target_pairs={{0,3},{1,0},{2,1},{3,2},{4,7},{5,4},{6,5},{7,6},{8,11},{9,8},{10,9... | collective-permute-start | bytes 98312 | tf_op jit(solution)/shard_map/ppermute | solution.py:224
  90.3 1.6 %collective-permute-start.18 = (bf16[3,64,512]{2,1,0:T(8,128)(2,1)S(1)}, bf16[3,64,512]{2,1,0:T(8,128)(2,1)S(1)}, u32[]{:S(2)}, u32[]{:S(2)}) collective-permute-start(bf16[3,64,512]{2,1,0:T(8,128)(2,1)S(1)} %get-tuple-element.196), channel_id=1, source_target_pairs={{0,8},{4,12},{8,16},{12,20},{16,24},{20,28},{24,0},{28,4},{1,9},{5... | collective-permute-start | bytes 589832 | tf_op jit(solution)/shard_map/ppermute | solution.py:210
  92.0 3.2 %collective-permute-start.19 = (bf16[3,64,512]{2,1,0:T(8,128)(2,1)S(1)}, bf16[3,64,512]{2,1,0:T(8,128)(2,1)S(1)}, u32[]{:S(2)}, u32[]{:S(2)}) collective-permute-start(bf16[3,64,512]{2,1,0:T(8,128)(2,1)S(1)} %get-tuple-element.197), channel_id=1, source_target_pairs={{0,16},{4,20},{8,24},{12,28},{16,0},{20,4},{24,8},{28,12},{1,17},{... | collective-permute-start | bytes 589832 | tf_op jit(solution)/shard_map/ppermute | solution.py:210
  95.9 4.0 %shard_map.139 = (bf16[2,128,512]{2,1,0:T(8,128)(2,1)}, f32[512,512]{1,0:T(8,128)S(1)}, f32[512,512]{1,0:T(8,128)S(1)}, f32[512,512]{1,0:T(8,128)S(1)}) custom-call(bf16[128,512]{1,0:T(8,128)(2,1)S(1)} %get-tuple-element.142.grad_first, bf16[1024,512]{1,0:T(8,128)(2,1)S(1)} %get-tuple-element.157.queries, bf16[1024,512]{1,0:T(8,128)(2,1)S(1)} %get-tuple-element.158.upstream, ...), custom_call_target="tpu_custom_call" | custom-call | flops 1 | bytes 1 | tf_op jit(solution)/shard_map/pallas_call | solution.py:714
  99.9 8.3 %shard_map.140 = (bf16[512,512]{1,0:T(8,128)(2,1)S(1)}, bf16[512,512]{1,0:T(8,128)(2,1)S(1)}, bf16[512,512]{1,0:T(8,128)(2,1)S(1)}) custom-call(f32[512,512]{1,0:T(8,128)S(1)} %get-tuple-element.174.refs_0_.rate_g, f32[512,512]{1,0:T(8,128)S(1)} %get-tuple-element.175.refs_1_.rate_u, f32[512,512]{1,0:T(8,128)S(1)} %get-tuple-element.176.refs_2_.rate_d, ...), custom_call_target="tpu_custom_call" | custom-call | flops 1 | bytes 1 | tf_op jit(solution)/shard_map/pallas_call | solution.py:725
  108.7 5.2 %shard_map.142 = (bf16[128,512]{1,0:T(8,128)(2,1)}, bf16[128,512]{1,0:T(8,128)(2,1)}, f32[1,64,512]{2,1,0:T(8,128)}, f32[1,64,512]{2,1,0:T(8,128)}, f32[1,64,512]{2,1,0:T(8,128)}) custom-call(s32[1]{0:T(128)} %bitcast.me_ref, bf16[1024,512]{1,0:T(8,128)(2,1)S(1)} %get-tuple-element.165.keys, bf16[1024,512]{1,0:T(8,128)(2,1)S(1)} %get-tuple-element.166.values, ...), custom_call_target="tpu_custom_call" | custom-call | flops 1 | bytes 1 | tf_op jit(solution)/shard_map/pallas_call | solution.py:738
  (36 shorter events, 8.6 us)
Async XLA Ops:
  2.8 14.6 %collective-permute-start.2 = (bf16[448,512]{1,0:T(8,128)(2,1)}, bf16[448,512]{1,0:T(8,128)(2,1)S(1)}, u32[]{:S(2)}, u32[]{:S(2)}) collective-permute-start(bf16[448,512]{1,0:T(8,128)(2,1)} %get-tuple-element.113.refs_0_), channel_id=1, source_target_pairs={{0,4},{4,0},{8,12},{12,8},{16,20},{20,16},{24,28},{28,24},{1,5},{5... | collective-permute-start | bytes 1376264 | tf_op jit(solution)/shard_map/ppermute | solution.py:214
  5.8 15.7 %collective-permute-start = (bf16[448,512]{1,0:T(8,128)(2,1)}, bf16[448,512]{1,0:T(8,128)(2,1)S(1)}, u32[]{:S(2)}, u32[]{:S(2)}) collective-permute-start(bf16[448,512]{1,0:T(8,128)(2,1)} %get-tuple-element.113.refs_0_), channel_id=1, source_target_pairs={{0,8},{4,12},{8,16},{12,20},{16,24},{20,28},{24,0},{28,4},{1,9},{5... | collective-permute-start | bytes 1376264 | tf_op jit(solution)/shard_map/ppermute | solution.py:210
  7.3 17.9 %collective-permute-start.1 = (bf16[256,512]{1,0:T(8,128)(2,1)}, bf16[256,512]{1,0:T(8,128)(2,1)S(1)}, u32[]{:S(2)}, u32[]{:S(2)}) collective-permute-start(bf16[256,512]{1,0:T(8,128)(2,1)} %get-tuple-element.106.refs_2_), channel_id=1, source_target_pairs={{0,4},{4,0},{8,12},{12,8},{16,20},{20,16},{24,28},{28,24},{1,5},{5... | collective-permute-start | bytes 786440 | tf_op jit(solution)/shard_map/ppermute | solution.py:214
  17.3 15.5 %collective-permute-start.5 = (bf16[448,512]{1,0:T(8,128)(2,1)}, bf16[448,512]{1,0:T(8,128)(2,1)S(1)}, u32[]{:S(2)}, u32[]{:S(2)}) collective-permute-start(bf16[448,512]{1,0:T(8,128)(2,1)} %get-tuple-element.113.refs_0_), channel_id=1, source_target_pairs={{0,24},{4,28},{8,0},{12,4},{16,8},{20,12},{24,16},{28,20},{1,25},{... | collective-permute-start | bytes 1376264 | tf_op jit(solution)/shard_map/ppermute | solution.py:210
  21.5 11.3 %collective-permute-start.7 = (bf16[448,512]{1,0:T(8,128)(2,1)S(1)}, bf16[448,512]{1,0:T(8,128)(2,1)S(1)}, u32[]{:S(2)}, u32[]{:S(2)}) collective-permute-start(bf16[448,512]{1,0:T(8,128)(2,1)S(1)} %collective-permute-done.refs_0_.refs_1_), channel_id=1, source_target_pairs={{0,4},{4,0},{8,12},{12,8},{16,20},{20,16},{24,28},{28,24},{1,5},{5... | collective-permute-start | bytes 1376264 | tf_op jit(solution)/shard_map/ppermute | solution.py:214
  23.0 1.0 copy-start.2
  25.3 7.6 %copy-start.3 = (bf16[256,512]{1,0:T(8,128)(2,1)S(1)}, bf16[256,512]{1,0:T(8,128)(2,1)}, u32[]{:S(2)}) copy-start(bf16[256,512]{1,0:T(8,128)(2,1)} %get-tuple-element.106.refs_2_) | copy-start | bytes 786436
  26.2 16.3 %collective-permute-start.3 = (bf16[448,512]{1,0:T(8,128)(2,1)S(1)}, bf16[448,512]{1,0:T(8,128)(2,1)S(1)}, u32[]{:S(2)}, u32[]{:S(2)}) collective-permute-start(bf16[448,512]{1,0:T(8,128)(2,1)S(1)} %get-tuple-element.112), channel_id=1, source_target_pairs={{0,8},{4,12},{8,16},{12,20},{16,24},{20,28},{24,0},{28,4},{1,9},{5... | collective-permute-start | bytes 1376264 | tf_op jit(solution)/shard_map/ppermute | solution.py:210
  34.2 34.7 %collective-permute-start.13 = (bf16[512,512]{1,0:T(8,128)(2,1)S(1)}, bf16[512,512]{1,0:T(8,128)(2,1)S(1)}, u32[]{:S(2)}, u32[]{:S(2)}) collective-permute-start(bf16[512,512]{1,0:T(8,128)(2,1)S(1)} %get-tuple-element.148.refs_0_), channel_id=1, source_target_pairs={{0,8},{4,12},{8,16},{12,20},{16,24},{20,28},{24,0},{28,4},{1,9},{5... | collective-permute-start | bytes 1572872 | tf_op jit(solution)/shard_map/ppermute | solution.py:210
  35.2 13.5 %collective-permute-start.6 = (bf16[448,512]{1,0:T(8,128)(2,1)S(1)}, bf16[448,512]{1,0:T(8,128)(2,1)S(1)}, u32[]{:S(2)}, u32[]{:S(2)}) collective-permute-start(bf16[448,512]{1,0:T(8,128)(2,1)S(1)} %collective-permute-done.5.refs_0_), channel_id=1, source_target_pairs={{0,4},{4,0},{8,12},{12,8},{16,20},{20,16},{24,28},{28,24},{1,5},{5... | collective-permute-start | bytes 1376264 | tf_op jit(solution)/shard_map/ppermute | solution.py:214
  42.6 13.5 %collective-permute-start.4 = (bf16[448,512]{1,0:T(8,128)(2,1)S(1)}, bf16[448,512]{1,0:T(8,128)(2,1)S(1)}, u32[]{:S(2)}, u32[]{:S(2)}) collective-permute-start(bf16[448,512]{1,0:T(8,128)(2,1)S(1)} %collective-permute-done.3.refs_0_), channel_id=1, source_target_pairs={{0,4},{4,0},{8,12},{12,8},{16,20},{20,16},{24,28},{28,24},{1,5},{5... | collective-permute-start | bytes 1376264 | tf_op jit(solution)/shard_map/ppermute | solution.py:214
  44.9 25.6 %collective-permute-start.11 = (bf16[512,512]{1,0:T(8,128)(2,1)S(1)}, bf16[512,512]{1,0:T(8,128)(2,1)S(1)}, u32[]{:S(2)}, u32[]{:S(2)}) collective-permute-start(bf16[512,512]{1,0:T(8,128)(2,1)S(1)} %get-tuple-element.148.refs_0_), channel_id=1, source_target_pairs={{0,24},{4,28},{8,0},{12,4},{16,8},{20,12},{24,16},{28,20},{1,25},{... | collective-permute-start | bytes 1572872 | tf_op jit(solution)/shard_map/ppermute | solution.py:210
  49.9 12.2 %copy-start = (bf16[2,128,512]{2,1,0:T(8,128)(2,1)S(1)}, bf16[2,128,512]{2,1,0:T(8,128)(2,1)}, u32[]{:S(2)}) copy-start(bf16[2,128,512]{2,1,0:T(8,128)(2,1)} %queries_ref.1) | copy-start | bytes 786436
  49.9 12.2 %copy-start.1 = (bf16[2,128,512]{2,1,0:T(8,128)(2,1)S(1)}, bf16[2,128,512]{2,1,0:T(8,128)(2,1)}, u32[]{:S(2)}) copy-start(bf16[2,128,512]{2,1,0:T(8,128)(2,1)} %upstream_ref.1) | copy-start | bytes 786436
  49.9 12.2 %copy-start.4 = (f32[512]{0:T(512)S(1)}, f32[512]{0:T(512)}, u32[]{:S(2)}) copy-start(f32[512]{0:T(512)} %param.12) | copy-start | bytes 6148
  62.8 4.6 %collective-permute-start.10 = (f32[8,128]{1,0:T(8,128)S(1)}, f32[8,128]{1,0:T(8,128)S(1)}, u32[]{:S(2)}, u32[]{:S(2)}) collective-permute-start(f32[8,128]{1,0:T(8,128)S(1)} %get-tuple-element.141.refs_0_), channel_id=1, source_target_pairs={{0,3},{1,0},{2,1},{3,2},{4,7},{5,4},{6,5},{7,6},{8,11},{9,8},{10,9... | collective-permute-start | bytes 12296 | tf_op jit(solution)/shard_map/ppermute | solution.py:224
  62.8 4.6 %collective-permute-start.8 = (f32[8,128]{1,0:T(8,128)S(1)}, f32[8,128]{1,0:T(8,128)S(1)}, u32[]{:S(2)}, u32[]{:S(2)}) collective-permute-start(f32[8,128]{1,0:T(8,128)S(1)} %get-tuple-element.141.refs_0_), channel_id=1, source_target_pairs={{0,1},{1,2},{2,3},{3,0},{4,5},{5,6},{6,7},{7,4},{8,9},{9,10},{10,1... | collective-permute-start | bytes 12296 | tf_op jit(solution)/shard_map/ppermute | solution.py:224
  63.3 4.1 %collective-permute-start.9 = (f32[8,128]{1,0:T(8,128)S(1)}, f32[8,128]{1,0:T(8,128)S(1)}, u32[]{:S(2)}, u32[]{:S(2)}) collective-permute-start(f32[8,128]{1,0:T(8,128)S(1)} %get-tuple-element.141.refs_0_), channel_id=1, source_target_pairs={{0,2},{1,3},{2,0},{3,1},{4,6},{5,7},{6,4},{7,5},{8,10},{9,11},{10,... | collective-permute-start | bytes 12296 | tf_op jit(solution)/shard_map/ppermute | solution.py:224
  68.9 21.2 %collective-permute-start.17 = (bf16[4,3,64,512]{3,2,1,0:T(8,128)(2,1)S(1)}, bf16[4,3,64,512]{3,2,1,0:T(8,128)(2,1)S(1)}, u32[]{:S(2)}, u32[]{:S(2)}) collective-permute-start(bf16[4,3,64,512]{3,2,1,0:T(8,128)(2,1)S(1)} %get-tuple-element.194), channel_id=1, source_target_pairs={{0,4},{4,0},{8,12},{12,8},{16,20},{20,16},{24,28},{28,24},{1,5},{5... | collective-permute-start | bytes 2359304 | tf_op jit(solution)/shard_map/ppermute | solution.py:214
  70.5 13.4 %collective-permute-start.12 = (bf16[512,512]{1,0:T(8,128)(2,1)S(1)}, bf16[512,512]{1,0:T(8,128)(2,1)S(1)}, u32[]{:S(2)}, u32[]{:S(2)}) collective-permute-start(bf16[512,512]{1,0:T(8,128)(2,1)S(1)} %collective-permute-done.11.refs_2_), channel_id=1, source_target_pairs={{0,24},{4,28},{8,0},{12,4},{16,8},{20,12},{24,16},{28,20},{1,25},{... | collective-permute-start | bytes 1572872 | tf_op jit(solution)/shard_map/ppermute | solution.py:210
  85.5 3.4 %collective-permute-start.14 = (f32[8,1024]{1,0:T(8,128)S(1)}, f32[8,1024]{1,0:T(8,128)S(1)}, u32[]{:S(2)}, u32[]{:S(2)}) collective-permute-start(f32[8,1024]{1,0:T(8,128)S(1)} %get-tuple-element.163.refs_0_), channel_id=1, source_target_pairs={{0,1},{1,2},{2,3},{3,0},{4,5},{5,6},{6,7},{7,4},{8,9},{9,10},{10,1... | collective-permute-start | bytes 98312 | tf_op jit(solution)/shard_map/ppermute | solution.py:224
  85.6 4.0 %collective-permute-start.15 = (f32[8,1024]{1,0:T(8,128)S(1)}, f32[8,1024]{1,0:T(8,128)S(1)}, u32[]{:S(2)}, u32[]{:S(2)}) collective-permute-start(f32[8,1024]{1,0:T(8,128)S(1)} %get-tuple-element.163.refs_0_), channel_id=1, source_target_pairs={{0,2},{1,3},{2,0},{3,1},{4,6},{5,7},{6,4},{7,5},{8,10},{9,11},{10,... | collective-permute-start | bytes 98312 | tf_op jit(solution)/shard_map/ppermute | solution.py:224
  87.2 3.0 %collective-permute-start.16 = (f32[8,1024]{1,0:T(8,128)S(1)}, f32[8,1024]{1,0:T(8,128)S(1)}, u32[]{:S(2)}, u32[]{:S(2)}) collective-permute-start(f32[8,1024]{1,0:T(8,128)S(1)} %get-tuple-element.163.refs_0_), channel_id=1, source_target_pairs={{0,3},{1,0},{2,1},{3,2},{4,7},{5,4},{6,5},{7,6},{8,11},{9,8},{10,9... | collective-permute-start | bytes 98312 | tf_op jit(solution)/shard_map/ppermute | solution.py:224
  90.3 18.0 %collective-permute-start.18 = (bf16[3,64,512]{2,1,0:T(8,128)(2,1)S(1)}, bf16[3,64,512]{2,1,0:T(8,128)(2,1)S(1)}, u32[]{:S(2)}, u32[]{:S(2)}) collective-permute-start(bf16[3,64,512]{2,1,0:T(8,128)(2,1)S(1)} %get-tuple-element.196), channel_id=1, source_target_pairs={{0,8},{4,12},{8,16},{12,20},{16,24},{20,28},{24,0},{28,4},{1,9},{5... | collective-permute-start | bytes 589832 | tf_op jit(solution)/shard_map/ppermute | solution.py:210
  92.0 16.8 %collective-permute-start.19 = (bf16[3,64,512]{2,1,0:T(8,128)(2,1)S(1)}, bf16[3,64,512]{2,1,0:T(8,128)(2,1)S(1)}, u32[]{:S(2)}, u32[]{:S(2)}) collective-permute-start(bf16[3,64,512]{2,1,0:T(8,128)(2,1)S(1)} %get-tuple-element.197), channel_id=1, source_target_pairs={{0,16},{4,20},{8,24},{12,28},{16,0},{20,4},{24,8},{28,12},{1,17},{... | collective-permute-start | bytes 589832 | tf_op jit(solution)/shard_map/ppermute | solution.py:210
  95.1 13.6 %collective-permute-start.20 = (bf16[3,64,512]{2,1,0:T(8,128)(2,1)S(1)}, bf16[3,64,512]{2,1,0:T(8,128)(2,1)S(1)}, u32[]{:S(2)}, u32[]{:S(2)}) collective-permute-start(bf16[3,64,512]{2,1,0:T(8,128)(2,1)S(1)} %get-tuple-element.198), channel_id=1, source_target_pairs={{0,24},{4,28},{8,0},{12,4},{16,8},{20,12},{24,16},{28,20},{1,25},{... | collective-permute-start | bytes 589832 | tf_op jit(solution)/shard_map/ppermute | solution.py:210

commit v6 on v5

--- a/solution.py
+++ b/solution.py
@@ -490,13 +490,10 @@
 
 
 def last_kernel(
-    own, scale, me_ref, keys, values, wg, wu, wd, by_gate, by_up, by_lower, by_upper, pk, rk, hk,
+    own, me_ref, keys, values, wg, wu, wd, by_gate, by_up, by_lower, by_upper, pk, rk, hk,
     cot_g, cot_u, cot_d, rate_g, rate_u, rate_d, *refs,
 ):
-    count = len(refs) - 10
-    firsts = refs[:count]
-    grad_keys, grad_values, grad_g, grad_u, grad_d = refs[count:count + 5]
-    lower, upper, d_back, keys_t, back_t = refs[count + 5:]
+    grad_keys, grad_values, rest_g, rest_u, rest_d, lower, upper, d_back, keys_t, back_t = refs
     for part in chunks_of(keys.shape[0]):
         along, active, bent = by_gate[part], by_up[part], by_upper[part]
         ek = product(keys[part], cot_g[...])
@@ -517,15 +514,22 @@
     grad_values[...] = (
         -product(hk[...], cot_d[...]) - product(d_back[:own], wd[...])
     ).astype(bf16)
-    rows = grad_g.shape[1]
+    rows = rest_g.shape[0]
     start = pl.multiple_of(me_ref[0] * rows, 16)
-    for which, (left, right, rate, grad) in enumerate((
-        (keys_t, lower, rate_g, grad_g), (keys_t, upper, rate_u, grad_u), (back_t, values, rate_d, grad_d)
-    )):
+    for left, right, rate, rest, sign in (
+        (keys_t, lower, rate_g, rest_g, 1.0),
+        (keys_t, upper, rate_u, rest_u, 1.0),
+        (back_t, values, rate_d, rest_d, -1.0),
+    ):
         second = product(left[pl.ds(start, rows)], right[...])
+        rest[...] = rate[pl.ds(start, rows)] + sign * second
+
+
+def total_kernel(scale, rest_g, rest_u, rest_d, *refs):
+    firsts, grads = refs[:-3], refs[-3:]
+    for which, (rest, grad) in enumerate(zip((rest_g, rest_u, rest_d), grads)):
         first = sum(ref[which].astype(f32) for ref in firsts)
-        both = first - second if which == 2 else first + second
-        grad[0] = (both + rate[pl.ds(start, rows)]) * scale
+        grad[0] = (first + rest[...]) * scale
 
 
 def vmem():
@@ -735,13 +739,13 @@
         *(forward[which][4] for which in range(3)),
     )
 
-    return (grad_queries, *pl.pallas_call(
-        functools.partial(last_kernel, own, scale),
+    grad_keys, grad_values, *rests = pl.pallas_call(
+        functools.partial(last_kernel, own),
         out_shape=(
             S((own, depth), bf16), S((own, depth), bf16),
-            S((1, rows, hidden), f32), S((1, rows, hidden), f32), S((1, rows, hidden), f32),
+            *[S((rows, hidden), f32)] * 3,
         ),
-        in_specs=[smem()] + [vmem()] * (18 + len(firsts)),
+        in_specs=[smem()] + [vmem()] * 18,
         out_specs=[vmem()] * 5,
         scratch_shapes=[
             pltpu.VMEM((tokens, hidden), bf16),
@@ -753,8 +757,18 @@
         cost_estimate=light(),
         compiler_params=params(24),
     )(
-        me_ref, all_keys, all_values, wg, wu, wd, *slopes, *own_rows, *cots, *rates, *firsts,
-    ))
+        me_ref, all_keys, all_values, wg, wu, wd, *slopes, *own_rows, *cots, *rates,
+    )
+
+    grads = pl.pallas_call(
+        functools.partial(total_kernel, scale),
+        out_shape=(S((1, rows, hidden), f32),) * 3,
+        in_specs=[vmem()] * (3 + len(firsts)),
+        out_specs=[vmem()] * 3,
+        cost_estimate=light(),
+        compiler_params=params(6),
+    )(*rests, *firsts)
+    return (grad_queries, grad_keys, grad_values, *grads)
 
 
 def per_device(queries, keys, values, upstream, out_gain, gate_weight, up_weight, down_weight):

time: 116 us -> 114 us (0.983); the launches traced: 114 us -> 114 us
    pallas_call x1 -> x2, Pallas kernels: 5.25 us -> 5.94 us  [the longest x1 5.13 us: gather_tokens(): pl.pallas_call(functools.partial(last_kernel, own), out_shape=(S((own, de...]
  transfers between devices with their start and end apart: 21 -> 21, of which waited for: 10 -> 9; matrix products, arithmetic and copies ran while one was open for 0% -> 0% of each run, Pallas kernels for 33% -> 38%
where the time goes in v6:
time: 114 us
  Pallas kernels  46.1 us (40%)
  waiting for transfers between devices  35.2 us (31%)
  starting transfers between devices  31 us (27%)
    ppermute x6, waiting for transfers between devices, swap(): return lax.ppermute(array, 'tok', [(i, i ^ 1) for i in range(2 * ring)])  18.5 us
    ppermute x9, starting transfers between devices, shift(): return lax.ppermute(array, 'tok', pairs)  15.5 us
    ppermute x9, waiting for transfers between devices, shift(): return lax.ppermute(array, 'tok', pairs)  15.1 us
    ppermute x6, starting transfers between devices, swap(): return lax.ppermute(array, 'tok', [(i, i ^ 1) for i in range(2 * ring)])  10.4 us
    pallas_call x1, Pallas kernels, gather_tokens(): pl.pallas_call(schulz_back_kernel, out_shape=(narrow,) * 3, in_specs=[vme...  8.33 us
    pallas_call x2, Pallas kernels, schulz(): pl.pallas_call(functools.partial(schulz_kernel, count), out_shape=(S((NS_...  6.69 us
    pallas_call x1, Pallas kernels, gather_tokens(): pl.pallas_call(functools.partial(fast_kernel, layout, ring), out_shape=(n...  6 us
    pallas_call x2, Pallas kernels, second_forward(): pl.pallas_call(functools.partial(second_forward_kernel, first, len(arrive...  5.85 us
  transfers between devices with their start and end apart: 21, of which 9 were waited for; matrix products, arithmetic and copies ran while one was open for 0% of the time, Pallas kernels for 38%

profile of v6, /device:TPU:0, one launch (start us, length us, event | category | flops | bytes accessed | tf_op | source)
XLA Modules:
  0.0 114.2 jit_solution(425771570434284195)
XLA Ops:
  0.6 2.1 %shard_map.127 = (bf16[448,512]{1,0:T(8,128)(2,1)}, bf16[256,512]{1,0:T(8,128)(2,1)}) custom-call(bf16[1,64,512]{2,1,0:T(8,128)(2,1)} %gate.1, bf16[1,64,512]{2,1,0:T(8,128)(2,1)} %up.1, bf16[1,64,512]{2,1,0:T(8,128)(2,1)} %down.1, bf16[128,512]{1,0:T(8,128)(2,1)} %keys.1, bf16[128,512]{1,0:T(8,128)(2,1)} %values.1, bf16[2,128,512]{2,1,0:T(8,128)(2,1)} %queries_ref.1, ...), custom_call_target="tpu_custom_call" | custom-call | tf_op jit(solution)/shard_map/pallas_call | solution.py:576
  2.8 3.0 %collective-permute-start.2 = (bf16[448,512]{1,0:T(8,128)(2,1)}, bf16[448,512]{1,0:T(8,128)(2,1)S(1)}, u32[]{:S(2)}, u32[]{:S(2)}) collective-permute-start(bf16[448,512]{1,0:T(8,128)(2,1)} %get-tuple-element.116.refs_0_), channel_id=1, source_target_pairs={{0,4},{4,0},{8,12},{12,8},{16,20},{20,16},{24,28},{28,24},{1,5},{5... | collective-permute-start | bytes 1376264 | tf_op jit(solution)/shard_map/ppermute | solution.py:214
  5.8 1.6 %collective-permute-start = (bf16[448,512]{1,0:T(8,128)(2,1)}, bf16[448,512]{1,0:T(8,128)(2,1)S(1)}, u32[]{:S(2)}, u32[]{:S(2)}) collective-permute-start(bf16[448,512]{1,0:T(8,128)(2,1)} %get-tuple-element.116.refs_0_), channel_id=1, source_target_pairs={{0,8},{4,12},{8,16},{12,20},{16,24},{20,28},{24,0},{28,4},{1,9},{5... | collective-permute-start | bytes 1376264 | tf_op jit(solution)/shard_map/ppermute | solution.py:210
  7.9 9.4 %collective-permute-done.2.refs_1_ = bf16[448,512]{1,0:T(8,128)(2,1)S(1)} collective-permute-done((bf16[448,512]{1,0:T(8,128)(2,1)}, bf16[448,512]{1,0:T(8,128)(2,1)S(1)}, u32[]{:S(2)}, u32[]{:S(2)}) %collective-permute-start.2) | collective-permute-done | bytes 458784 | tf_op jit(solution)/shard_map/ppermute | solution.py:214
  17.3 4.2 %collective-permute-start.5 = (bf16[448,512]{1,0:T(8,128)(2,1)}, bf16[448,512]{1,0:T(8,128)(2,1)S(1)}, u32[]{:S(2)}, u32[]{:S(2)}) collective-permute-start(bf16[448,512]{1,0:T(8,128)(2,1)} %get-tuple-element.116.refs_0_), channel_id=1, source_target_pairs={{0,24},{4,28},{8,0},{12,4},{16,8},{20,12},{24,16},{28,20},{1,25},{... | collective-permute-start | bytes 1376264 | tf_op jit(solution)/shard_map/ppermute | solution.py:210
  21.5 1.5 %collective-permute-start.7 = (bf16[448,512]{1,0:T(8,128)(2,1)S(1)}, bf16[448,512]{1,0:T(8,128)(2,1)S(1)}, u32[]{:S(2)}, u32[]{:S(2)}) collective-permute-start(bf16[448,512]{1,0:T(8,128)(2,1)S(1)} %collective-permute-done.refs_0_.refs_1_), channel_id=1, source_target_pairs={{0,4},{4,0},{8,12},{12,8},{16,20},{20,16},{24,28},{28,24},{1,5},{5... | collective-permute-start | bytes 1376264 | tf_op jit(solution)/shard_map/ppermute | solution.py:214
  24.0 1.3 %shard_map.128 = (bf16[512,512]{1,0:T(8,128)(2,1)S(1)}, bf16[512,512]{1,0:T(8,128)(2,1)S(1)}, bf16[512,512]{1,0:T(8,128)(2,1)S(1)}, bf16[1024,512]{1,0:T(8,128)(2,1)S(1)}, bf16[1024,512]{1,0:T(8,128)(2,1)S(1)}) custom-call(s32[1]{0:T(128)} %bitcast.me_ref, bf16[448,512]{1,0:T(8,128)(2,1)S(1)} %copy-done.2, bf16[448,512]{1,0:T(8,128)(2,1)S(1)} %collective-permute-done.2.refs_1_), custom_call_target="tpu_custom_call" | custom-call | flops 1 | bytes 1 | tf_op jit(solution)/shard_map/pallas_call | solution.py:593
  26.3 6.5 %collective-permute-done.5.refs_0_ = bf16[448,512]{1,0:T(8,128)(2,1)S(1)} collective-permute-done((bf16[448,512]{1,0:T(8,128)(2,1)}, bf16[448,512]{1,0:T(8,128)(2,1)S(1)}, u32[]{:S(2)}, u32[]{:S(2)}) %collective-permute-start.5) | collective-permute-done | bytes 458784 | tf_op jit(solution)/shard_map/ppermute | solution.py:210
  32.8 1.3 %shard_map.130 = (bf16[512,512]{1,0:T(8,128)(2,1)S(1)}, bf16[512,512]{1,0:T(8,128)(2,1)S(1)}, bf16[512,512]{1,0:T(8,128)(2,1)S(1)}, bf16[1024,512]{1,0:T(8,128)(...) custom-call(s32[1]{0:T(128)} %bitcast.me_ref, ...), custom_call_target="tpu_custom_call", output_to_operand_aliasing={{0}: (5, {}), {1}: (6, {}), {2}: (7, {}), {3}: (8, {}), {4}... | custom-call | flops 1 | bytes 1 | tf_op jit(solution)/shard_map/pallas_call | solution.py:593
  35.2 1.5 %collective-permute-start.6 = (bf16[448,512]{1,0:T(8,128)(2,1)S(1)}, bf16[448,512]{1,0:T(8,128)(2,1)S(1)}, u32[]{:S(2)}, u32[]{:S(2)}) collective-permute-start(bf16[448,512]{1,0:T(8,128)(2,1)S(1)} %collective-permute-done.5.refs_0_), channel_id=1, source_target_pairs={{0,4},{4,0},{8,12},{12,8},{16,20},{20,16},{24,28},{28,24},{1,5},{5... | collective-permute-start | bytes 1376264 | tf_op jit(solution)/shard_map/ppermute | solution.py:214
  36.6 5.9 %collective-permute-done.3.refs_0_ = bf16[448,512]{1,0:T(8,128)(2,1)S(1)} collective-permute-done((bf16[448,512]{1,0:T(8,128)(2,1)S(1)}, bf16[448,512]{1,0:T(8,128)(2,1)S(1)}, u32[]{:S(2)}, u32[]{:S(2)}) %collective-permute-start.3) | collective-permute-done | bytes 458784 | tf_op jit(solution)/shard_map/ppermute | solution.py:210
  42.6 2.3 %collective-permute-start.4 = (bf16[448,512]{1,0:T(8,128)(2,1)S(1)}, bf16[448,512]{1,0:T(8,128)(2,1)S(1)}, u32[]{:S(2)}, u32[]{:S(2)}) collective-permute-start(bf16[448,512]{1,0:T(8,128)(2,1)S(1)} %collective-permute-done.3.refs_0_), channel_id=1, source_target_pairs={{0,4},{4,0},{8,12},{12,8},{16,20},{20,16},{24,28},{28,24},{1,5},{5... | collective-permute-start | bytes 1376264 | tf_op jit(solution)/shard_map/ppermute | solution.py:214
  45.7 2.9 %collective-permute-done.6.refs_1_ = bf16[448,512]{1,0:T(8,128)(2,1)S(1)} collective-permute-done((bf16[448,512]{1,0:T(8,128)(2,1)S(1)}, bf16[448,512]{1,0:T(8,128)(2,1)S(1)}, u32[]{:S(2)}, u32[]{:S(2)}) %collective-permute-start.6) | collective-permute-done | bytes 458784 | tf_op jit(solution)/shard_map/ppermute | solution.py:214
  48.6 1.3 %shard_map.131 = (bf16[512,512]{1,0:T(8,128)(2,1)S(1)}, bf16[512,512]{1,0:T(8,128)(2,1)S(1)}, bf16[512,512]{1,0:T(8,128)(2,1)S(1)}, bf16[1024,512]{1,0:T(8,128)(2,1)S(1)}, bf16[1024,512]{1,0:T(8,128)(2,1)S(1)}) custom-call(s32[1]{0:T(128)} %bitcast.me_ref, ...), custom_call_target="tpu_custom_call", output_to_operand_aliasing={{0}: (3, {}), {1}: (4, {}), {2}: (5, {}), {3}: (6, {}), {4}... | custom-call | flops 1 | bytes 1 | tf_op jit(solution)/shard_map/pallas_call | solution.py:593
  49.9 6.2 %collective-permute-done.4.refs_0_ = bf16[448,512]{1,0:T(8,128)(2,1)S(1)} collective-permute-done((bf16[448,512]{1,0:T(8,128)(2,1)S(1)}, bf16[448,512]{1,0:T(8,128)(2,1)S(1)}, u32[]{:S(2)}, u32[]{:S(2)}) %collective-permute-start.4) | collective-permute-done | bytes 458784 | tf_op jit(solution)/shard_map/ppermute | solution.py:214
  56.1 6.0 %shard_map.132 = (bf16[512,512]{1,0:T(8,128)(2,1)S(1)}, bf16[512,512]{1,0:T(8,128)(2,1)S(1)}, bf16[512,512]{1,0:T(8,128)(2,1)S(1)}, bf16[1024,512]{1,0:T(8,128)(...) custom-call(s32[1]{0:T(128)} %bitcast.me_ref, ...), custom_call_target="tpu_custom_call", output_to_operand_aliasing={{0}: (2, {}), {1}: (3, {}), {2}: (4, {}), {3}: (5, {}), {4}... | custom-call | flops 1 | bytes 1 | tf_op jit(solution)/shard_map/pallas_call | solution.py:620
  63.3 1.5 %collective-permute-start.9 = (f32[8,128]{1,0:T(8,128)S(1)}, f32[8,128]{1,0:T(8,128)S(1)}, u32[]{:S(2)}, u32[]{:S(2)}) collective-permute-start(f32[8,128]{1,0:T(8,128)S(1)} %get-tuple-element.144.refs_0_), channel_id=1, source_target_pairs={{0,2},{1,3},{2,0},{3,1},{4,6},{5,7},{6,4},{7,5},{8,10},{9,11},{10,... | collective-permute-start | bytes 12296 | tf_op jit(solution)/shard_map/ppermute | solution.py:224
  64.8 2.5 %shard_map.134 = (bf16[2,512,512]{2,1,0:T(8,128)(2,1)S(1)}, bf16[2,512,512]{2,1,0:T(8,128)(2,1)S(1)}, bf16[2,512,512]{2,1,0:T(8,128)(2,1)S(1)}, bf16[512,512]{1,0:T(8,128)(2,1)S(1)}, f32[8,128]{1,0:T(8,128)S(1)}) custom-call(f32[512,512]{1,0:T(8,128)S(1)} %get-tuple-element.142.refs_0_.refs_3_, bf16[512,512]{1,0:T(8,128)(2,1)S(1)} %get-tuple-element.132.wg.refs_1_), custom_call_target="tpu_custom_call" | custom-call | flops 1 | bytes 1 | tf_op jit(solution)/shard_map/pallas_call | solution.py:653
  67.4 1.5 %shard_map.135 = (bf16[128,512]{1,0:T(8,128)(2,1)S(1)}, bf16[4,3,64,512]{3,2,1,0:T(8,128)(2,1)S(1)}, bf16[4,3,64,512]{3,2,1,0:T(8,128)(2,1)S(1)}) custom-call(s32[1]{0:T(128)} %bitcast.me_ref, bf16[128,512]{1,0:T(8,128)(2,1)S(1)} %get-tuple-element.135.queries, bf16[128,512]{1,0:T(8,128)(2,1)S(1)} %get-tuple-element.136.upstream, f32[1,512]{1,0:T(1,128)S(1)} %bitcast.3, ...), custom_call_target="tpu_custom_call" | custom-call | flops 1 | bytes 1 | tf_op jit(solution)/shard_map/pallas_call | solution.py:669
  68.9 1.6 %collective-permute-start.17 = (bf16[4,3,64,512]{3,2,1,0:T(8,128)(2,1)S(1)}, bf16[4,3,64,512]{3,2,1,0:T(8,128)(2,1)S(1)}, u32[]{:S(2)}, u32[]{:S(2)}) collective-permute-start(bf16[4,3,64,512]{3,2,1,0:T(8,128)(2,1)S(1)} %get-tuple-element.202), channel_id=1, source_target_pairs={{0,4},{4,0},{8,12},{12,8},{16,20},{20,16},{24,28},{28,24},{1,5},{5... | collective-permute-start | bytes 2359304 | tf_op jit(solution)/shard_map/ppermute | solution.py:214
  70.5 2.4 %collective-permute-start.12 = (bf16[512,512]{1,0:T(8,128)(2,1)S(1)}, bf16[512,512]{1,0:T(8,128)(2,1)S(1)}, u32[]{:S(2)}, u32[]{:S(2)}) collective-permute-start(bf16[512,512]{1,0:T(8,128)(2,1)S(1)} %collective-permute-done.11.refs_2_), channel_id=1, source_target_pairs={{0,24},{4,28},{8,0},{12,4},{16,8},{20,12},{24,16},{28,20},{1,25},{... | collective-permute-start | bytes 1572872 | tf_op jit(solution)/shard_map/ppermute | solution.py:210
  72.9 4.2 %shard_map.136 = (bf16[2,512,512]{2,1,0:T(8,128)(2,1)S(1)}, bf16[2,512,512]{2,1,0:T(8,128)(2,1)S(1)}, bf16[2,512,512]{2,1,0:T(8,128)(2,1)S(1)}, bf16[512,512]{1,...) custom-call(f32[512,512]{1,0:T(8,128)S(1)} %get-tuple-element.147.re, ...), custom_call_target="tpu_custom_call" | custom-call | flops 1 | bytes 1 | tf_op jit(solution)/shard_map/pallas_call | solution.py:653
  77.0 4.3 %shard_map.137 = (bf16[1024,512]{1,0:T(8,128)(2,1)S(1)}, bf16[1024,512]{1,0:T(8,128)(2,1)S(1)}, f32[1024,512]{1,0:T(8,128)S(1)}, f32[1024,512]{1,0:T(8,128)S(1)}...) custom-call(f32[1,512]{1,0:T(1,128)S(1)} %bitcast.4, ...), custom_call_target="tpu_custom_call" | custom-call | flops 1 | bytes 1 | tf_op jit(solution)/shard_map/pallas_call | solution.py:687
  81.3 2.6 %collective-permute-done.12.refs_0_ = bf16[512,512]{1,0:T(8,128)(2,1)S(1)} collective-permute-done((bf16[512,512]{1,0:T(8,128)(2,1)S(1)}, bf16[512,512]{1,0:T(8,128)(2,1)S(1)}, u32[]{:S(2)}, u32[]{:S(2)}) %collective-permute-start.12) | collective-permute-done | bytes 524320 | tf_op jit(solution)/shard_map/ppermute | solution.py:210
  83.9 1.6 %shard_map.138 = (bf16[1024,512]{1,0:T(8,128)(2,1)S(1)}, bf16[1024,512]{1,0:T(8,128)(2,1)S(1)}, f32[1024,512]{1,0:T(8,128)S(1)}, f32[1024,512]{1,0:T(8,128)S(1)}...) custom-call(f32[1,512]{1,0:T(1,128)S(1)} %bitcast.5, ...), custom_call_target="tpu_custom_call", output_to_operand_aliasing={{0}: (5, {}), {1}: (6, {}), {2}: (7, {}), {3}: (8, {}), {4}... | custom-call | flops 1 | bytes 1 | tf_op jit(solution)/shard_map/pallas_call | solution.py:687
  85.6 1.6 %collective-permute-start.15 = (f32[8,1024]{1,0:T(8,128)S(1)}, f32[8,1024]{1,0:T(8,128)S(1)}, u32[]{:S(2)}, u32[]{:S(2)}) collective-permute-start(f32[8,1024]{1,0:T(8,128)S(1)} %get-tuple-element.166.refs_0_), channel_id=1, source_target_pairs={{0,2},{1,3},{2,0},{3,1},{4,6},{5,7},{6,4},{7,5},{8,10},{9,11},{10,... | collective-permute-start | bytes 98312 | tf_op jit(solution)/shard_map/ppermute | solution.py:224
  87.2 1.4 %collective-permute-start.16 = (f32[8,1024]{1,0:T(8,128)S(1)}, f32[8,1024]{1,0:T(8,128)S(1)}, u32[]{:S(2)}, u32[]{:S(2)}) collective-permute-start(f32[8,1024]{1,0:T(8,128)S(1)} %get-tuple-element.166.refs_0_), channel_id=1, source_target_pairs={{0,3},{1,0},{2,1},{3,2},{4,7},{5,4},{6,5},{7,6},{8,11},{9,8},{10,9... | collective-permute-start | bytes 98312 | tf_op jit(solution)/shard_map/ppermute | solution.py:224
  90.3 1.6 %collective-permute-start.18 = (bf16[3,64,512]{2,1,0:T(8,128)(2,1)S(1)}, bf16[3,64,512]{2,1,0:T(8,128)(2,1)S(1)}, u32[]{:S(2)}, u32[]{:S(2)}) collective-permute-start(bf16[3,64,512]{2,1,0:T(8,128)(2,1)S(1)} %get-tuple-element.204), channel_id=1, source_target_pairs={{0,8},{4,12},{8,16},{12,20},{16,24},{20,28},{24,0},{28,4},{1,9},{5... | collective-permute-start | bytes 589832 | tf_op jit(solution)/shard_map/ppermute | solution.py:210
  92.0 3.2 %collective-permute-start.19 = (bf16[3,64,512]{2,1,0:T(8,128)(2,1)S(1)}, bf16[3,64,512]{2,1,0:T(8,128)(2,1)S(1)}, u32[]{:S(2)}, u32[]{:S(2)}) collective-permute-start(bf16[3,64,512]{2,1,0:T(8,128)(2,1)S(1)} %get-tuple-element.205), channel_id=1, source_target_pairs={{0,16},{4,20},{8,24},{12,28},{16,0},{20,4},{24,8},{28,12},{1,17},{... | collective-permute-start | bytes 589832 | tf_op jit(solution)/shard_map/ppermute | solution.py:210
  95.9 4.0 %shard_map.139 = (bf16[2,128,512]{2,1,0:T(8,128)(2,1)}, f32[512,512]{1,0:T(8,128)S(1)}, f32[512,512]{1,0:T(8,128)S(1)}, f32[512,512]{1,0:T(8,128)S(1)}) custom-call(bf16[128,512]{1,0:T(8,128)(2,1)S(1)} %get-tuple-element.145.grad_first, bf16[1024,512]{1,0:T(8,128)(2,1)S(1)} %get-tuple-element.160.queries, bf16[1024,512]{1,0:T(8,128)(2,1)S(1)} %get-tuple-element.161.upstream, ...), custom_call_target="tpu_custom_call" | custom-call | flops 1 | bytes 1 | tf_op jit(solution)/shard_map/pallas_call | solution.py:718
  99.9 8.3 %shard_map.140 = (bf16[512,512]{1,0:T(8,128)(2,1)S(1)}, bf16[512,512]{1,0:T(8,128)(2,1)S(1)}, bf16[512,512]{1,0:T(8,128)(2,1)S(1)}) custom-call(f32[512,512]{1,0:T(8,128)S(1)} %get-tuple-element.177.refs_0_.rate_g, f32[512,512]{1,0:T(8,128)S(1)} %get-tuple-element.178.refs_1_.rate_u, f32[512,512]{1,0:T(8,128)S(1)} %get-tuple-element.179.refs_2_.rate_d, ...), custom_call_target="tpu_custom_call" | custom-call | flops 1 | bytes 1 | tf_op jit(solution)/shard_map/pallas_call | solution.py:729
  108.3 5.1 %shard_map.141 = (bf16[128,512]{1,0:T(8,128)(2,1)}, bf16[128,512]{1,0:T(8,128)(2,1)}, f32[64,512]{1,0:T(8,128)S(1)}, f32[64,512]{1,0:T(8,128)S(1)}, f32[64,512]{1,0:T(8,128)S(1)}) custom-call(s32[1]{0:T(128)} %bitcast.me_ref, bf16[1024,512]{1,0:T(8,128)(2,1)S(1)} %get-tuple-element.168.keys, bf16[1024,512]{1,0:T(8,128)(2,1)S(1)} %get-tuple-element.169.values, ...), custom_call_target="tpu_custom_call" | custom-call | flops 1 | bytes 1 | tf_op jit(solution)/shard_map/pallas_call | solution.py:742
  (37 shorter events, 9.0 us)
Async XLA Ops:
  2.8 14.6 %collective-permute-start.2 = (bf16[448,512]{1,0:T(8,128)(2,1)}, bf16[448,512]{1,0:T(8,128)(2,1)S(1)}, u32[]{:S(2)}, u32[]{:S(2)}) collective-permute-start(bf16[448,512]{1,0:T(8,128)(2,1)} %get-tuple-element.116.refs_0_), channel_id=1, source_target_pairs={{0,4},{4,0},{8,12},{12,8},{16,20},{20,16},{24,28},{28,24},{1,5},{5... | collective-permute-start | bytes 1376264 | tf_op jit(solution)/shard_map/ppermute | solution.py:214
  5.8 15.7 %collective-permute-start = (bf16[448,512]{1,0:T(8,128)(2,1)}, bf16[448,512]{1,0:T(8,128)(2,1)S(1)}, u32[]{:S(2)}, u32[]{:S(2)}) collective-permute-start(bf16[448,512]{1,0:T(8,128)(2,1)} %get-tuple-element.116.refs_0_), channel_id=1, source_target_pairs={{0,8},{4,12},{8,16},{12,20},{16,24},{20,28},{24,0},{28,4},{1,9},{5... | collective-permute-start | bytes 1376264 | tf_op jit(solution)/shard_map/ppermute | solution.py:210
  7.3 17.9 %collective-permute-start.1 = (bf16[256,512]{1,0:T(8,128)(2,1)}, bf16[256,512]{1,0:T(8,128)(2,1)S(1)}, u32[]{:S(2)}, u32[]{:S(2)}) collective-permute-start(bf16[256,512]{1,0:T(8,128)(2,1)} %get-tuple-element.109.refs_2_), channel_id=1, source_target_pairs={{0,4},{4,0},{8,12},{12,8},{16,20},{20,16},{24,28},{28,24},{1,5},{5... | collective-permute-start | bytes 786440 | tf_op jit(solution)/shard_map/ppermute | solution.py:214
  17.3 15.5 %collective-permute-start.5 = (bf16[448,512]{1,0:T(8,128)(2,1)}, bf16[448,512]{1,0:T(8,128)(2,1)S(1)}, u32[]{:S(2)}, u32[]{:S(2)}) collective-permute-start(bf16[448,512]{1,0:T(8,128)(2,1)} %get-tuple-element.116.refs_0_), channel_id=1, source_target_pairs={{0,24},{4,28},{8,0},{12,4},{16,8},{20,12},{24,16},{28,20},{1,25},{... | collective-permute-start | bytes 1376264 | tf_op jit(solution)/shard_map/ppermute | solution.py:210
  21.5 11.3 %collective-permute-start.7 = (bf16[448,512]{1,0:T(8,128)(2,1)S(1)}, bf16[448,512]{1,0:T(8,128)(2,1)S(1)}, u32[]{:S(2)}, u32[]{:S(2)}) collective-permute-start(bf16[448,512]{1,0:T(8,128)(2,1)S(1)} %collective-permute-done.refs_0_.refs_1_), channel_id=1, source_target_pairs={{0,4},{4,0},{8,12},{12,8},{16,20},{20,16},{24,28},{28,24},{1,5},{5... | collective-permute-start | bytes 1376264 | tf_op jit(solution)/shard_map/ppermute | solution.py:214
  23.0 1.0 copy-start.2
  25.3 7.6 %copy-start.3 = (bf16[256,512]{1,0:T(8,128)(2,1)S(1)}, bf16[256,512]{1,0:T(8,128)(2,1)}, u32[]{:S(2)}) copy-start(bf16[256,512]{1,0:T(8,128)(2,1)} %get-tuple-element.109.refs_2_) | copy-start | bytes 786436
  26.2 16.3 %collective-permute-start.3 = (bf16[448,512]{1,0:T(8,128)(2,1)S(1)}, bf16[448,512]{1,0:T(8,128)(2,1)S(1)}, u32[]{:S(2)}, u32[]{:S(2)}) collective-permute-start(bf16[448,512]{1,0:T(8,128)(2,1)S(1)} %get-tuple-element.115), channel_id=1, source_target_pairs={{0,8},{4,12},{8,16},{12,20},{16,24},{20,28},{24,0},{28,4},{1,9},{5... | collective-permute-start | bytes 1376264 | tf_op jit(solution)/shard_map/ppermute | solution.py:210
  34.2 34.8 %collective-permute-start.13 = (bf16[512,512]{1,0:T(8,128)(2,1)S(1)}, bf16[512,512]{1,0:T(8,128)(2,1)S(1)}, u32[]{:S(2)}, u32[]{:S(2)}) collective-permute-start(bf16[512,512]{1,0:T(8,128)(2,1)S(1)} %get-tuple-element.151.refs_0_), channel_id=1, source_target_pairs={{0,8},{4,12},{8,16},{12,20},{16,24},{20,28},{24,0},{28,4},{1,9},{5... | collective-permute-start | bytes 1572872 | tf_op jit(solution)/shard_map/ppermute | solution.py:210
  35.2 13.5 %collective-permute-start.6 = (bf16[448,512]{1,0:T(8,128)(2,1)S(1)}, bf16[448,512]{1,0:T(8,128)(2,1)S(1)}, u32[]{:S(2)}, u32[]{:S(2)}) collective-permute-start(bf16[448,512]{1,0:T(8,128)(2,1)S(1)} %collective-permute-done.5.refs_0_), channel_id=1, source_target_pairs={{0,4},{4,0},{8,12},{12,8},{16,20},{20,16},{24,28},{28,24},{1,5},{5... | collective-permute-start | bytes 1376264 | tf_op jit(solution)/shard_map/ppermute | solution.py:214
  42.6 13.5 %collective-permute-start.4 = (bf16[448,512]{1,0:T(8,128)(2,1)S(1)}, bf16[448,512]{1,0:T(8,128)(2,1)S(1)}, u32[]{:S(2)}, u32[]{:S(2)}) collective-permute-start(bf16[448,512]{1,0:T(8,128)(2,1)S(1)} %collective-permute-done.3.refs_0_), channel_id=1, source_target_pairs={{0,4},{4,0},{8,12},{12,8},{16,20},{20,16},{24,28},{28,24},{1,5},{5... | collective-permute-start | bytes 1376264 | tf_op jit(solution)/shard_map/ppermute | solution.py:214
  44.9 25.6 %collective-permute-start.11 = (bf16[512,512]{1,0:T(8,128)(2,1)S(1)}, bf16[512,512]{1,0:T(8,128)(2,1)S(1)}, u32[]{:S(2)}, u32[]{:S(2)}) collective-permute-start(bf16[512,512]{1,0:T(8,128)(2,1)S(1)} %get-tuple-element.151.refs_0_), channel_id=1, source_target_pairs={{0,24},{4,28},{8,0},{12,4},{16,8},{20,12},{24,16},{28,20},{1,25},{... | collective-permute-start | bytes 1572872 | tf_op jit(solution)/shard_map/ppermute | solution.py:210
  49.9 12.2 %copy-start = (bf16[2,128,512]{2,1,0:T(8,128)(2,1)S(1)}, bf16[2,128,512]{2,1,0:T(8,128)(2,1)}, u32[]{:S(2)}) copy-start(bf16[2,128,512]{2,1,0:T(8,128)(2,1)} %queries_ref.1) | copy-start | bytes 786436
  49.9 12.2 %copy-start.1 = (bf16[2,128,512]{2,1,0:T(8,128)(2,1)S(1)}, bf16[2,128,512]{2,1,0:T(8,128)(2,1)}, u32[]{:S(2)}) copy-start(bf16[2,128,512]{2,1,0:T(8,128)(2,1)} %upstream_ref.1) | copy-start | bytes 786436
  49.9 12.2 %copy-start.4 = (f32[512]{0:T(512)S(1)}, f32[512]{0:T(512)}, u32[]{:S(2)}) copy-start(f32[512]{0:T(512)} %param.12) | copy-start | bytes 6148
  62.8 4.6 %collective-permute-start.10 = (f32[8,128]{1,0:T(8,128)S(1)}, f32[8,128]{1,0:T(8,128)S(1)}, u32[]{:S(2)}, u32[]{:S(2)}) collective-permute-start(f32[8,128]{1,0:T(8,128)S(1)} %get-tuple-element.144.refs_0_), channel_id=1, source_target_pairs={{0,3},{1,0},{2,1},{3,2},{4,7},{5,4},{6,5},{7,6},{8,11},{9,8},{10,9... | collective-permute-start | bytes 12296 | tf_op jit(solution)/shard_map/ppermute | solution.py:224
  62.8 4.6 %collective-permute-start.8 = (f32[8,128]{1,0:T(8,128)S(1)}, f32[8,128]{1,0:T(8,128)S(1)}, u32[]{:S(2)}, u32[]{:S(2)}) collective-permute-start(f32[8,128]{1,0:T(8,128)S(1)} %get-tuple-element.144.refs_0_), channel_id=1, source_target_pairs={{0,1},{1,2},{2,3},{3,0},{4,5},{5,6},{6,7},{7,4},{8,9},{9,10},{10,1... | collective-permute-start | bytes 12296 | tf_op jit(solution)/shard_map/ppermute | solution.py:224
  63.3 4.1 %collective-permute-start.9 = (f32[8,128]{1,0:T(8,128)S(1)}, f32[8,128]{1,0:T(8,128)S(1)}, u32[]{:S(2)}, u32[]{:S(2)}) collective-permute-start(f32[8,128]{1,0:T(8,128)S(1)} %get-tuple-element.144.refs_0_), channel_id=1, source_target_pairs={{0,2},{1,3},{2,0},{3,1},{4,6},{5,7},{6,4},{7,5},{8,10},{9,11},{10,... | collective-permute-start | bytes 12296 | tf_op jit(solution)/shard_map/ppermute | solution.py:224
  68.9 21.2 %collective-permute-start.17 = (bf16[4,3,64,512]{3,2,1,0:T(8,128)(2,1)S(1)}, bf16[4,3,64,512]{3,2,1,0:T(8,128)(2,1)S(1)}, u32[]{:S(2)}, u32[]{:S(2)}) collective-permute-start(bf16[4,3,64,512]{3,2,1,0:T(8,128)(2,1)S(1)} %get-tuple-element.202), channel_id=1, source_target_pairs={{0,4},{4,0},{8,12},{12,8},{16,20},{20,16},{24,28},{28,24},{1,5},{5... | collective-permute-start | bytes 2359304 | tf_op jit(solution)/shard_map/ppermute | solution.py:214
  70.5 13.4 %collective-permute-start.12 = (bf16[512,512]{1,0:T(8,128)(2,1)S(1)}, bf16[512,512]{1,0:T(8,128)(2,1)S(1)}, u32[]{:S(2)}, u32[]{:S(2)}) collective-permute-start(bf16[512,512]{1,0:T(8,128)(2,1)S(1)} %collective-permute-done.11.refs_2_), channel_id=1, source_target_pairs={{0,24},{4,28},{8,0},{12,4},{16,8},{20,12},{24,16},{28,20},{1,25},{... | collective-permute-start | bytes 1572872 | tf_op jit(solution)/shard_map/ppermute | solution.py:210
  85.5 3.4 %collective-permute-start.14 = (f32[8,1024]{1,0:T(8,128)S(1)}, f32[8,1024]{1,0:T(8,128)S(1)}, u32[]{:S(2)}, u32[]{:S(2)}) collective-permute-start(f32[8,1024]{1,0:T(8,128)S(1)} %get-tuple-element.166.refs_0_), channel_id=1, source_target_pairs={{0,1},{1,2},{2,3},{3,0},{4,5},{5,6},{6,7},{7,4},{8,9},{9,10},{10,1... | collective-permute-start | bytes 98312 | tf_op jit(solution)/shard_map/ppermute | solution.py:224
  85.6 4.0 %collective-permute-start.15 = (f32[8,1024]{1,0:T(8,128)S(1)}, f32[8,1024]{1,0:T(8,128)S(1)}, u32[]{:S(2)}, u32[]{:S(2)}) collective-permute-start(f32[8,1024]{1,0:T(8,128)S(1)} %get-tuple-element.166.refs_0_), channel_id=1, source_target_pairs={{0,2},{1,3},{2,0},{3,1},{4,6},{5,7},{6,4},{7,5},{8,10},{9,11},{10,... | collective-permute-start | bytes 98312 | tf_op jit(solution)/shard_map/ppermute | solution.py:224
  87.2 3.0 %collective-permute-start.16 = (f32[8,1024]{1,0:T(8,128)S(1)}, f32[8,1024]{1,0:T(8,128)S(1)}, u32[]{:S(2)}, u32[]{:S(2)}) collective-permute-start(f32[8,1024]{1,0:T(8,128)S(1)} %get-tuple-element.166.refs_0_), channel_id=1, source_target_pairs={{0,3},{1,0},{2,1},{3,2},{4,7},{5,4},{6,5},{7,6},{8,11},{9,8},{10,9... | collective-permute-start | bytes 98312 | tf_op jit(solution)/shard_map/ppermute | solution.py:224
  90.3 23.1 %collective-permute-start.18 = (bf16[3,64,512]{2,1,0:T(8,128)(2,1)S(1)}, bf16[3,64,512]{2,1,0:T(8,128)(2,1)S(1)}, u32[]{:S(2)}, u32[]{:S(2)}) collective-permute-start(bf16[3,64,512]{2,1,0:T(8,128)(2,1)S(1)} %get-tuple-element.204), channel_id=1, source_target_pairs={{0,8},{4,12},{8,16},{12,20},{16,24},{20,28},{24,0},{28,4},{1,9},{5... | collective-permute-start | bytes 589832 | tf_op jit(solution)/shard_map/ppermute | solution.py:210
  92.0 21.5 %collective-permute-start.19 = (bf16[3,64,512]{2,1,0:T(8,128)(2,1)S(1)}, bf16[3,64,512]{2,1,0:T(8,128)(2,1)S(1)}, u32[]{:S(2)}, u32[]{:S(2)}) collective-permute-start(bf16[3,64,512]{2,1,0:T(8,128)(2,1)S(1)} %get-tuple-element.205), channel_id=1, source_target_pairs={{0,16},{4,20},{8,24},{12,28},{16,0},{20,4},{24,8},{28,12},{1,17},{... | collective-permute-start | bytes 589832 | tf_op jit(solution)/shard_map/ppermute | solution.py:210
  95.1 18.3 %collective-permute-start.20 = (bf16[3,64,512]{2,1,0:T(8,128)(2,1)S(1)}, bf16[3,64,512]{2,1,0:T(8,128)(2,1)S(1)}, u32[]{:S(2)}, u32[]{:S(2)}) collective-permute-start(bf16[3,64,512]{2,1,0:T(8,128)(2,1)S(1)} %get-tuple-element.206), channel_id=1, source_target_pairs={{0,24},{4,28},{8,0},{12,4},{16,8},{20,12},{24,16},{28,20},{1,25},{... | collective-permute-start | bytes 589832 | tf_op jit(solution)/shard_map/ppermute | solution.py:210
